TPU v7x, 128 devices: a whole 4x4x4 slice. The times are simulated.
128 devices in a mesh: bx: 16 (over y_lo, z, core), by: 8 (over y_hi, x).
Axes of the slice: x: 4, y: 4 (y_hi: 2, y_lo: 2; y = y_hi * 2 + y_lo), z: 4, core: 2. Of those that a mesh axis runs over, the one named last changes fastest.
Arguments:
- weights: float32 [16, 8, 2, 64, 8192], P('bx', 'by'), may hold values from -6 to 6
- phase_slope: float32 [8, 16, 8, 8192], P(None, 'bx', 'by'), may hold values from -3.140625 to 3.140625
- interp_matrix: float32 [2, 2, 2, 64, 2, 64], replicated, may hold values from -0.375 to 0.375
- evaluation: float32 [2, 64, 64], replicated, may hold values from -0.5 to 0.5
Outputs:
- target_field: float32 [16, 8, 64, 8192], P('bx', 'by')
All inputs are finite; a program needn't handle non-finite values.
Results may differ from a plain program's by a relative error of at most 0.00011.
Values sent between devices are 32-bit elements; how exact they have to be, the bound alone decides.
No kernel may reach another device: no remote copies, remote signals or barrier semaphores. Data moves between devices by JAX's collectives and lax.ppermute only.
A program may use at most 128 MiB of HBM per device.

v0:
```python
import jax
import jax.numpy as jnp
from jax import lax
from jax.sharding import PartitionSpec as P

CHEB = 8
LEVELS = 4


def from_partner(value, axis, apart):
    mask = 2**apart
    pairs = [(source, source ^ mask) for source in range(lax.axis_size(axis))]
    return lax.ppermute(value, axis, pairs)


def cheb_nodes(direction):
    points = jnp.cos(jnp.pi * (2.0 * jnp.arange(CHEB, dtype=jnp.float32) + 1.0) / (2.0 * CHEB))
    return jnp.repeat(points, CHEB) if direction == 0 else jnp.tile(points, CHEB)


def real_blocks(interp_dir):
    real_part = jnp.transpose(interp_dir[0], (1, 0, 2, 3))
    imag_part = jnp.transpose(interp_dir[1], (1, 0, 2, 3))
    upper_rows = jnp.stack([real_part, -imag_part], axis=3)
    lower_rows = jnp.stack([imag_part, real_part], axis=3)
    return jnp.stack([upper_rows, lower_rows], axis=0)


def swap_half(payload, direction, bit_no):
    if direction == 0:
        return from_partner(payload, "bx", bit_no)
    return from_partner(payload, "by", bit_no)


def shards(weights, phase_slope, interp_matrix, evaluation):
    high = lax.Precision.HIGHEST
    current = weights[0, 0]
    slopes = phase_slope[:, 0, 0]
    rank = current.shape[1]
    slots = current.shape[2]
    half = slots // 2
    for level_no in range(LEVELS):
        for direction in (0, 1):
            if direction == 0:
                axis_count = lax.axis_size("bx")
                axis_place = lax.axis_index("bx")
            else:
                axis_count = lax.axis_size("by")
                axis_place = lax.axis_index("by")
            bit_no = level_no % (axis_count.bit_length() - 1)
            side_bit = axis_place >> bit_no & 1
            kept = lax.dynamic_slice_in_dim(current, side_bit * half, half, 2)
            outgoing = lax.dynamic_slice_in_dim(current, (1 - side_bit) * half, half, 2)
            blocks = real_blocks(interp_matrix[direction])
            ordered = jnp.where(side_bit == 0, blocks, blocks[:, :, :, ::-1]).reshape(
                4 * rank, 4 * rank
            )
            incoming = swap_half(outgoing, direction, bit_no)
            stacked = jnp.concatenate([kept, incoming], axis=0).reshape(4 * rank, half)
            merged = jnp.dot(ordered, stacked, precision=high)
            merged = merged.reshape(2, rank, slots)
            phase = cheb_nodes(direction)[:, None] * slopes[2 * level_no + direction][None, :]
            cosine = jnp.cos(phase)
            sine_part = jnp.sin(phase)
            current = jnp.stack(
                [
                    merged[0] * cosine - merged[1] * sine_part,
                    merged[0] * sine_part + merged[1] * cosine,
                ],
                axis=0,
            )
    eval_rows = jnp.concatenate([evaluation[0], -evaluation[1]], axis=1)
    devices_all = lax.axis_size("bx") * lax.axis_size("by")
    piece = slots // devices_all
    moved = lax.all_to_all(
        current.reshape(2, rank, devices_all, piece),
        ("bx", "by"),
        split_axis=2,
        concat_axis=3,
        tiled=True,
    )
    field = jnp.dot(eval_rows, moved.reshape(2 * rank, slots), precision=high)
    return field[None, None]


def solution(mesh):
    in_specs = (P("bx", "by", None, None, None), P(None, "bx", "by", None), P(), P())
    out_specs = P("bx", "by", None, None)
    return jax.shard_map(shards, mesh=mesh, in_specs=in_specs, out_specs=out_specs, check_vma=False)
```

profile of v0, /device:TPU:0, one launch (start us, length us, event | category | flops | bytes accessed | tf_op | source)
XLA Modules:
  0.0 672.8 jit_solution(11564270716415219115)
XLA Ops:
  0.0 4.0 dynamic-slice_bitcast_fusion.1
  5.9 3.6 rev.5
  9.4 3.0 broadcast_select_fusion
  17.6 3.8 fusion.76
  25.7 2.9 squeeze.48
  28.6 9.1 %fusion.47 = (f32[1,64,8192]{2,1,0:T(8,128)S(1)}, f32[1,64,8192]{2,1,0:T(8,128)S(1)}) fusion(f32[1,64,8192]{2,1,0:T(8,128)S(1)} %squeeze.47, f32[1,64,8192]{2,1,0:T(8,128)} %squeeze.48, f32[8192]{0:T(1024)S(1)} %bitcast.106, f32[64]{0:T(128)S(1)} %mul.634), kind=kLoop, calls=%fused_computation.101 | loop fusion | flops 3670016 | bytes 8421632 | tf_op jit(solution)/shard_map/add | solution.py:68
  43.6 2.7 broadcast_select_fusion.2
  47.3 40.7 %collective-permute-done.1 = f32[2,64,4096]{2,1,0:T(8,128)} collective-permute-done((f32[2,64,4096]{2,1,0:T(8,128)}, f32[2,64,4096]{2,1,0:T(8,128)}, u32[]{:S(2)}, u32[]{:S(2)}) %collective-permute-start.1) | collective-permute-done | bytes 2097184 | tf_op jit(solution)/shard_map/ppermute | solution.py:13
  89.9 3.8 fusion.77
  97.9 2.9 squeeze.50
  100.8 9.1 %fusion.45 = (f32[1,64,8192]{2,1,0:T(8,128)S(1)}, f32[1,64,8192]{2,1,0:T(8,128)S(1)}) fusion(f32[1,64,8192]{2,1,0:T(8,128)S(1)} %squeeze.49, f32[1,64,8192]{2,1,0:T(8,128)} %squeeze.50, f32[8192]{0:T(1024)S(1)} %bitcast.105, f32[64]{0:T(128)S(1)} %mul.645), kind=kLoop, calls=%fused_computation.99 | loop fusion | flops 3670016 | bytes 8421632 | tf_op jit(solution)/shard_map/add | solution.py:68
  114.9 45.0 %collective-permute-done.2 = f32[2,64,4096]{2,1,0:T(8,128)} collective-permute-done((f32[2,64,4096]{2,1,0:T(8,128)}, f32[2,64,4096]{2,1,0:T(8,128)}, u32[]{:S(2)}, u32[]{:S(2)}) %collective-permute-start.2) | collective-permute-done | bytes 2097184 | tf_op jit(solution)/shard_map/ppermute | solution.py:13
  161.8 3.8 fusion.78
  169.9 2.9 squeeze.52
  172.8 9.1 %fusion.43 = (f32[1,64,8192]{2,1,0:T(8,128)S(1)}, f32[1,64,8192]{2,1,0:T(8,128)S(1)}) fusion(f32[1,64,8192]{2,1,0:T(8,128)S(1)} %squeeze.51, f32[1,64,8192]{2,1,0:T(8,128)} %squeeze.52, f32[8192]{0:T(1024)S(1)} %bitcast.104, f32[64]{0:T(128)S(1)} %mul.634), kind=kLoop, calls=%fused_computation.97 | loop fusion | flops 3670016 | bytes 8421632 | tf_op jit(solution)/shard_map/add | solution.py:68
  183.6 3.2 collective-permute-start.3
  187.6 44.6 %collective-permute-done.3 = f32[2,64,4096]{2,1,0:T(8,128)} collective-permute-done((f32[2,64,4096]{2,1,0:T(8,128)}, f32[2,64,4096]{2,1,0:T(8,128)}, u32[]{:S(2)}, u32[]{:S(2)}) %collective-permute-start.3) | collective-permute-done | bytes 2097184 | tf_op jit(solution)/shard_map/ppermute | solution.py:13
  234.1 3.8 fusion.79
  242.2 2.9 squeeze.54
  245.1 9.1 %fusion.41 = (f32[1,64,8192]{2,1,0:T(8,128)S(1)}, f32[1,64,8192]{2,1,0:T(8,128)S(1)}) fusion(f32[1,64,8192]{2,1,0:T(8,128)S(1)} %squeeze.53, f32[1,64,8192]{2,1,0:T(8,128)} %squeeze.54, f32[8192]{0:T(1024)S(1)} %bitcast.103, f32[64]{0:T(128)S(1)} %mul.645), kind=kLoop, calls=%fused_computation.95 | loop fusion | flops 3670016 | bytes 8421632 | tf_op jit(solution)/shard_map/add | solution.py:68
  255.9 3.6 collective-permute-start.4
  260.4 43.3 %collective-permute-done.4 = f32[2,64,4096]{2,1,0:T(8,128)} collective-permute-done((f32[2,64,4096]{2,1,0:T(8,128)}, f32[2,64,4096]{2,1,0:T(8,128)}, u32[]{:S(2)}, u32[]{:S(2)}) %collective-permute-start.4) | collective-permute-done | bytes 2097184 | tf_op jit(solution)/shard_map/ppermute | solution.py:13
  305.6 3.8 fusion.80
  313.7 2.9 squeeze.56
  316.6 9.1 %fusion.39 = (f32[1,64,8192]{2,1,0:T(8,128)S(1)}, f32[1,64,8192]{2,1,0:T(8,128)S(1)}) fusion(f32[1,64,8192]{2,1,0:T(8,128)S(1)} %squeeze.55, f32[1,64,8192]{2,1,0:T(8,128)} %squeeze.56, f32[8192]{0:T(1024)S(1)} %bitcast.102, f32[64]{0:T(128)S(1)} %mul.634), kind=kLoop, calls=%fused_computation.93 | loop fusion | flops 3670016 | bytes 8421632 | tf_op jit(solution)/shard_map/add | solution.py:68
  327.4 3.4 collective-permute-start.5
  331.7 42.7 %collective-permute-done.5 = f32[2,64,4096]{2,1,0:T(8,128)} collective-permute-done((f32[2,64,4096]{2,1,0:T(8,128)}, f32[2,64,4096]{2,1,0:T(8,128)}, u32[]{:S(2)}, u32[]{:S(2)}) %collective-permute-start.5) | collective-permute-done | bytes 2097184 | tf_op jit(solution)/shard_map/ppermute | solution.py:13
  376.3 3.8 fusion.81
  384.4 2.9 squeeze.58
  387.3 9.1 %fusion.37 = (f32[1,64,8192]{2,1,0:T(8,128)S(1)}, f32[1,64,8192]{2,1,0:T(8,128)S(1)}) fusion(f32[1,64,8192]{2,1,0:T(8,128)S(1)} %squeeze.57, f32[1,64,8192]{2,1,0:T(8,128)} %squeeze.58, f32[8192]{0:T(1024)S(1)} %bitcast.101, f32[64]{0:T(128)S(1)} %mul.645), kind=kLoop, calls=%fused_computation.91 | loop fusion | flops 3670016 | bytes 8421632 | tf_op jit(solution)/shard_map/add | solution.py:68
  400.5 42.0 %collective-permute-done.6 = f32[2,64,4096]{2,1,0:T(8,128)} collective-permute-done((f32[2,64,4096]{2,1,0:T(8,128)}, f32[2,64,4096]{2,1,0:T(8,128)}, u32[]{:S(2)}, u32[]{:S(2)}) %collective-permute-start.6) | collective-permute-done | bytes 2097184 | tf_op jit(solution)/shard_map/ppermute | solution.py:13
  444.4 3.8 fusion.82
  452.5 2.9 squeeze.59
  455.4 9.1 %fusion.35 = (f32[1,64,8192]{2,1,0:T(8,128)S(1)}, f32[1,64,8192]{2,1,0:T(8,128)S(1)}) fusion(f32[1,64,8192]{2,1,0:T(8,128)} %squeeze.59, f32[1,64,8192]{2,1,0:T(8,128)S(1)} %squeeze.120, f32[8192]{0:T(1024)S(1)} %bitcast.100, f32[64]{0:T(128)S(1)} %mul.634), kind=kLoop, calls=%fused_computation.89 | loop fusion | flops 3670016 | bytes 8421632 | tf_op jit(solution)/shard_map/add | solution.py:68
  467.5 42.0 %collective-permute-done.7 = f32[2,64,4096]{2,1,0:T(8,128)} collective-permute-done((f32[2,64,4096]{2,1,0:T(8,128)}, f32[2,64,4096]{2,1,0:T(8,128)}, u32[]{:S(2)}, u32[]{:S(2)}) %collective-permute-start.7) | collective-permute-done | bytes 2097184 | tf_op jit(solution)/shard_map/ppermute | solution.py:13
  511.4 3.8 fusion.83
  516.9 4.9 squeeze.121
  521.8 3.0 squeeze.122
  524.8 17.9 %fusion.4 = (f32[1,64,128,64]{3,2,1,0:T(8,128)S(1)}, f32[1,64,128,64]{3,2,1,0:T(8,128)S(1)}) fusion(f32[1,64,128,64]{3,2,1,0:T(8,128)} %squeeze.122, f32[1,64,128,64]{3,2,1,0:T(8,128)} %squeeze.121, f32[128,64]{1,0:T(8,128)S(1)} %mul.700, f32[64]{0:T(128)S(1)} %mul.645), kind=kLoop, calls=%fused_computation.36 | loop fusion | flops 3670016 | bytes 8421632 | tf_op jit(solution)/shard_map/sub | solution.py:67
  544.4 8.1 %copy.22 = f32[2,64,128,64]{3,1,0,2:T(8,128)} copy(f32[2,64,128,64]{3,2,1,0:T(8,128)S(1)} %pad_maximum_fusion) | data formatting | bytes 8388608 | tf_op jit(solution)/shard_map/stack | solution.py:65
  552.5 9.4 %reshape.1367 = f32[128,1,8192]{2,1,0:T(1,128)} reshape(f32[128,2,64,64]{3,2,1,0:T(8,128)} %bitcast.90) | data formatting | bytes 8388608
  561.9 10.2 %all-to-all-start = ((f32[128,1,8192]{2,1,0:T(1,128)}), f32[128,1,8192]{2,1,0:T(1,128)}, u32[]{:S(2)}, u32[]{:S(2)}) async-start(f32[128,1,8192]{2,1,0:T(1,128)} %reshape.1367), calls=%async_computation | async-start | bytes 8388608 | tf_op jit(solution)/shard_map/all_to_all | solution.py:75
  572.1 52.8 %all-to-all-done = f32[128,1,8192]{2,1,0:T(1,128)} async-done(((f32[128,1,8192]{2,1,0:T(1,128)}), f32[128,1,8192]{2,1,0:T(1,128)}, u32[]{:S(2)}, u32[]{:S(2)}) %all-to-all-start) | async-done | bytes 4194336 | tf_op jit(solution)/shard_map/all_to_all | solution.py:75
  625.4 13.9 %reduce.4 = f32[128,8192]{1,0:T(8,128)} reduce(f32[128,1,8192]{2,1,0:T(1,128)} %all-to-all-done, f32[]{:T(128)} %broadcast.505), dimensions={1}, to_apply=%all_to_all.2.reduce_sub_computation | reduce | bytes 8388612 | tf_op jit(solution)/shard_map/all_to_all | solution.py:75
  639.3 7.9 %reshape.1368 = f32[128,2,64,64]{3,2,1,0:T(8,128)} reshape(f32[128,8192]{1,0:T(8,128)} %reduce.4) | data formatting | bytes 8388608
  647.2 11.5 %copy.20 = f32[2,64,128,64]{3,2,1,0:T(8,128)} copy(f32[2,64,128,64]{3,1,0,2:T(8,128)} %bitcast.91) | data formatting | bytes 8388608 | tf_op jit(solution)/shard_map/all_to_all | solution.py:75
  658.7 7.9 %reshape.1359 = f32[128,8192]{1,0:T(8,128)} reshape(f32[2,64,128,64]{3,2,1,0:T(8,128)} %copy.20) | data formatting | bytes 8388608 | tf_op jit(solution)/shard_map/reshape | solution.py:82
  666.6 5.8 convolution_bitcast_fusion
  (86 shorter events, 81.0 us)
Async XLA Ops:
  0.0 4.0 copy-start.5
  4.0 11.7 %collective-permute-start = (f32[2,64,4096]{2,1,0:T(8,128)}, f32[2,64,4096]{2,1,0:T(8,128)}, u32[]{:S(2)}, u32[]{:S(2)}) collective-permute-start(f32[2,64,4096]{2,1,0:T(8,128)} %get-tuple-element.52), channel_id=1, source_target_pairs={{0,8},{8,0},{16,24},{24,16},{32,40},{40,32},{48,56},{56,48},{64,72... | collective-permute-start | bytes 6291464 | tf_op jit(solution)/shard_map/ppermute | solution.py:13
  39.4 48.5 %collective-permute-start.1 = (f32[2,64,4096]{2,1,0:T(8,128)}, f32[2,64,4096]{2,1,0:T(8,128)}, u32[]{:S(2)}, u32[]{:S(2)}) collective-permute-start(f32[2,64,4096]{2,1,0:T(8,128)} %get-tuple-element.48), channel_id=1, source_target_pairs={{0,1},{1,0},{2,3},{3,2},{4,5},{5,4},{6,7},{7,6},{8,9},{9,8},{10,11... | collective-permute-start | bytes 6291464 | tf_op jit(solution)/shard_map/ppermute | solution.py:13
  97.9 2.9 copy-start.7
  109.9 4.1 copy-start.3
  111.6 48.2 %collective-permute-start.2 = (f32[2,64,4096]{2,1,0:T(8,128)}, f32[2,64,4096]{2,1,0:T(8,128)}, u32[]{:S(2)}, u32[]{:S(2)}) collective-permute-start(f32[2,64,4096]{2,1,0:T(8,128)} %get-tuple-element.44), channel_id=1, source_target_pairs={{0,16},{8,24},{16,0},{24,8},{32,48},{40,56},{48,32},{56,40},{64,80... | collective-permute-start | bytes 6291464 | tf_op jit(solution)/shard_map/ppermute | solution.py:13
  169.9 2.9 copy-start.6
  181.8 4.9 copy-start.4
  183.6 48.6 %collective-permute-start.3 = (f32[2,64,4096]{2,1,0:T(8,128)}, f32[2,64,4096]{2,1,0:T(8,128)}, u32[]{:S(2)}, u32[]{:S(2)}) collective-permute-start(f32[2,64,4096]{2,1,0:T(8,128)} %get-tuple-element.40), channel_id=1, source_target_pairs={{0,2},{1,3},{2,0},{3,1},{4,6},{5,7},{6,4},{7,5},{8,10},{9,11},{10,... | collective-permute-start | bytes 6291464 | tf_op jit(solution)/shard_map/ppermute | solution.py:13
  254.2 5.3 copy-start.1
  255.9 47.8 %collective-permute-start.4 = (f32[2,64,4096]{2,1,0:T(8,128)}, f32[2,64,4096]{2,1,0:T(8,128)}, u32[]{:S(2)}, u32[]{:S(2)}) collective-permute-start(f32[2,64,4096]{2,1,0:T(8,128)} %get-tuple-element.36), channel_id=1, source_target_pairs={{0,32},{8,40},{16,48},{24,56},{32,0},{40,8},{48,16},{56,24},{64,96... | collective-permute-start | bytes 6291464 | tf_op jit(solution)/shard_map/ppermute | solution.py:13
  325.6 5.2 copy-start.2
  327.4 47.0 %collective-permute-start.5 = (f32[2,64,4096]{2,1,0:T(8,128)}, f32[2,64,4096]{2,1,0:T(8,128)}, u32[]{:S(2)}, u32[]{:S(2)}) collective-permute-start(f32[2,64,4096]{2,1,0:T(8,128)} %get-tuple-element.32), channel_id=1, source_target_pairs={{0,4},{1,5},{2,6},{3,7},{4,0},{5,1},{6,2},{7,3},{8,12},{9,13},{10,... | collective-permute-start | bytes 6291464 | tf_op jit(solution)/shard_map/ppermute | solution.py:13
  396.4 3.3 copy-start
  398.1 44.4 %collective-permute-start.6 = (f32[2,64,4096]{2,1,0:T(8,128)}, f32[2,64,4096]{2,1,0:T(8,128)}, u32[]{:S(2)}, u32[]{:S(2)}) collective-permute-start(f32[2,64,4096]{2,1,0:T(8,128)} %get-tuple-element.28), channel_id=1, source_target_pairs={{0,64},{8,72},{16,80},{24,88},{32,96},{40,104},{48,112},{56,120},{... | collective-permute-start | bytes 6291464 | tf_op jit(solution)/shard_map/ppermute | solution.py:13
  464.5 3.0 copy-start.8
  466.2 43.3 %collective-permute-start.7 = (f32[2,64,4096]{2,1,0:T(8,128)}, f32[2,64,4096]{2,1,0:T(8,128)}, u32[]{:S(2)}, u32[]{:S(2)}) collective-permute-start(f32[2,64,4096]{2,1,0:T(8,128)} %get-tuple-element.24), channel_id=1, source_target_pairs={{0,1},{1,0},{2,3},{3,2},{4,5},{5,4},{6,7},{7,6},{8,9},{9,8},{10,11... | collective-permute-start | bytes 6291464 | tf_op jit(solution)/shard_map/ppermute | solution.py:13
  561.9 10.2 %copy-start.9 = (f32[2,64,64]{2,1,0:T(8,128)S(1)}, f32[2,64,64]{2,1,0:T(8,128)}, u32[]{:S(2)}) copy-start(f32[2,64,64]{2,1,0:T(8,128)} %param.7) | copy-start | bytes 98308
  561.9 63.0 %all-to-all-start = ((f32[128,1,8192]{2,1,0:T(1,128)}), f32[128,1,8192]{2,1,0:T(1,128)}, u32[]{:S(2)}, u32[]{:S(2)}) async-start(f32[128,1,8192]{2,1,0:T(1,128)} %reshape.1367), calls=%async_computation | async-start | bytes 8388608 | tf_op jit(solution)/shard_map/all_to_all | solution.py:75
where the time goes:
time: 683 us; the launch traced here: 673 us
  waiting for transfers between devices  353 us (52%)
  other arithmetic  132 us (19%)
  local copies, waits for them, and re-layouts  123 us (18%)
  matrix products  36.2 us (5%)
  starting transfers between devices  27.2 us (4%)
    ppermute x8, waiting for transfers between devices, from_partner(): return lax.ppermute(value, axis, pairs)  300 us
    add x7, other arithmetic, shards(): merged[0] * sine_part + merged[1] * cosine  63.4 us
    all_to_all x1, waiting for transfers between devices, shards(): lax.all_to_all(current.reshape(2, rank, devices_all, piece), ('bx', 'by')...  52.8 us
    dot_general x8, matrix products, shards(): merged = jnp.dot(ordered, stacked, precision=high)  30.4 us
    squeeze x8, local copies, waits for them, and re-layouts, shards(): merged[1] * sine_part  22.3 us
    squeeze x8, local copies, waits for them, and re-layouts, shards(): merged[0] * cosine - merged[1] * sine_part  19.4 us
    sub x1, other arithmetic, shards(): merged[0] * cosine - merged[1] * sine_part  17.9 us
    unnamed x22, local copies, waits for them, and re-layouts  17.4 us
  transfers between devices with their start and end apart: 9, of which 8 were waited for; matrix products, arithmetic and copies ran while one was open for 3% of the time, Pallas kernels for 0%

commit v1 on v0

v1 whole, which is shorter than its diff:
```python
import functools

import jax
import jax.numpy as jnp
import numpy as np
from jax import lax
from jax.experimental import pallas as pl
from jax.experimental.pallas import tpu as pltpu
from jax.sharding import PartitionSpec as P

AXES = ("bx", "by")
ROWS = 64
WIDE = 72
NODES = [float(np.cos(np.pi * (2 * m + 1) / 16)) for m in range(4)]
STEP_BITS = [(None, 0), (0, 1), (3, 0), (1, 1), (4, 0), (2, 1), (5, 0), (0, 1)]
F32 = jnp.float32
BF16 = jnp.bfloat16


def split_two(value):
    high = value.astype(BF16)
    low = (value - high.astype(F32)).astype(BF16)
    return high, low


def pack_kernel(w0_ref, w1_ref, p0_ref, p1_ref, out_ref):
    for pair in range(w0_ref.shape[1] // 128):
        lanes = slice(pair * 128, pair * 128 + 128)
        for top, (w_ref, p_ref) in enumerate(((w0_ref, p0_ref), (w1_ref, p1_ref))):
            turned = w_ref[:, lanes].T
            for b in range(2):
                for w in range(2):
                    out_ref[w, 2 * pair + b, 32 * top : 32 * top + 32, :] = turned[
                        64 * b + 32 * w : 64 * b + 32 * w + 32
                    ]
        s0 = p0_ref[:, lanes]
        s1 = p1_ref[:, lanes]
        for b in range(2):
            both = jnp.concatenate([s0[:, 64 * b : 64 * b + 64], s1[:, 64 * b : 64 * b + 64]], axis=1)
            for w in range(2):
                out_ref[w, 2 * pair + b, ROWS:WIDE, :] = both


def pack(weights, slopes):
    block = 512
    half = weights.shape[1] // 2 // block
    return pl.pallas_call(
        pack_kernel,
        out_shape=jax.ShapeDtypeStruct((2, 64, WIDE, 128), F32),
        grid=(half,),
        in_specs=[
            pl.BlockSpec((128, block), lambda i: (0, i)),
            pl.BlockSpec((128, block), lambda i: (0, i + half)),
            pl.BlockSpec((8, block), lambda i: (0, i)),
            pl.BlockSpec((8, block), lambda i: (0, i + half)),
        ],
        out_specs=pl.BlockSpec((2, block // 64, WIDE, 128), lambda i: (0, i, 0, 0)),
        compiler_params=pltpu.CompilerParams(vmem_limit_bytes=32 << 20),
        cost_estimate=pl.CostEstimate(flops=0, bytes_accessed=9 << 20, transcendentals=0),
    )(weights, weights, slopes, slopes)


def sincos(angle):
    h = angle * 0.5
    q = h * h
    s = q * (-1 / 39916800) + 1 / 362880
    s = s * q - 1 / 5040
    s = s * q + 1 / 120
    s = s * q - 1 / 6
    s = (s * q + 1.0) * h
    c = q * (1 / 479001600) - 1 / 3628800
    c = c * q + 1 / 40320
    c = c * q - 1 / 720
    c = c * q + 1 / 24
    c = c * q - 0.5
    c = c * q + 1.0
    return 2.0 * s * c, 1.0 - 2.0 * s * s


def lane_gather(value, index):
    return jnp.take_along_axis(value, index, axis=1, mode="promise_in_bounds")


def build_tables(w, a_ref, cos_ref, sin_ref):
    lane = lax.broadcasted_iota(jnp.int32, (32, 128), 1)
    m = lane % 4
    node = jnp.where(m == 0, NODES[0], jnp.where(m == 1, NODES[1], jnp.where(m == 2, NODES[2], NODES[3])))
    second = lane // 4 % 2 == 1
    g = lane // 8

    @pl.loop(0, 8)
    def _(step):
        slab = a_ref[pl.ds(ROWS + step, 128, stride=WIDE), :]
        turned = slab.T
        t0 = jnp.where(w == 0, turned[0:32], turned[32:64])
        t1 = jnp.where(w == 0, turned[64:96], turned[96:128])
        for tile in range(4):
            for h in range(2):
                index = ((2 * (2 * tile + g // 8) + h) * 8) + g % 8
                slope = jnp.where(second, lane_gather(t1, index), lane_gather(t0, index))
                s, c = sincos(slope * node)
                cos_ref[step * 4 + tile, 32 * h : 32 * h + 32, :] = c
                sin_ref[step * 4 + tile, 32 * h : 32 * h + 32, :] = s


def factors(step, box, direction, cos_ref, sin_ref):
    lane = lax.broadcasted_iota(jnp.int32, (ROWS, 128), 1)
    p = lane % 64
    m = p // 8 if direction == 0 else p % 8
    index = lane // 64 * 4 + jnp.where(m < 4, m, 7 - m) + (box % 16) * 8
    tile = step * 4 + box // 16
    c = lane_gather(cos_ref[tile], index)
    s = lane_gather(sin_ref[tile], index)
    return c, jnp.where(m < 4, s, -s)


def rotate(merged, c, s):
    re = merged[:, :128]
    im = merged[:, 128:]
    return re * c - im * s, re * s + im * c


def by_top(re, im):
    lower = lax.broadcasted_iota(jnp.int32, re.shape, 1) < 64
    first = jnp.where(lower, re, pltpu.roll(im, 64, 1))
    second = jnp.where(lower, pltpu.roll(re, 64, 1), im)
    return first, second


def insert_bit(q, bit, value):
    return ((q >> bit) << (bit + 1)) | (value << bit) | (q & ((1 << bit) - 1))


GROUPS = 4


def main_kernel(w_ref, a_ref, k_ref, e_ref, own_ref, send_ref, hi_ref, lo_ref, k3_ref, e3_ref, cos_ref, sin_ref):
    build_tables(w_ref[0], a_ref, cos_ref, sin_ref)
    for d in range(2):
        high, low = split_two(k_ref[d])
        k3_ref[d, 0:256] = high
        k3_ref[d, 256:512] = high
        k3_ref[d, 512:768] = low
    high, low = split_two(e_ref[...])
    e3_ref[:, 0:256] = high
    e3_ref[:, 256:512] = high
    e3_ref[:, 512:768] = low

    def store(box, re, im):
        for top, tile in enumerate(by_top(re, im)):
            high, low = split_two(tile)
            hi_ref[2 * box + top] = high
            lo_ref[2 * box + top] = low

    @pl.loop(0, 64 // (2 * GROUPS))
    def _(i):
        rows = []
        for n in range(2 * GROUPS):
            box = i * 2 * GROUPS + n
            at = box // 8 * 16 + box % 8
            parts = [split_two(a_ref[pl.ds(pl.multiple_of((at + 8 * c) * WIDE, 8), ROWS), :]) for c in range(2)]
            highs = [p[0] for p in parts]
            lows = [p[1] for p in parts]
            rows.append(jnp.concatenate(highs + lows + highs, axis=1))
        merged = jnp.dot(jnp.concatenate(rows, axis=0), k3_ref[0], preferred_element_type=F32)
        for n in range(2 * GROUPS):
            box = i * 2 * GROUPS + n
            c, s = factors(0, box, 0, cos_ref, sin_ref)
            store(box, *rotate(merged[ROWS * n : ROWS * n + ROWS], c, s))

    def gather_rows(boxes):
        rows = []
        for pair in boxes:
            for h in range(2):
                highs = [hi_ref[2 * box + h] for box in pair]
                lows = [lo_ref[2 * box + h] for box in pair]
                rows.append(jnp.concatenate(highs + lows + highs, axis=1))
        return jnp.concatenate(rows, axis=0)

    for step in range(1, 7):
        bit, direction = STEP_BITS[step]

        @pl.loop(0, 32 // GROUPS)
        def _(i, step=step, bit=bit, direction=direction):
            boxes = [[insert_bit(i * GROUPS + n, bit, c) for c in range(2)] for n in range(GROUPS)]
            merged = jnp.dot(gather_rows(boxes), k3_ref[direction], preferred_element_type=F32)
            for n in range(GROUPS):
                for h in range(2):
                    box = boxes[n][h]
                    at = ROWS * (2 * n + h)
                    c, s = factors(step, box, direction, cos_ref, sin_ref)
                    store(box, *rotate(merged[at : at + ROWS], c, s))

    @pl.loop(0, 16)
    def _(i):
        boxes = [[i * 4 + 2 * y1 + c for c in range(2)] for y1 in range(2)]
        merged = jnp.dot(gather_rows(boxes), k3_ref[1], preferred_element_type=F32)
        tiles = {}
        for y in range(4):
            c, s = factors(7, i * 4 + y, 1, cos_ref, sin_ref)
            re, im = rotate(merged[ROWS * y : ROWS * y + ROWS], c, s)
            tiles[y] = split_two(jnp.concatenate([re, im], axis=1))
        rows = []
        for h in range(2):
            for y in (0, 2, 1, 3):
                high, low = (t[32 * h : 32 * h + 32] for t in tiles[y])
                rows.append(jnp.concatenate([high, low, high], axis=1))
        field = lax.dot_general(
            e3_ref[...], jnp.concatenate(rows, axis=0), (((1,), (1,)), ((), ())), preferred_element_type=F32
        )
        for h in range(2):
            at = pl.multiple_of(((i // 2) * 4 + 2 * h + i % 2) * 128, 128)
            own_ref[:, pl.ds(at, 128)] = field[0:64, 128 * h : 128 * h + 128]
            send_ref[:, pl.ds(at, 128)] = field[64:128, 128 * h : 128 * h + 128]


def butterfly(w, arrived, k, e):
    vmem = pl.BlockSpec(memory_space=pltpu.VMEM)
    return pl.pallas_call(
        main_kernel,
        out_shape=[jax.ShapeDtypeStruct((64, 4096), F32)] * 2,
        in_specs=[pl.BlockSpec(memory_space=pltpu.SMEM), vmem, vmem, vmem],
        out_specs=[vmem, vmem],
        scratch_shapes=[
            pltpu.VMEM((128, ROWS, 128), BF16),
            pltpu.VMEM((128, ROWS, 128), BF16),
            pltpu.VMEM((2, 768, 256), BF16),
            pltpu.VMEM((128, 768), BF16),
            pltpu.VMEM((32, ROWS, 128), F32),
            pltpu.VMEM((32, ROWS, 128), F32),
        ],
        compiler_params=pltpu.CompilerParams(vmem_limit_bytes=48 << 20),
        cost_estimate=pl.CostEstimate(flops=15_000_000_000, bytes_accessed=7 << 20, transcendentals=0),
    )(w, arrived, k, e)


def join_kernel(w_ref, own_ref, got_ref, out_ref):
    first = w_ref[0] == 0
    lane = lax.broadcasted_iota(jnp.int32, (64, 128), 1)
    even = lane // 32 % 2 == 0
    for tile in range(own_ref.shape[1] // 128):
        lanes = slice(128 * tile, 128 * tile + 128)
        own = own_ref[:, lanes]
        got = got_ref[:, lanes]
        a = jnp.where(first, own, got)
        b = jnp.where(first, got, own)
        out_ref[:, 256 * tile : 256 * tile + 128] = jnp.where(even, a, pltpu.roll(b, 32, 1))
        out_ref[:, 256 * tile + 128 : 256 * tile + 256] = jnp.where(even, pltpu.roll(a, 96, 1), b)


def join(w, own, got):
    block = 1024
    return pl.pallas_call(
        join_kernel,
        out_shape=jax.ShapeDtypeStruct((64, 8192), F32),
        grid=(4096 // block,),
        in_specs=[
            pl.BlockSpec(memory_space=pltpu.SMEM),
            pl.BlockSpec((64, block), lambda i: (0, i)),
            pl.BlockSpec((64, block), lambda i: (0, i)),
        ],
        out_specs=pl.BlockSpec((64, 2 * block), lambda i: (0, i)),
        compiler_params=pltpu.CompilerParams(vmem_limit_bytes=32 << 20),
        cost_estimate=pl.CostEstimate(flops=0, bytes_accessed=4 << 20, transcendentals=0),
    )(w, own, got)


def merge_matrices(interp_matrix):
    re = jnp.transpose(interp_matrix[:, 0], (0, 3, 4, 1, 2)).reshape(2, 2, 64, 128)
    im = jnp.transpose(interp_matrix[:, 1], (0, 3, 4, 1, 2)).reshape(2, 2, 64, 128)
    from_re = jnp.concatenate([re, im], axis=3)
    from_im = jnp.concatenate([-im, re], axis=3)
    return jnp.stack([from_re, from_im], axis=2).reshape(2, 256, 256)


def evaluation_matrix(evaluation, w):
    zero = jnp.zeros((64, 64), F32)
    re, im = evaluation[0], -evaluation[1]
    low = jnp.concatenate([re, zero, im, zero], axis=1)
    high = jnp.concatenate([zero, re, zero, im], axis=1)
    return jnp.where(w == 0, jnp.concatenate([low, high], axis=0), jnp.concatenate([high, low], axis=0))


def shards(weights, phase_slope, interp_matrix, evaluation):
    w = lax.axis_index("bx") >> 3
    w_one = w.astype(jnp.int32).reshape(1)
    packed = pack(weights.reshape(128, 8192), phase_slope.reshape(8, 8192))
    arrived = lax.all_to_all(packed.reshape(128, WIDE, 128), AXES, split_axis=0, concat_axis=0, tiled=True)
    own, send = butterfly(
        w_one, arrived.reshape(128 * WIDE, 128), merge_matrices(interp_matrix), evaluation_matrix(evaluation, w)
    )
    got = lax.ppermute(send, "bx", [(i, i ^ 8) for i in range(16)])
    return join(w_one, own, got)[None, None]


def solution(mesh):
    in_specs = (P("bx", "by", None, None, None), P(None, "bx", "by", None), P(), P())
    out_specs = P("bx", "by", None, None)
    return jax.shard_map(shards, mesh=mesh, in_specs=in_specs, out_specs=out_specs, check_vma=False)
```

time: 683 us -> 146 us (0.21); the launches traced: 673 us -> 145 us
  waiting for transfers between devices: 353 us -> 79.5 us
  other arithmetic: 132 us -> 0.27 us
  local copies, waits for them, and re-layouts: 123 us -> 5.75 us
  Pallas kernels: 0 us -> 46.5 us
  matrix products: 36.2 us -> 0 us
  starting transfers between devices: 27.2 us -> 12.8 us
    ppermute x8 -> x1, waiting for transfers between devices: 300 us -> 23 us  [shards(): got = lax.ppermute(send, 'bx', [(i, i ^ 8) for i in range(16)])]
    add x7 -> x0, other arithmetic: 63.4 us -> none  [shards(): merged[0] * sine_part + merged[1] * cosine]
    pallas_call x0 -> x3, Pallas kernels: none -> 46.5 us  [the longest x1 41.9 us: butterfly(): pl.pallas_call(main_kernel, out_shape=[jax.ShapeDtypeStruct((64, 4096), F...]
    squeeze x16 -> x0, local copies, waits for them, and re-layouts: 41.7 us -> none  [the longest x8 22.3 us: shards(): merged[1] * sine_part]
    dot_general x9 -> x0, matrix products: 36.2 us -> none  [the longest x8 30.4 us: shards(): merged = jnp.dot(ordered, stacked, precision=high)]
    slice x9 -> x1, local copies, waits for them, and re-layouts: 20.1 us -> 0.04 us  [merge_matrices(): interp_matrix[:, 1]]
    sub x1 -> x0, other arithmetic: 17.9 us -> none  [shards(): merged[0] * cosine - merged[1] * sine_part]
    ppermute x8 -> x1, starting transfers between devices: 17.1 us -> 1.16 us  [shards(): got = lax.ppermute(send, 'bx', [(i, i ^ 8) for i in range(16)])]
  transfers between devices with their start and end apart: 9 -> 2, of which waited for: 8 -> 2; matrix products, arithmetic and copies ran while one was open for 3% -> 0% of each run, Pallas kernels for 0% -> 0%
where the time goes in v1:
time: 146 us; the launch traced here: 145 us
  waiting for transfers between devices  79.5 us (54%)
  Pallas kernels  46.5 us (32%)
  starting transfers between devices  12.8 us (9%)
  local copies, waits for them, and re-layouts  5.75 us (4%)
    all_to_all x1, waiting for transfers between devices, shards(): lax.all_to_all(packed.reshape(128, WIDE, 128), AXES, split_axis=0, concat...  56.5 us
    pallas_call x1, Pallas kernels, butterfly(): pl.pallas_call(main_kernel, out_shape=[jax.ShapeDtypeStruct((64, 4096), F...  41.9 us
    ppermute x1, waiting for transfers between devices, shards(): got = lax.ppermute(send, 'bx', [(i, i ^ 8) for i in range(16)])  23 us
    all_to_all x1, starting transfers between devices, shards(): lax.all_to_all(packed.reshape(128, WIDE, 128), AXES, split_axis=0, concat...  11.6 us
    unnamed x9, local copies, waits for them, and re-layouts  5.48 us
  transfers between devices with their start and end apart: 2, of which 2 were waited for; matrix products, arithmetic and copies ran while one was open for 0% of the time, Pallas kernels for 0%

profile of v1, /device:TPU:0, one launch (start us, length us, event | category | flops | bytes accessed | tf_op | source)
XLA Modules:
  0.0 145.0 jit_solution(1059524402029493978)
XLA Ops:
  0.0 1.1 copy.11
  1.1 0.0 copy-start.1
  1.1 2.2 %copy-done.1 = f32[1,1,2,64,8192]{4,3,2,1,0:T(8,128)S(1)} copy-done((f32[1,1,2,64,8192]{4,3,2,1,0:T(8,128)S(1)}, f32[1,1,2,64,8192]{4,3,2,1,0:T(8,128)}, u32[]{:S(2)}) %copy-start.1) | copy-done | bytes 4194328
  3.3 2.3 %shard_map.46 = f32[2,64,72,128]{3,2,1,0:T(8,128)S(1)} custom-call(f32[128,8192]{1,0:T(8,128)S(1)} %bitcast.28, f32[128,8192]{1,0:T(8,128)S(1)} %bitcast.29, f32[8,8192]{1,0:T(8,128)S(1)} %bitcast.30, f32[8,8192]{1,0:T(8,128)S(1)} %bitcast.31), custom_call_target="tpu_custom_call" | custom-call | bytes 9437184 | tf_op jit(solution)/shard_map/pallas_call | solution.py:47
  5.6 0.0 copy-start
  5.7 2.2 %copy-done = f32[2,64,72,128]{3,2,1,0:T(8,128)} copy-done((f32[2,64,72,128]{3,2,1,0:T(8,128)}, f32[2,64,72,128]{3,2,1,0:T(8,128)S(1)}, u32[]{:S(2)}) %copy-start) | copy-done | bytes 4718616
  7.8 0.0 copy-start.2
  7.8 0.0 copy-start.3
  7.8 11.6 %all-to-all-start = ((f32[128,72,128]{2,1,0:T(8,128)}), f32[128,72,128]{2,1,0:T(8,128)}, u32[]{:S(2)}, u32[]{:S(2)}) async-start(f32[128,72,128]{2,1,0:T(8,128)} %bitcast.27), calls=%async_computation | async-start | bytes 9437184 | tf_op jit(solution)/shard_map/all_to_all | solution.py:288
  19.5 0.0 copy-done.2
  19.5 0.1 copy.6
  19.6 0.1 copy.5
  19.8 0.0 copy-done.3
  19.8 0.2 maximum_select_fusion.e_ref
  20.1 56.5 %all-to-all-done = f32[128,72,128]{2,1,0:T(8,128)} async-done(((f32[128,72,128]{2,1,0:T(8,128)}), f32[128,72,128]{2,1,0:T(8,128)}, u32[]{:S(2)}, u32[]{:S(2)}) %all-to-all-start) | async-done | bytes 4718624 | tf_op jit(solution)/shard_map/all_to_all | solution.py:288
  76.6 41.9 %shard_map.47 = (f32[64,4096]{1,0:T(8,128)S(1)}, f32[64,4096]{1,0:T(8,128)S(1)}) custom-call(s32[1]{0:T(128)} %bitcast.w_ref, f32[9216,128]{1,0:T(8,128)} %bitcast.3.a_ref, f32[2,256,256]{2,1,0:T(8,128)S(1)} %bitcast.32, f32[128,256]{1,0:T(8,128)S(1)} %maximum_select_fusion.e_ref), custom_call_target="tpu_custom_call" | custom-call | flops 15000000512 | bytes 7340032 | tf_op jit(solution)/shard_map/pallas_call | solution.py:219
  118.5 1.2 collective-permute-start
  119.7 23.0 %collective-permute-done.got_ref = f32[64,4096]{1,0:T(8,128)S(1)} collective-permute-done((f32[64,4096]{1,0:T(8,128)S(1)}, f32[64,4096]{1,0:T(8,128)S(1)}, u32[]{:S(2)}, u32[]{:S(2)}) %collective-permute-start) | collective-permute-done | bytes 1048608 | tf_op jit(solution)/shard_map/ppermute | solution.py:292
  142.6 2.3 %shard_map.48 = f32[64,8192]{1,0:T(8,128)} custom-call(s32[1]{0:T(128)} %bitcast.w_ref, f32[64,4096]{1,0:T(8,128)S(1)} %get-tuple-element.7.own_ref, f32[64,4096]{1,0:T(8,128)S(1)} %collective-permute-done.got_ref), custom_call_target="tpu_custom_call" | custom-call | bytes 4194304 | tf_op jit(solution)/shard_map/pallas_call | solution.py:253
  (6 shorter events, 0.1 us)
Async XLA Ops:
  1.1 2.2 %copy-start.1 = (f32[1,1,2,64,8192]{4,3,2,1,0:T(8,128)S(1)}, f32[1,1,2,64,8192]{4,3,2,1,0:T(8,128)}, u32[]{:S(2)}) copy-start(f32[1,1,2,64,8192]{4,3,2,1,0:T(8,128)} %param.4) | copy-start | bytes 12582916
  5.6 2.2 %copy-start = (f32[2,64,72,128]{3,2,1,0:T(8,128)}, f32[2,64,72,128]{3,2,1,0:T(8,128)S(1)}, u32[]{:S(2)}) copy-start(f32[2,64,72,128]{3,2,1,0:T(8,128)S(1)} %shard_map.46) | copy-start | bytes 14155780
  7.8 11.6 %copy-start.2 = (f32[2,2,2,64,2,64]{5,4,3,2,1,0:T(2,128)S(1)}, f32[2,2,2,64,2,64]{5,4,3,2,1,0:T(2,128)}, u32[]{:S(2)}) copy-start(f32[2,2,2,64,2,64]{5,4,3,2,1,0:T(2,128)} %param.6) | copy-start | bytes 786436
  7.8 11.9 %copy-start.3 = (f32[2,64,64]{2,1,0:T(8,128)S(1)}, f32[2,64,64]{2,1,0:T(8,128)}, u32[]{:S(2)}) copy-start(f32[2,64,64]{2,1,0:T(8,128)} %param.7) | copy-start | bytes 98308
  7.8 68.8 %all-to-all-start = ((f32[128,72,128]{2,1,0:T(8,128)}), f32[128,72,128]{2,1,0:T(8,128)}, u32[]{:S(2)}, u32[]{:S(2)}) async-start(f32[128,72,128]{2,1,0:T(8,128)} %bitcast.27), calls=%async_computation | async-start | bytes 9437184 | tf_op jit(solution)/shard_map/all_to_all | solution.py:288
  118.5 24.2 %collective-permute-start = (f32[64,4096]{1,0:T(8,128)S(1)}, f32[64,4096]{1,0:T(8,128)S(1)}, u32[]{:S(2)}, u32[]{:S(2)}) collective-permute-start(f32[64,4096]{1,0:T(8,128)S(1)} %get-tuple-element.8), channel_id=1, source_target_pairs={{0,64},{8,72},{16,80},{24,88},{32,96},{40,104},{48,112},{56,120},{... | collective-permute-start | bytes 3145736 | tf_op jit(solution)/shard_map/ppermute | solution.py:292

commit v2 on v1

v2 whole, which is shorter than its diff:
```python
import functools

import jax
import jax.numpy as jnp
import numpy as np
from jax import lax
from jax.experimental import pallas as pl
from jax.experimental.pallas import tpu as pltpu
from jax.sharding import PartitionSpec as P

PACK_VMEM = 60 << 20
MAIN_VMEM = 24 << 20
AXES = ("bx", "by")
ROWS = 32
SLOPES = 8
NODES = [float(np.cos(np.pi * (2 * m + 1) / 16)) for m in range(4)]
F32 = jnp.float32
BF16 = jnp.bfloat16


def split_two(value):
    high = value.astype(BF16)
    low = (value - high.astype(F32)).astype(BF16)
    return high, low


def pack_weights_kernel(w_ref, out_ref):
    for pair in range(w_ref.shape[1] // 128):
        turned = w_ref[:, pair * 128 : pair * 128 + 128].T
        for b in range(2):
            for w in range(2):
                at = 64 * b + 32 * w
                out_ref[w, 2 * pair + b, 0:ROWS, :] = turned[at : at + 32]


def pack_both_kernel(w_ref, p0_ref, p1_ref, out_ref):
    pack_weights_kernel(w_ref, out_ref)
    for b in range(w_ref.shape[1] // 64):
        both = jnp.concatenate([p_ref[:, 0, 64 * b : 64 * b + 64] for p_ref in (p0_ref, p1_ref)], axis=1)
        for w in range(2):
            out_ref[w, b, ROWS : ROWS + SLOPES, :] = both


def pack(weights, slopes, top):
    block = 512
    half = weights.shape[1] // 2 // block
    first = top * half
    if slopes is None:
        kernel, rows, more, specs = pack_weights_kernel, ROWS, [], []
    else:
        kernel, rows, more = pack_both_kernel, ROWS + SLOPES, [slopes, slopes]
        specs = [
            pl.BlockSpec((8, 1, block), lambda i: (0, 0, i)),
            pl.BlockSpec((8, 1, block), lambda i: (0, 0, i + half)),
        ]
    out = pl.pallas_call(
        kernel,
        out_shape=jax.ShapeDtypeStruct((2, 64, rows, 128), F32),
        grid=(half,),
        in_specs=[pl.BlockSpec((128, block), lambda i: (0, first + i))] + specs,
        out_specs=pl.BlockSpec((2, block // 64, rows, 128), lambda i: (0, i, 0, 0)),
        compiler_params=pltpu.CompilerParams(vmem_limit_bytes=PACK_VMEM),
        cost_estimate=pl.CostEstimate(flops=0, bytes_accessed=5 << 20, transcendentals=0),
    )(weights, *more)
    return out.reshape(128, rows, 128)


def sincos(angle):
    h = angle * 0.5
    q = h * h
    s = q * (-1 / 39916800) + 1 / 362880
    s = s * q - 1 / 5040
    s = s * q + 1 / 120
    s = s * q - 1 / 6
    s = (s * q + 1.0) * h
    c = q * (1 / 479001600) - 1 / 3628800
    c = c * q + 1 / 40320
    c = c * q - 1 / 720
    c = c * q + 1 / 24
    c = c * q - 0.5
    c = c * q + 1.0
    return 2.0 * s * c, 1.0 - 2.0 * s * s


def lane_gather(value, index):
    return jnp.take_along_axis(value, index, axis=1, mode="promise_in_bounds")


def build_tables(w, a_ref, tables):
    lane = lax.broadcasted_iota(jnp.int32, (ROWS, 128), 1)
    m = lane % 4
    node = jnp.where(m == 0, NODES[0], jnp.where(m == 1, NODES[1], jnp.where(m == 2, NODES[2], NODES[3])))
    second = lane // 4 % 2 == 1
    g = lane // 8

    @pl.loop(0, 8)
    def _(step):
        slab = a_ref[pl.ds(ROWS + step, 128, stride=ROWS + SLOPES), :]
        turned = slab.T
        t0 = jnp.where(w == 0, turned[0:32], turned[32:64])
        t1 = jnp.where(w == 0, turned[64:96], turned[96:128])
        for tile in range(4):
            for h, (cos_ref, sin_ref) in enumerate(tables):
                index = ((2 * (2 * tile + g // 8) + h) * 8) + g % 8
                slope = jnp.where(second, lane_gather(t1, index), lane_gather(t0, index))
                s, c = sincos(slope * node)
                cos_ref[step * 4 + tile] = c
                sin_ref[step * 4 + tile] = s


def factors(step, box, direction, cos_ref, sin_ref):
    lane = lax.broadcasted_iota(jnp.int32, (ROWS, 128), 1)
    p = lane % 64
    m = p // 8 if direction == 0 else p % 8
    index = lane // 64 * 4 + jnp.where(m < 4, m, 7 - m) + (box % 16) * 8
    tile = step * 4 + box // 16
    c = lane_gather(cos_ref[tile], index)
    s = lane_gather(sin_ref[tile], index)
    return c, jnp.where(m < 4, s, -s)


def rotate(merged, c, s):
    re = merged[:, :128]
    im = merged[:, 128:]
    return re * c - im * s, re * s + im * c


def by_top(re, im):
    lower = lax.broadcasted_iota(jnp.int32, re.shape, 1) < 64
    first = jnp.where(lower, re, pltpu.roll(im, 64, 1))
    second = jnp.where(lower, pltpu.roll(re, 64, 1), im)
    return first, second


def insert_bit(q, bit, value):
    return ((q >> bit) << (bit + 1)) | (value << bit) | (q & ((1 << bit) - 1))


SUB = 4


def fill_matrices(k_ref, k3_ref):
    for d in range(2):
        high, low = split_two(k_ref[d])
        k3_ref[d, 0:256] = high
        k3_ref[d, 256:512] = high
        k3_ref[d, 512:768] = low


def widen(first, second):
    return jnp.concatenate([first[0], second[0], first[1], second[1], first[0], second[0]], axis=1)


def load(state, at):
    return state[0][at], state[1][at]


def product(rows, matrix):
    return jnp.dot(jnp.concatenate(rows, axis=0), matrix, preferred_element_type=F32)


def early_steps(a_ref, stride, k_ref, cos_ref, sin_ref, outs, hi_ref, lo_ref, k3_ref):
    fill_matrices(k_ref, k3_ref)

    @pl.loop(0, 2)
    def _(i):
        for sub in range(0, 32, 2 * SUB):
            boxes = [i * 32 + sub + n for n in range(2 * SUB)]
            rows = []
            for box in boxes:
                at = box // 8 * 16 + box % 8
                rows.append(
                    widen(
                        *(
                            split_two(a_ref[pl.ds(pl.multiple_of((at + 8 * c) * stride, 8), ROWS), :])
                            for c in range(2)
                        )
                    )
                )
            merged = product(rows, k3_ref[0])
            for n, box in enumerate(boxes):
                c, s = factors(0, box, 0, cos_ref, sin_ref)
                re, im = rotate(merged[ROWS * n : ROWS * n + ROWS], c, s)
                for top, tile in enumerate(by_top(re, im)):
                    hi_ref[2 * box + top], lo_ref[2 * box + top] = split_two(tile)

    @pl.loop(0, 2)
    def _(i):
        for sub in range(0, 16, SUB):
            pairs = [i * 16 + sub + n for n in range(SUB)]
            rows = [widen(*(load((hi_ref, lo_ref), 4 * q + 2 * c + h) for c in range(2))) for q in pairs for h in range(2)]
            merged = product(rows, k3_ref[1])
            for n in range(2 * SUB):
                box = 2 * pairs[0] + n
                c, s = factors(1, box, 1, cos_ref, sin_ref)
                re, im = rotate(merged[ROWS * n : ROWS * n + ROWS], c, s)
                for top, tile in enumerate(by_top(re, im)):
                    outs[2 * top][box], outs[2 * top + 1][box] = split_two(tile)


def first_kernel(w_ref, a_ref, k_ref, *refs):
    outs, (cos0_ref, sin0_ref, cos1_ref, sin1_ref), scratch = refs[:4], refs[4:8], refs[8:]
    build_tables(w_ref[0], a_ref, ((cos0_ref, sin0_ref), (cos1_ref, sin1_ref)))
    early_steps(a_ref, ROWS + SLOPES, k_ref, cos0_ref, sin0_ref, outs, *scratch)


def second_kernel(a_ref, k_ref, cos_ref, sin_ref, *refs):
    early_steps(a_ref, ROWS, k_ref, cos_ref, sin_ref, refs[:4], *refs[4:])


def late_kernel(
    x1, hi_ref, lo_ref, k_ref, e_ref, cos_ref, sin_ref, own_ref, send_ref, hi0_ref, lo0_ref, hi1_ref, lo1_ref, k3_ref, e3_ref
):
    fill_matrices(k_ref, k3_ref)
    high, low = split_two(e_ref[...])
    e3_ref[:, 0:256] = high
    e3_ref[:, 256:512] = high
    e3_ref[:, 512:768] = low
    states = ((hi0_ref, lo0_ref), (hi1_ref, lo1_ref))

    def finish(merged, n, step, box, direction):
        c, s = factors(step, insert_bit(box, 3, x1), direction, cos_ref, sin_ref)
        return rotate(merged[ROWS * n : ROWS * n + ROWS], c, s)

    def store(state, box, re, im):
        for top, tile in enumerate(by_top(re, im)):
            state[0][2 * box + top], state[1][2 * box + top] = split_two(tile)

    for sub in range(0, 32, 2 * SUB):
        boxes = range(sub, sub + 2 * SUB)
        rows = [widen(*(load((hi_ref, lo_ref), insert_bit(box, 3, c)) for c in range(2))) for box in boxes]
        merged = product(rows, k3_ref[0])
        for n, box in enumerate(boxes):
            store(states[0], box, *finish(merged, n, 2, box, 0))

    def middle(step, bit, direction, source, target):
        for sub in range(0, 16, SUB):
            pairs = [[insert_bit(sub + n, bit, c) for c in range(2)] for n in range(SUB)]
            rows = [widen(*(load(source, 2 * box + h) for box in pair)) for pair in pairs for h in range(2)]
            merged = product(rows, k3_ref[direction])
            for n in range(2 * SUB):
                box = pairs[n // 2][n % 2]
                store(target, box, *finish(merged, n, step, box, direction))

    @pl.loop(0, 2)
    def _(level):
        middle(2 * level + 3, level + 1, 1, states[0], states[1])
        middle(2 * level + 4, level + 3, 0, states[1], states[0])

    for sub in range(0, 16, SUB):
        boxes = [[2 * (sub + n) + c for c in range(2)] for n in range(SUB)]
        rows = [widen(*(load(states[0], 2 * box + h) for box in pair)) for pair in boxes for h in range(2)]
        merged = product(rows, k3_ref[1])
        rows = [None] * (2 * SUB)
        for n in range(2 * SUB):
            high, low = split_two(jnp.concatenate(finish(merged, n, 7, 2 * sub + n, 1), axis=1))
            rows[n // 4 * 4 + (0, 2, 1, 3)[n % 4]] = jnp.concatenate([high, low, high], axis=1)
        field = lax.dot_general(
            e3_ref[...], jnp.concatenate(rows, axis=0), (((1,), (1,)), ((), ())), preferred_element_type=F32
        )
        own_ref[:, 64 * sub : 64 * sub + 64 * SUB] = field[0:64]
        send_ref[:, 64 * sub : 64 * sub + 64 * SUB] = field[64:128]


VMEM = pl.BlockSpec(memory_space=pltpu.VMEM)
TABLE = jax.ShapeDtypeStruct((32, ROWS, 128), F32)
HALF = jax.ShapeDtypeStruct((64, ROWS, 128), BF16)
FIELD = jax.ShapeDtypeStruct((64, 1024), F32)
MATRICES = pltpu.VMEM((2, 768, 256), BF16)


def cost(flops):
    return pl.CostEstimate(flops=flops, bytes_accessed=4 << 20, transcendentals=0)


def first_part(w, arrived, k):
    return pl.pallas_call(
        first_kernel,
        out_shape=[HALF] * 4 + [TABLE] * 4,
        in_specs=[pl.BlockSpec(memory_space=pltpu.SMEM), VMEM, VMEM],
        out_specs=[VMEM] * 8,
        scratch_shapes=[pltpu.VMEM((128, ROWS, 128), BF16)] * 2 + [MATRICES],
        compiler_params=pltpu.CompilerParams(vmem_limit_bytes=MAIN_VMEM),
        cost_estimate=cost(4_000_000_000),
    )(w, arrived, k)


def second_part(arrived, k, cos, sin):
    return pl.pallas_call(
        second_kernel,
        out_shape=[HALF] * 4,
        in_specs=[VMEM] * 4,
        out_specs=[VMEM] * 4,
        scratch_shapes=[pltpu.VMEM((128, ROWS, 128), BF16)] * 2 + [MATRICES],
        compiler_params=pltpu.CompilerParams(vmem_limit_bytes=MAIN_VMEM),
        cost_estimate=cost(3_000_000_000),
    )(arrived, k, cos, sin)


def late_part(x1, high, low, k, e, cos, sin):
    return pl.pallas_call(
        functools.partial(late_kernel, x1),
        out_shape=[FIELD, FIELD],
        in_specs=[VMEM] * 6,
        out_specs=[VMEM] * 2,
        scratch_shapes=[pltpu.VMEM((64, ROWS, 128), BF16)] * 4 + [MATRICES, pltpu.VMEM((128, 768), BF16)],
        compiler_params=pltpu.CompilerParams(vmem_limit_bytes=MAIN_VMEM),
        cost_estimate=cost(5_000_000_000),
    )(high, low, k, e, cos, sin)


def join_kernel(place, w_ref, own_ref, got_ref, *rest):
    out_ref, held_ref, sems = rest[-3:]
    first = w_ref[0] == 0
    lane = lax.broadcasted_iota(jnp.int32, (64, 128), 1)
    even = lane // 32 % 2 == 0
    copies = []
    for box in range(4):
        for y2 in range(2):
            lanes = slice(256 * box + 128 * y2, 256 * box + 128 * y2 + 128)
            own = own_ref[:, lanes]
            got = got_ref[:, lanes]
            a = jnp.where(first, own, got)
            b = jnp.where(first, got, own)
            held_ref[box, :, 256 * y2 : 256 * y2 + 128] = jnp.where(even, a, pltpu.roll(b, 32, 1))
            held_ref[box, :, 256 * y2 + 128 : 256 * y2 + 256] = jnp.where(even, pltpu.roll(a, 96, 1), b)
        at = (4 * box + place) * 512
        copies.append(pltpu.make_async_copy(held_ref.at[box], out_ref.at[:, at : at + 512], sems.at[box]))
        copies[-1].start()
    for copy in copies:
        copy.wait()


def join(w, own, got, place, out):
    more = [] if out is None else [out]
    anywhere = pl.BlockSpec(memory_space=pl.ANY)
    return pl.pallas_call(
        functools.partial(join_kernel, place),
        out_shape=jax.ShapeDtypeStruct((64, 8192), F32),
        in_specs=[pl.BlockSpec(memory_space=pltpu.SMEM), VMEM, VMEM] + [anywhere] * len(more),
        out_specs=anywhere,
        scratch_shapes=[pltpu.VMEM((4, 64, 512), F32), pltpu.SemaphoreType.DMA((4,))],
        input_output_aliases={3: 0} if more else {},
        compiler_params=pltpu.CompilerParams(vmem_limit_bytes=MAIN_VMEM),
        cost_estimate=pl.CostEstimate(flops=0, bytes_accessed=1 << 20, transcendentals=0),
    )(w, own, got, *more)


def merge_matrices(interp_matrix):
    re = jnp.transpose(interp_matrix[:, 0], (0, 3, 4, 1, 2)).reshape(2, 2, 64, 128)
    im = jnp.transpose(interp_matrix[:, 1], (0, 3, 4, 1, 2)).reshape(2, 2, 64, 128)
    from_re = jnp.concatenate([re, im], axis=3)
    from_im = jnp.concatenate([-im, re], axis=3)
    return jnp.stack([from_re, from_im], axis=2).reshape(2, 256, 256)


def evaluation_matrix(evaluation, w):
    zero = jnp.zeros((64, 64), F32)
    re, im = evaluation[0], -evaluation[1]
    low = jnp.concatenate([re, zero, im, zero], axis=1)
    high = jnp.concatenate([zero, re, zero, im], axis=1)
    return jnp.where(w == 0, jnp.concatenate([low, high], axis=0), jnp.concatenate([high, low], axis=0))


def shards(weights, phase_slope, interp_matrix, evaluation):
    w = lax.axis_index("bx") >> 3
    w_one = w.astype(jnp.int32).reshape(1)
    planes = weights.reshape(128, 8192)
    k = merge_matrices(interp_matrix)
    e = evaluation_matrix(evaluation, w)

    def spread(packed):
        return lax.all_to_all(packed, AXES, split_axis=0, concat_axis=0, tiled=True).reshape(-1, 128)

    def swap(field):
        return lax.ppermute(field, "bx", [(i, i ^ 8) for i in range(16)])

    arrived0 = spread(pack(planes, phase_slope.reshape(8, 1, 8192), 0))
    arrived1 = spread(pack(planes, None, 1))
    out = None
    for top in range(2):
        if top == 0:
            *halves, cos, sin, cos1, sin1 = first_part(w_one, arrived0, k)
        else:
            cos, sin = cos1, sin1
            halves = second_part(arrived1, k, cos, sin)
        for x1 in range(2):
            own, send = late_part(x1, halves[2 * x1], halves[2 * x1 + 1], k, e, cos, sin)
            out = join(w_one, own, swap(send), 2 * x1 + top, out)
    return out[None, None]


def solution(mesh):
    in_specs = (P("bx", "by", None, None, None), P(None, "bx", "by", None), P(), P())
    out_specs = P("bx", "by", None, None)
    return jax.shard_map(shards, mesh=mesh, in_specs=in_specs, out_specs=out_specs, check_vma=False)
```

time: 146 us -> 113 us (0.77)
  waiting for transfers between devices: 79.5 us -> 37.2 us
  starting transfers between devices: 12.8 us -> 22.5 us
  local copies, waits for them, and re-layouts: 5.75 us -> 2.13 us
  Pallas kernels: 46.5 us -> 49.3 us
    all_to_all x1 -> x2, waiting for transfers between devices: 56.5 us -> 34.2 us  [spread(): lax.all_to_all(packed, AXES, split_axis=0, concat_axis=0, tiled=True)]
    ppermute x1 -> x4, waiting for transfers between devices: 23 us -> 3.06 us  [swap(): return lax.ppermute(field, 'bx', [(i, i ^ 8) for i in range(16)])]
    all_to_all x1 -> x2, starting transfers between devices: 11.6 us -> 18 us  [spread(): lax.all_to_all(packed, AXES, split_axis=0, concat_axis=0, tiled=True)]
    unnamed x9 -> x14, local copies, waits for them, and re-layouts: 5.48 us -> 0.81 us
    ppermute x1 -> x4, starting transfers between devices: 1.16 us -> 4.55 us  [swap(): return lax.ppermute(field, 'bx', [(i, i ^ 8) for i in range(16)])]
    pallas_call x3 -> x12, Pallas kernels: 46.5 us -> 49.3 us  [the longest x4 22 us: late_part(): pl.pallas_call(functools.partial(late_kernel, x1), out_shape=[FIELD, FIEL...]
  transfers between devices with their start and end apart: 2 -> 6, of which waited for: 2 -> 3; matrix products, arithmetic and copies ran while one was open for 0% -> 1% of each run, Pallas kernels for 0% -> 38%
where the time goes in v2:
time: 113 us; the launch traced here: 112 us
  Pallas kernels  49.3 us (44%)
  waiting for transfers between devices  37.2 us (33%)
  starting transfers between devices  22.5 us (20%)
  local copies, waits for them, and re-layouts  2.13 us (2%)
    all_to_all x2, waiting for transfers between devices, spread(): lax.all_to_all(packed, AXES, split_axis=0, concat_axis=0, tiled=True)  34.2 us
    pallas_call x4, Pallas kernels, late_part(): pl.pallas_call(functools.partial(late_kernel, x1), out_shape=[FIELD, FIEL...  22 us
    all_to_all x2, starting transfers between devices, spread(): lax.all_to_all(packed, AXES, split_axis=0, concat_axis=0, tiled=True)  18 us
    pallas_call x2, Pallas kernels, pack(): pl.pallas_call(kernel, out_shape=jax.ShapeDtypeStruct((2, 64, rows, 128),...  12.4 us
    pallas_call x1, Pallas kernels, first_part(): pl.pallas_call(first_kernel, out_shape=[HALF] * 4 + [TABLE] * 4, in_specs...  6.34 us
    pallas_call x1, Pallas kernels, second_part(): pl.pallas_call(second_kernel, out_shape=[HALF] * 4, in_specs=[VMEM] * 4,...  4.99 us
    ppermute x4, starting transfers between devices, swap(): return lax.ppermute(field, 'bx', [(i, i ^ 8) for i in range(16)])  4.55 us
    pallas_call x4, Pallas kernels, join(): pl.pallas_call(functools.partial(join_kernel, place), out_shape=jax.Shape...  3.7 us
  transfers between devices with their start and end apart: 6, of which 3 were waited for; matrix products, arithmetic and copies ran while one was open for 1% of the time, Pallas kernels for 38%

profile of v2, /device:TPU:0, one launch (start us, length us, event | category | flops | bytes accessed | tf_op | source)
XLA Modules:
  0.0 111.9 jit_solution(5179378659295202860)
XLA Ops:
  0.0 6.3 %shard_map.47 = f32[2,64,40,128]{3,2,1,0:T(8,128)} custom-call(f32[128,8192]{1,0:T(8,128)} %bitcast.34, f32[8,1,8192]{2,1,0:T(1,128)} %bitcast.38, f32[8,1,8192]{2,1,0:T(1,128)} %bitcast.39), custom_call_target="tpu_custom_call" | custom-call | bytes 5242880 | tf_op jit(solution)/shard_map/pallas_call | solution.py:56
  6.3 11.1 %all-to-all-start.1 = ((f32[128,40,128]{2,1,0:T(8,128)}), f32[128,40,128]{2,1,0:T(8,128)S(1)}, u32[]{:S(2)}, u32[]{:S(2)}) async-start(f32[128,40,128]{2,1,0:T(8,128)} %bitcast.36), calls=%async_computation.1 | async-start | bytes 5242880 | tf_op jit(solution)/shard_map/all_to_all | solution.py:373
  17.5 6.0 %shard_map.46 = f32[2,64,32,128]{3,2,1,0:T(8,128)} custom-call(f32[128,8192]{1,0:T(8,128)} %bitcast.35), custom_call_target="tpu_custom_call" | custom-call | bytes 5242880 | tf_op jit(solution)/shard_map/pallas_call | solution.py:56
  23.5 28.2 %all-to-all-done.1 = f32[128,40,128]{2,1,0:T(8,128)S(1)} async-done(((f32[128,40,128]{2,1,0:T(8,128)}), f32[128,40,128]{2,1,0:T(8,128)S(1)}, u32[]{:S(2)}, u32[]{:S(2)}) %all-to-all-start.1) | async-done | bytes 2621472 | tf_op jit(solution)/shard_map/all_to_all | solution.py:373
  51.7 6.8 %all-to-all-start = ((f32[128,32,128]{2,1,0:T(8,128)}), f32[128,32,128]{2,1,0:T(8,128)}, u32[]{:S(2)}, u32[]{:S(2)}) async-start(f32[128,32,128]{2,1,0:T(8,128)} %bitcast.37), calls=%async_computation | async-start | bytes 4194304 | tf_op jit(solution)/shard_map/all_to_all | solution.py:373
  58.5 0.0 copy-start.6
  58.6 1.1 fusion
  59.7 0.1 copy.9
  59.8 0.1 copy.8
  59.9 0.0 copy-done.6
  60.0 0.2 maximum_select_fusion.e_ref
  60.2 6.3 %shard_map.48 = (bf16[64,32,128]{2,1,0:T(8,128)(2,1)S(1)}, bf16[64,32,128]{2,1,0:T(8,128)(2,1)S(1)}, bf16[64,32,128]{2,1,0:T(8,128)(2,1)S(1)}, bf16[64,32,128]{2...) custom-call(s32[1]{0:T(128)} %bitcast.w_ref, ...), custom_call_target="tpu_custom_call" | custom-call | flops 4000000000 | bytes 4194304 | tf_op jit(solution)/shard_map/pallas_call | solution.py:277
  66.6 0.0 copy-start.3
  66.6 0.8 copy-done.3
  67.4 0.0 copy-start
  67.4 5.5 %shard_map.53 = (f32[64,1024]{1,0:T(8,128)S(1)}, f32[64,1024]{1,0:T(8,128)S(1)}) custom-call(bf16[64,32,128]{2,1,0:T(8,128)(2,1)S(1)} %get-tuple-element.41.hi_ref, bf16[64,32,128]{2,1,0:T(8,128)(2,1)S(1)} %get-tuple-element.42.lo_ref, f32[2,256,256]{2,1,0:T(8,128)S(1)} %bitcast.29, f32[128,256]{1,0:T(8,128)S(1)} %maximum_select_fusion.e_ref, ...), custom_call_target="tpu_custom_call" | custom-call | flops 5000000000 | bytes 4194304 | tf_op jit(solution)/shard_map/pallas_call | solution.py:301
  72.9 0.0 copy-done
  72.9 1.0 collective-permute-start.3
  73.9 0.0 copy-start.1
  73.9 0.0 copy-start.4
  73.9 5.5 %shard_map.52 = (f32[64,1024]{1,0:T(8,128)S(1)}, f32[64,1024]{1,0:T(8,128)S(1)}) custom-call(bf16[64,32,128]{2,1,0:T(8,128)(2,1)S(1)} %get-tuple-element.35.hi_ref, bf16[64,32,128]{2,1,0:T(8,128)(2,1)S(1)} %get-tuple-element.36.lo_ref, f32[2,256,256]{2,1,0:T(8,128)S(1)} %bitcast.30, f32[128,256]{1,0:T(8,128)S(1)} %maximum_select_fusion.e_ref, ...), custom_call_target="tpu_custom_call" | custom-call | flops 5000000000 | bytes 4194304 | tf_op jit(solution)/shard_map/pallas_call | solution.py:301
  79.4 1.4 %collective-permute-start.2 = (f32[64,1024]{1,0:T(8,128)S(1)}, f32[64,1024]{1,0:T(8,128)S(1)}, u32[]{:S(2)}, u32[]{:S(2)}) collective-permute-start(f32[64,1024]{1,0:T(8,128)S(1)} %get-tuple-element.40), channel_id=1, source_target_pairs={{0,64},{8,72},{16,80},{24,88},{32,96},{40,104},{48,112},{56,120},{... | collective-permute-start | bytes 786440 | tf_op jit(solution)/shard_map/ppermute | solution.py:376
  80.8 6.0 %all-to-all-done = f32[128,32,128]{2,1,0:T(8,128)} async-done(((f32[128,32,128]{2,1,0:T(8,128)}), f32[128,32,128]{2,1,0:T(8,128)}, u32[]{:S(2)}, u32[]{:S(2)}) %all-to-all-start) | async-done | bytes 2097184 | tf_op jit(solution)/shard_map/all_to_all | solution.py:373
  86.8 0.0 copy-done.1
  86.8 0.0 copy-done.4
  86.8 0.0 copy-start.5
  86.8 5.0 %shard_map.49 = (bf16[64,32,128]{2,1,0:T(8,128)(2,1)S(1)}, bf16[64,32,128]{2,1,0:T(8,128)(2,1)S(1)}, bf16[64,32,128]{2,1,0:T(8,128)(2,1)S(1)}, bf16[64,32,128]{2,1,0:T(8,128)(2,1)S(1)}) custom-call(f32[4096,128]{1,0:T(8,128)} %bitcast.3.a_ref, f32[2,256,256]{2,1,0:T(8,128)S(1)} %bitcast.31, f32[32,32,128]{2,1,0:T(8,128)S(1)} %copy-done.1, ...), custom_call_target="tpu_custom_call" | custom-call | flops 3000000000 | bytes 4194304 | tf_op jit(solution)/shard_map/pallas_call | solution.py:289
  91.8 0.0 copy-done.5
  91.8 0.0 copy-start.2
  91.8 5.4 %shard_map.51 = (f32[64,1024]{1,0:T(8,128)S(1)}, f32[64,1024]{1,0:T(8,128)S(1)}) custom-call(bf16[64,32,128]{2,1,0:T(8,128)(2,1)S(1)} %get-tuple-element.31.hi_ref, bf16[64,32,128]{2,1,0:T(8,128)(2,1)S(1)} %get-tuple-element.32.lo_ref, f32[2,256,256]{2,1,0:T(8,128)S(1)} %bitcast.32, f32[128,256]{1,0:T(8,128)S(1)} %maximum_select_fusion.e_ref, ...), custom_call_target="tpu_custom_call" | custom-call | flops 5000000000 | bytes 4194304 | tf_op jit(solution)/shard_map/pallas_call | solution.py:301
  97.2 0.4 collective-permute-start.1
  97.6 0.0 copy-done.2
  97.6 5.5 %shard_map.50 = (f32[64,1024]{1,0:T(8,128)S(1)}, f32[64,1024]{1,0:T(8,128)S(1)}) custom-call(bf16[64,32,128]{2,1,0:T(8,128)(2,1)S(1)} %get-tuple-element.27.hi_ref, bf16[64,32,128]{2,1,0:T(8,128)(2,1)S(1)} %get-tuple-element.28.lo_ref, f32[2,256,256]{2,1,0:T(8,128)S(1)} %bitcast.33, f32[128,256]{1,0:T(8,128)S(1)} %maximum_select_fusion.e_ref, ...), custom_call_target="tpu_custom_call" | custom-call | flops 5000000000 | bytes 4194304 | tf_op jit(solution)/shard_map/pallas_call | solution.py:301
  103.1 1.8 %collective-permute-start = (f32[64,1024]{1,0:T(8,128)S(1)}, f32[64,1024]{1,0:T(8,128)S(1)}, u32[]{:S(2)}, u32[]{:S(2)}) collective-permute-start(f32[64,1024]{1,0:T(8,128)S(1)} %get-tuple-element.30), channel_id=1, source_target_pairs={{0,64},{8,72},{16,80},{24,88},{32,96},{40,104},{48,112},{56,120},{... | collective-permute-start | bytes 786440 | tf_op jit(solution)/shard_map/ppermute | solution.py:376
  104.9 0.0 collective-permute-done.3.got_ref
  104.9 0.9 shard_map.54.rest_0_
  105.8 0.0 collective-permute-done.2.got_ref
  105.8 0.9 shard_map.55.rest_0_
  106.8 0.0 collective-permute-done.1.got_ref
  106.8 0.9 shard_map.56.rest_0_
  107.7 3.1 %collective-permute-done.got_ref = f32[64,1024]{1,0:T(8,128)S(1)} collective-permute-done((f32[64,1024]{1,0:T(8,128)S(1)}, f32[64,1024]{1,0:T(8,128)S(1)}, u32[]{:S(2)}, u32[]{:S(2)}) %collective-permute-start) | collective-permute-done | bytes 262176 | tf_op jit(solution)/shard_map/ppermute | solution.py:376
  110.8 0.9 shard_map.57
  (5 shorter events, 0.1 us)
Async XLA Ops:
  6.3 45.4 %all-to-all-start.1 = ((f32[128,40,128]{2,1,0:T(8,128)}), f32[128,40,128]{2,1,0:T(8,128)S(1)}, u32[]{:S(2)}, u32[]{:S(2)}) async-start(f32[128,40,128]{2,1,0:T(8,128)} %bitcast.36), calls=%async_computation.1 | async-start | bytes 5242880 | tf_op jit(solution)/shard_map/all_to_all | solution.py:373
  51.7 35.0 %all-to-all-start = ((f32[128,32,128]{2,1,0:T(8,128)}), f32[128,32,128]{2,1,0:T(8,128)}, u32[]{:S(2)}, u32[]{:S(2)}) async-start(f32[128,32,128]{2,1,0:T(8,128)} %bitcast.37), calls=%async_computation | async-start | bytes 4194304 | tf_op jit(solution)/shard_map/all_to_all | solution.py:373
  58.5 1.4 %copy-start.6 = (f32[2,64,64]{2,1,0:T(8,128)S(1)}, f32[2,64,64]{2,1,0:T(8,128)}, u32[]{:S(2)}) copy-start(f32[2,64,64]{2,1,0:T(8,128)} %param.7) | copy-start | bytes 98308
  66.6 0.8 copy-start.3
  67.4 5.5 %copy-start = (f32[32,32,128]{2,1,0:T(8,128)}, f32[32,32,128]{2,1,0:T(8,128)S(1)}, u32[]{:S(2)}) copy-start(f32[32,32,128]{2,1,0:T(8,128)S(1)} %get-tuple-element.25.cos_ref) | copy-start | bytes 1572868
  72.9 32.0 %collective-permute-start.3 = (f32[64,1024]{1,0:T(8,128)S(1)}, f32[64,1024]{1,0:T(8,128)S(1)}, u32[]{:S(2)}, u32[]{:S(2)}) collective-permute-start(f32[64,1024]{1,0:T(8,128)S(1)} %get-tuple-element.44), channel_id=1, source_target_pairs={{0,64},{8,72},{16,80},{24,88},{32,96},{40,104},{48,112},{56,120},{... | collective-permute-start | bytes 786440 | tf_op jit(solution)/shard_map/ppermute | solution.py:376
  73.9 12.9 %copy-start.1 = (f32[32,32,128]{2,1,0:T(8,128)S(1)}, f32[32,32,128]{2,1,0:T(8,128)}, u32[]{:S(2)}) copy-start(f32[32,32,128]{2,1,0:T(8,128)} %copy-done) | copy-start | bytes 1572868
  73.9 12.9 %copy-start.4 = (f32[32,32,128]{2,1,0:T(8,128)S(1)}, f32[32,32,128]{2,1,0:T(8,128)}, u32[]{:S(2)}) copy-start(f32[32,32,128]{2,1,0:T(8,128)} %copy-done.3) | copy-start | bytes 1572868
  79.4 26.5 %collective-permute-start.2 = (f32[64,1024]{1,0:T(8,128)S(1)}, f32[64,1024]{1,0:T(8,128)S(1)}, u32[]{:S(2)}, u32[]{:S(2)}) collective-permute-start(f32[64,1024]{1,0:T(8,128)S(1)} %get-tuple-element.40), channel_id=1, source_target_pairs={{0,64},{8,72},{16,80},{24,88},{32,96},{40,104},{48,112},{56,120},{... | collective-permute-start | bytes 786440 | tf_op jit(solution)/shard_map/ppermute | solution.py:376
  86.8 5.0 %copy-start.5 = (f32[32,32,128]{2,1,0:T(8,128)S(1)}, f32[32,32,128]{2,1,0:T(8,128)}, u32[]{:S(2)}) copy-start(f32[32,32,128]{2,1,0:T(8,128)} %copy-done.3) | copy-start | bytes 1572868
  91.8 5.8 %copy-start.2 = (f32[32,32,128]{2,1,0:T(8,128)S(1)}, f32[32,32,128]{2,1,0:T(8,128)}, u32[]{:S(2)}) copy-start(f32[32,32,128]{2,1,0:T(8,128)} %copy-done) | copy-start | bytes 1572868
  97.2 9.6 %collective-permute-start.1 = (f32[64,1024]{1,0:T(8,128)S(1)}, f32[64,1024]{1,0:T(8,128)S(1)}, u32[]{:S(2)}, u32[]{:S(2)}) collective-permute-start(f32[64,1024]{1,0:T(8,128)S(1)} %get-tuple-element.34), channel_id=1, source_target_pairs={{0,64},{8,72},{16,80},{24,88},{32,96},{40,104},{48,112},{56,120},{... | collective-permute-start | bytes 786440 | tf_op jit(solution)/shard_map/ppermute | solution.py:376
  103.1 7.7 %collective-permute-start = (f32[64,1024]{1,0:T(8,128)S(1)}, f32[64,1024]{1,0:T(8,128)S(1)}, u32[]{:S(2)}, u32[]{:S(2)}) collective-permute-start(f32[64,1024]{1,0:T(8,128)S(1)} %get-tuple-element.30), channel_id=1, source_target_pairs={{0,64},{8,72},{16,80},{24,88},{32,96},{40,104},{48,112},{56,120},{... | collective-permute-start | bytes 786440 | tf_op jit(solution)/shard_map/ppermute | solution.py:376

commit v3 on v2

--- a/solution.py
+++ b/solution.py
@@ -9,10 +9,11 @@
 from jax.sharding import PartitionSpec as P
 
 PACK_VMEM = 60 << 20
+PACK_BLOCK = 1024
 MAIN_VMEM = 24 << 20
 AXES = ("bx", "by")
 ROWS = 32
-SLOPES = 8
+SLOPES = 4
 NODES = [float(np.cos(np.pi * (2 * m + 1) / 16)) for m in range(4)]
 F32 = jnp.float32
 BF16 = jnp.bfloat16
@@ -24,45 +25,46 @@
     return high, low
 
 
-def pack_weights_kernel(w_ref, out_ref):
+def pack_kernel(w_ref, *refs):
+    *slopes, out_ref = refs
+    rows = ROWS + SLOPES * (len(slopes) > 0)
     for pair in range(w_ref.shape[1] // 128):
         turned = w_ref[:, pair * 128 : pair * 128 + 128].T
         for b in range(2):
             for w in range(2):
                 at = 64 * b + 32 * w
-                out_ref[w, 2 * pair + b, 0:ROWS, :] = turned[at : at + 32]
-
-
-def pack_both_kernel(w_ref, p0_ref, p1_ref, out_ref):
-    pack_weights_kernel(w_ref, out_ref)
-    for b in range(w_ref.shape[1] // 64):
-        both = jnp.concatenate([p_ref[:, 0, 64 * b : 64 * b + 64] for p_ref in (p0_ref, p1_ref)], axis=1)
-        for w in range(2):
-            out_ref[w, b, ROWS : ROWS + SLOPES, :] = both
+                to = (2 * pair + b) * rows
+                out_ref[w, to : to + ROWS, :] = turned[at : at + 32]
+    if slopes:
+        p0 = slopes[0][:, 0, :]
+        p1 = slopes[1][:, 0, :]
+        for b in range(w_ref.shape[1] // 64):
+            for w in range(2):
+                at = slice(64 * b + 32 * w, 64 * b + 32 * w + 32)
+                parts = [p0[0:4, at], p1[0:4, at], p0[4:8, at], p1[4:8, at]]
+                out_ref[w, b * rows + ROWS : b * rows + rows, :] = jnp.concatenate(parts, axis=1)
 
 
 def pack(weights, slopes, top):
-    block = 512
+    block = PACK_BLOCK
     half = weights.shape[1] // 2 // block
     first = top * half
-    if slopes is None:
-        kernel, rows, more, specs = pack_weights_kernel, ROWS, [], []
-    else:
-        kernel, rows, more = pack_both_kernel, ROWS + SLOPES, [slopes, slopes]
+    rows, more, specs = ROWS, [], []
+    if slopes is not None:
+        rows, more = ROWS + SLOPES, [slopes, slopes]
         specs = [
             pl.BlockSpec((8, 1, block), lambda i: (0, 0, i)),
             pl.BlockSpec((8, 1, block), lambda i: (0, 0, i + half)),
         ]
-    out = pl.pallas_call(
-        kernel,
-        out_shape=jax.ShapeDtypeStruct((2, 64, rows, 128), F32),
+    return pl.pallas_call(
+        pack_kernel,
+        out_shape=jax.ShapeDtypeStruct((2, 64 * rows, 128), F32),
         grid=(half,),
         in_specs=[pl.BlockSpec((128, block), lambda i: (0, first + i))] + specs,
-        out_specs=pl.BlockSpec((2, block // 64, rows, 128), lambda i: (0, i, 0, 0)),
+        out_specs=pl.BlockSpec((2, block // 64 * rows, 128), lambda i: (0, i, 0)),
         compiler_params=pltpu.CompilerParams(vmem_limit_bytes=PACK_VMEM),
         cost_estimate=pl.CostEstimate(flops=0, bytes_accessed=5 << 20, transcendentals=0),
     )(weights, *more)
-    return out.reshape(128, rows, 128)
 
 
 def sincos(angle):
@@ -86,26 +88,27 @@
     return jnp.take_along_axis(value, index, axis=1, mode="promise_in_bounds")
 
 
-def build_tables(w, a_ref, tables):
+def build_tables(a_ref, tables):
     lane = lax.broadcasted_iota(jnp.int32, (ROWS, 128), 1)
     m = lane % 4
     node = jnp.where(m == 0, NODES[0], jnp.where(m == 1, NODES[1], jnp.where(m == 2, NODES[2], NODES[3])))
     second = lane // 4 % 2 == 1
     g = lane // 8
 
-    @pl.loop(0, 8)
-    def _(step):
-        slab = a_ref[pl.ds(ROWS + step, 128, stride=ROWS + SLOPES), :]
-        turned = slab.T
-        t0 = jnp.where(w == 0, turned[0:32], turned[32:64])
-        t1 = jnp.where(w == 0, turned[64:96], turned[96:128])
-        for tile in range(4):
-            for h, (cos_ref, sin_ref) in enumerate(tables):
-                index = ((2 * (2 * tile + g // 8) + h) * 8) + g % 8
-                slope = jnp.where(second, lane_gather(t1, index), lane_gather(t0, index))
-                s, c = sincos(slope * node)
-                cos_ref[step * 4 + tile] = c
-                sin_ref[step * 4 + tile] = s
+    @pl.loop(0, SLOPES)
+    def _(row):
+        turned = a_ref[pl.ds(ROWS + row, 128, stride=ROWS + SLOPES), :].T
+        for late in range(2):
+            t0 = turned[64 * late : 64 * late + 32]
+            t1 = turned[64 * late + 32 : 64 * late + 64]
+            for tile in range(4):
+                for h, (cos_ref, sin_ref) in enumerate(tables):
+                    index = ((2 * (2 * tile + g // 8) + h) * 8) + g % 8
+                    slope = jnp.where(second, lane_gather(t1, index), lane_gather(t0, index))
+                    s, c = sincos(slope * node)
+                    at = (row + SLOPES * late) * 4 + tile
+                    cos_ref[at] = c
+                    sin_ref[at] = s
 
 
 def factors(step, box, direction, cos_ref, sin_ref):
@@ -162,21 +165,21 @@
 def early_steps(a_ref, stride, k_ref, cos_ref, sin_ref, outs, hi_ref, lo_ref, k3_ref):
     fill_matrices(k_ref, k3_ref)
 
+    def arrived(pair, odd):
+        at = pl.multiple_of(pair * 2 * stride, 8)
+        if stride % 8 == 0:
+            return a_ref[pl.ds(at + odd * stride, ROWS), :]
+        shift = odd * stride % 8
+        return a_ref[pl.ds(at + (odd * stride - shift), ROWS + 2 * shift), :][shift : shift + ROWS]
+
     @pl.loop(0, 2)
     def _(i):
         for sub in range(0, 32, 2 * SUB):
             boxes = [i * 32 + sub + n for n in range(2 * SUB)]
             rows = []
-            for box in boxes:
-                at = box // 8 * 16 + box % 8
-                rows.append(
-                    widen(
-                        *(
-                            split_two(a_ref[pl.ds(pl.multiple_of((at + 8 * c) * stride, 8), ROWS), :])
-                            for c in range(2)
-                        )
-                    )
-                )
+            for n in range(2 * SUB):
+                pair = (i * 32 + sub) // 8 * 8 + n // 2 + sub % 8 // 2
+                rows.append(widen(*(split_two(arrived(pair + 4 * c, n % 2)) for c in range(2))))
             merged = product(rows, k3_ref[0])
             for n, box in enumerate(boxes):
                 c, s = factors(0, box, 0, cos_ref, sin_ref)
@@ -198,9 +201,9 @@
                     outs[2 * top][box], outs[2 * top + 1][box] = split_two(tile)
 
 
-def first_kernel(w_ref, a_ref, k_ref, *refs):
+def first_kernel(a_ref, k_ref, *refs):
     outs, (cos0_ref, sin0_ref, cos1_ref, sin1_ref), scratch = refs[:4], refs[4:8], refs[8:]
-    build_tables(w_ref[0], a_ref, ((cos0_ref, sin0_ref), (cos1_ref, sin1_ref)))
+    build_tables(a_ref, ((cos0_ref, sin0_ref), (cos1_ref, sin1_ref)))
     early_steps(a_ref, ROWS + SLOPES, k_ref, cos0_ref, sin0_ref, outs, *scratch)
 
 
@@ -273,16 +276,16 @@
     return pl.CostEstimate(flops=flops, bytes_accessed=4 << 20, transcendentals=0)
 
 
-def first_part(w, arrived, k):
+def first_part(arrived, k):
     return pl.pallas_call(
         first_kernel,
         out_shape=[HALF] * 4 + [TABLE] * 4,
-        in_specs=[pl.BlockSpec(memory_space=pltpu.SMEM), VMEM, VMEM],
+        in_specs=[VMEM, VMEM],
         out_specs=[VMEM] * 8,
         scratch_shapes=[pltpu.VMEM((128, ROWS, 128), BF16)] * 2 + [MATRICES],
         compiler_params=pltpu.CompilerParams(vmem_limit_bytes=MAIN_VMEM),
         cost_estimate=cost(4_000_000_000),
-    )(w, arrived, k)
+    )(arrived, k)
 
 
 def second_part(arrived, k, cos, sin):
@@ -370,7 +373,7 @@
     e = evaluation_matrix(evaluation, w)
 
     def spread(packed):
-        return lax.all_to_all(packed, AXES, split_axis=0, concat_axis=0, tiled=True).reshape(-1, 128)
+        return lax.all_to_all(packed.reshape(128, 1, -1), AXES, split_axis=0, concat_axis=0, tiled=True).reshape(-1, 128)
 
     def swap(field):
         return lax.ppermute(field, "bx", [(i, i ^ 8) for i in range(16)])
@@ -380,7 +383,7 @@
     out = None
     for top in range(2):
         if top == 0:
-            *halves, cos, sin, cos1, sin1 = first_part(w_one, arrived0, k)
+            *halves, cos, sin, cos1, sin1 = first_part(arrived0, k)
         else:
             cos, sin = cos1, sin1
             halves = second_part(arrived1, k, cos, sin)

time: 113 us -> 108 us (0.956)
  Pallas kernels: 49.3 us -> 44.1 us
  waiting for transfers between devices: 37.2 us -> 38.5 us
    pallas_call x2, Pallas kernels: 12.4 us -> 8.57 us  [pack(): pl.pallas_call(pack_kernel, out_shape=jax.ShapeDtypeStruct((2, 64 * rows,...]
    all_to_all x2, waiting for transfers between devices: 34.2 us -> 35.4 us  [spread(): lax.all_to_all(packed.reshape(128, 1, -1), AXES, split_axis=0, concat_axi...]
    pallas_call x1, Pallas kernels: 6.34 us -> 5.14 us  [first_part(): pl.pallas_call(first_kernel, out_shape=[HALF] * 4 + [TABLE] * 4, in_specs...]
  transfers between devices with their start and end apart: 6 -> 6, of which waited for: 3 -> 3; matrix products, arithmetic and copies ran while one was open for 1% -> 1% of each run, Pallas kernels for 38% -> 36%
where the time goes in v3:
time: 108 us; the launch traced here: 107 us
  Pallas kernels  44.1 us (41%)
  waiting for transfers between devices  38.5 us (36%)
  starting transfers between devices  22.5 us (21%)
  local copies, waits for them, and re-layouts  1.35 us (1%)
    all_to_all x2, waiting for transfers between devices, spread(): lax.all_to_all(packed.reshape(128, 1, -1), AXES, split_axis=0, concat_axi...  35.4 us
    pallas_call x4, Pallas kernels, late_part(): pl.pallas_call(functools.partial(late_kernel, x1), out_shape=[FIELD, FIEL...  21.8 us
    all_to_all x2, starting transfers between devices, spread(): lax.all_to_all(packed.reshape(128, 1, -1), AXES, split_axis=0, concat_axi...  18 us
    pallas_call x2, Pallas kernels, pack(): pl.pallas_call(pack_kernel, out_shape=jax.ShapeDtypeStruct((2, 64 * rows,...  8.57 us
    pallas_call x1, Pallas kernels, first_part(): pl.pallas_call(first_kernel, out_shape=[HALF] * 4 + [TABLE] * 4, in_specs...  5.14 us
    pallas_call x1, Pallas kernels, second_part(): pl.pallas_call(second_kernel, out_shape=[HALF] * 4, in_specs=[VMEM] * 4,...  4.95 us
    ppermute x4, starting transfers between devices, swap(): return lax.ppermute(field, 'bx', [(i, i ^ 8) for i in range(16)])  4.55 us
    pallas_call x4, Pallas kernels, join(): pl.pallas_call(functools.partial(join_kernel, place), out_shape=jax.Shape...  3.69 us
  transfers between devices with their start and end apart: 6, of which 3 were waited for; matrix products, arithmetic and copies ran while one was open for 1% of the time, Pallas kernels for 36%

profile of v3, /device:TPU:0, one launch (start us, length us, event | category | flops | bytes accessed | tf_op | source)
XLA Modules:
  0.0 107.1 jit_solution(16104956712203480387)
XLA Ops:
  0.0 4.5 %shard_map.47 = f32[2,2304,128]{2,1,0:T(8,128)} custom-call(f32[128,8192]{1,0:T(8,128)} %bitcast.34, f32[8,1,8192]{2,1,0:T(1,128)} %bitcast.38, f32[8,1,8192]{2,1,0:T(1,128)} %bitcast.39), custom_call_target="tpu_custom_call" | custom-call | bytes 5242880 | tf_op jit(solution)/shard_map/pallas_call | solution.py:59
  4.5 11.1 %all-to-all-start.1 = ((f32[128,1,4608]{2,1,0:T(1,128)}), f32[128,1,4608]{2,1,0:T(1,128)S(1)}, u32[]{:S(2)}, u32[]{:S(2)}) async-start(f32[128,1,4608]{2,1,0:T(1,128)} %bitcast.36), calls=%async_computation.1 | async-start | bytes 4718592 | tf_op jit(solution)/shard_map/all_to_all | solution.py:376
  15.6 4.1 %shard_map.46 = f32[2,2048,128]{2,1,0:T(8,128)} custom-call(f32[128,8192]{1,0:T(8,128)} %bitcast.35), custom_call_target="tpu_custom_call" | custom-call | bytes 5242880 | tf_op jit(solution)/shard_map/pallas_call | solution.py:59
  19.7 27.3 %all-to-all-done.1 = f32[128,1,4608]{2,1,0:T(1,128)S(1)} async-done(((f32[128,1,4608]{2,1,0:T(1,128)}), f32[128,1,4608]{2,1,0:T(1,128)S(1)}, u32[]{:S(2)}, u32[]{:S(2)}) %all-to-all-start.1) | async-done | bytes 2359328 | tf_op jit(solution)/shard_map/all_to_all | solution.py:376
  47.0 6.8 %all-to-all-start = ((f32[128,1,4096]{2,1,0:T(1,128)}), f32[128,1,4096]{2,1,0:T(1,128)}, u32[]{:S(2)}, u32[]{:S(2)}) async-start(f32[128,1,4096]{2,1,0:T(1,128)} %bitcast.37), calls=%async_computation | async-start | bytes 4194304 | tf_op jit(solution)/shard_map/all_to_all | solution.py:376
  53.9 0.0 copy-start.3
  53.9 1.1 %fusion = (f32[2,1,2,64,2,64]{5,4,3,2,1,0:T(2,128)S(1)}, f32[2,1,2,64,2,64]{5,4,3,2,1,0:T(2,128)S(1)}) fusion(f32[2,2,2,64,2,64]{5,4,3,2,1,0:T(2,128)} %param.6), kind=kLoop, calls=%fused_computation.6 | loop fusion | bytes 524288 | tf_op jit(solution)/shard_map/slice | solution.py:354
  55.0 0.1 copy.14
  55.1 0.1 copy.13
  55.3 0.0 copy-done.3
  55.3 0.2 maximum_select_fusion.e_ref
  55.6 5.1 %shard_map.48 = (bf16[64,32,128]{2,1,0:T(8,128)(2,1)S(1)}, bf16[64,32,128]{2,1,0:T(8,128)(2,1)S(1)}, bf16[64,32,128]{2,1,0:T(8,128)(2,1)S(1)}, bf16[64,32,128]{2...) custom-call(f32[4608,128]{1,0:T(8,128)S(1)} %bitcast.27, ...), custom_call_target="tpu_custom_call" | custom-call | flops 4000000000 | bytes 4194304 | tf_op jit(solution)/shard_map/pallas_call | solution.py:280
  60.7 0.0 copy-start
  60.7 5.4 %shard_map.53 = (f32[64,1024]{1,0:T(8,128)S(1)}, f32[64,1024]{1,0:T(8,128)S(1)}) custom-call(bf16[64,32,128]{2,1,0:T(8,128)(2,1)S(1)} %get-tuple-element.41.hi_ref, bf16[64,32,128]{2,1,0:T(8,128)(2,1)S(1)} %get-tuple-element.42.lo_ref, f32[2,256,256]{2,1,0:T(8,128)S(1)} %bitcast.29, f32[128,256]{1,0:T(8,128)S(1)} %maximum_select_fusion.e_ref, ...), custom_call_target="tpu_custom_call" | custom-call | flops 5000000000 | bytes 4194304 | tf_op jit(solution)/shard_map/pallas_call | solution.py:304
  66.2 0.0 copy-done
  66.2 1.0 collective-permute-start.3
  67.2 0.0 copy-start.1
  67.2 5.4 %shard_map.52 = (f32[64,1024]{1,0:T(8,128)S(1)}, f32[64,1024]{1,0:T(8,128)S(1)}) custom-call(bf16[64,32,128]{2,1,0:T(8,128)(2,1)S(1)} %get-tuple-element.35.hi_ref, bf16[64,32,128]{2,1,0:T(8,128)(2,1)S(1)} %get-tuple-element.36.lo_ref, f32[2,256,256]{2,1,0:T(8,128)S(1)} %bitcast.30, f32[128,256]{1,0:T(8,128)S(1)} %maximum_select_fusion.e_ref, ...), custom_call_target="tpu_custom_call" | custom-call | flops 5000000000 | bytes 4194304 | tf_op jit(solution)/shard_map/pallas_call | solution.py:304
  72.6 1.4 %collective-permute-start.2 = (f32[64,1024]{1,0:T(8,128)S(1)}, f32[64,1024]{1,0:T(8,128)S(1)}, u32[]{:S(2)}, u32[]{:S(2)}) collective-permute-start(f32[64,1024]{1,0:T(8,128)S(1)} %get-tuple-element.40), channel_id=1, source_target_pairs={{0,64},{8,72},{16,80},{24,88},{32,96},{40,104},{48,112},{56,120},{... | collective-permute-start | bytes 786440 | tf_op jit(solution)/shard_map/ppermute | solution.py:379
  74.0 8.1 %all-to-all-done = f32[128,1,4096]{2,1,0:T(1,128)} async-done(((f32[128,1,4096]{2,1,0:T(1,128)}), f32[128,1,4096]{2,1,0:T(1,128)}, u32[]{:S(2)}, u32[]{:S(2)}) %all-to-all-start) | async-done | bytes 2097184 | tf_op jit(solution)/shard_map/all_to_all | solution.py:376
  82.1 0.0 copy-done.1
  82.1 0.0 copy-start.2
  82.1 5.0 %shard_map.49 = (bf16[64,32,128]{2,1,0:T(8,128)(2,1)S(1)}, bf16[64,32,128]{2,1,0:T(8,128)(2,1)S(1)}, bf16[64,32,128]{2,1,0:T(8,128)(2,1)S(1)}, bf16[64,32,128]{2,1,0:T(8,128)(2,1)S(1)}) custom-call(f32[4096,128]{1,0:T(8,128)} %bitcast.3.a_ref, f32[2,256,256]{2,1,0:T(8,128)S(1)} %bitcast.31, f32[32,32,128]{2,1,0:T(8,128)S(1)} %get-tuple-element.25.cos_ref, ...), custom_call_target="tpu_custom_call" | custom-call | flops 3000000000 | bytes 4194304 | tf_op jit(solution)/shard_map/pallas_call | solution.py:292
  87.1 0.0 copy-done.2
  87.1 5.4 %shard_map.51 = (f32[64,1024]{1,0:T(8,128)S(1)}, f32[64,1024]{1,0:T(8,128)S(1)}) custom-call(bf16[64,32,128]{2,1,0:T(8,128)(2,1)S(1)} %get-tuple-element.31.hi_ref, bf16[64,32,128]{2,1,0:T(8,128)(2,1)S(1)} %get-tuple-element.32.lo_ref, f32[2,256,256]{2,1,0:T(8,128)S(1)} %bitcast.32, f32[128,256]{1,0:T(8,128)S(1)} %maximum_select_fusion.e_ref, ...), custom_call_target="tpu_custom_call" | custom-call | flops 5000000000 | bytes 4194304 | tf_op jit(solution)/shard_map/pallas_call | solution.py:304
  92.5 0.4 collective-permute-start.1
  92.9 5.4 %shard_map.50 = (f32[64,1024]{1,0:T(8,128)S(1)}, f32[64,1024]{1,0:T(8,128)S(1)}) custom-call(bf16[64,32,128]{2,1,0:T(8,128)(2,1)S(1)} %get-tuple-element.27.hi_ref, bf16[64,32,128]{2,1,0:T(8,128)(2,1)S(1)} %get-tuple-element.28.lo_ref, f32[2,256,256]{2,1,0:T(8,128)S(1)} %bitcast.33, f32[128,256]{1,0:T(8,128)S(1)} %maximum_select_fusion.e_ref, ...), custom_call_target="tpu_custom_call" | custom-call | flops 5000000000 | bytes 4194304 | tf_op jit(solution)/shard_map/pallas_call | solution.py:304
  98.3 1.8 %collective-permute-start = (f32[64,1024]{1,0:T(8,128)S(1)}, f32[64,1024]{1,0:T(8,128)S(1)}, u32[]{:S(2)}, u32[]{:S(2)}) collective-permute-start(f32[64,1024]{1,0:T(8,128)S(1)} %get-tuple-element.30), channel_id=1, source_target_pairs={{0,64},{8,72},{16,80},{24,88},{32,96},{40,104},{48,112},{56,120},{... | collective-permute-start | bytes 786440 | tf_op jit(solution)/shard_map/ppermute | solution.py:379
  100.1 0.0 collective-permute-done.3.got_ref
  100.1 0.9 shard_map.54.rest_0_
  101.1 0.0 collective-permute-done.2.got_ref
  101.1 0.9 shard_map.55.rest_0_
  102.0 0.0 collective-permute-done.1.got_ref
  102.0 0.9 shard_map.56.rest_0_
  103.0 3.1 %collective-permute-done.got_ref = f32[64,1024]{1,0:T(8,128)S(1)} collective-permute-done((f32[64,1024]{1,0:T(8,128)S(1)}, f32[64,1024]{1,0:T(8,128)S(1)}, u32[]{:S(2)}, u32[]{:S(2)}) %collective-permute-start) | collective-permute-done | bytes 262176 | tf_op jit(solution)/shard_map/ppermute | solution.py:379
  106.1 0.9 shard_map.57
  (5 shorter events, 0.1 us)
Async XLA Ops:
  4.5 42.6 %all-to-all-start.1 = ((f32[128,1,4608]{2,1,0:T(1,128)}), f32[128,1,4608]{2,1,0:T(1,128)S(1)}, u32[]{:S(2)}, u32[]{:S(2)}) async-start(f32[128,1,4608]{2,1,0:T(1,128)} %bitcast.36), calls=%async_computation.1 | async-start | bytes 4718592 | tf_op jit(solution)/shard_map/all_to_all | solution.py:376
  47.0 35.0 %all-to-all-start = ((f32[128,1,4096]{2,1,0:T(1,128)}), f32[128,1,4096]{2,1,0:T(1,128)}, u32[]{:S(2)}, u32[]{:S(2)}) async-start(f32[128,1,4096]{2,1,0:T(1,128)} %bitcast.37), calls=%async_computation | async-start | bytes 4194304 | tf_op jit(solution)/shard_map/all_to_all | solution.py:376
  53.9 1.4 %copy-start.3 = (f32[2,64,64]{2,1,0:T(8,128)S(1)}, f32[2,64,64]{2,1,0:T(8,128)}, u32[]{:S(2)}) copy-start(f32[2,64,64]{2,1,0:T(8,128)} %param.7) | copy-start | bytes 98308
  60.7 5.5 %copy-start = (f32[32,32,128]{2,1,0:T(8,128)}, f32[32,32,128]{2,1,0:T(8,128)S(1)}, u32[]{:S(2)}) copy-start(f32[32,32,128]{2,1,0:T(8,128)S(1)} %get-tuple-element.26.sin_ref) | copy-start | bytes 1572868
  66.2 34.0 %collective-permute-start.3 = (f32[64,1024]{1,0:T(8,128)S(1)}, f32[64,1024]{1,0:T(8,128)S(1)}, u32[]{:S(2)}, u32[]{:S(2)}) collective-permute-start(f32[64,1024]{1,0:T(8,128)S(1)} %get-tuple-element.44), channel_id=1, source_target_pairs={{0,64},{8,72},{16,80},{24,88},{32,96},{40,104},{48,112},{56,120},{... | collective-permute-start | bytes 786440 | tf_op jit(solution)/shard_map/ppermute | solution.py:379
  67.2 14.9 %copy-start.1 = (f32[32,32,128]{2,1,0:T(8,128)S(1)}, f32[32,32,128]{2,1,0:T(8,128)}, u32[]{:S(2)}) copy-start(f32[32,32,128]{2,1,0:T(8,128)} %copy-done) | copy-start | bytes 1572868
  72.6 28.4 %collective-permute-start.2 = (f32[64,1024]{1,0:T(8,128)S(1)}, f32[64,1024]{1,0:T(8,128)S(1)}, u32[]{:S(2)}, u32[]{:S(2)}) collective-permute-start(f32[64,1024]{1,0:T(8,128)S(1)} %get-tuple-element.40), channel_id=1, source_target_pairs={{0,64},{8,72},{16,80},{24,88},{32,96},{40,104},{48,112},{56,120},{... | collective-permute-start | bytes 786440 | tf_op jit(solution)/shard_map/ppermute | solution.py:379
  82.1 5.0 %copy-start.2 = (f32[32,32,128]{2,1,0:T(8,128)S(1)}, f32[32,32,128]{2,1,0:T(8,128)}, u32[]{:S(2)}) copy-start(f32[32,32,128]{2,1,0:T(8,128)} %copy-done) | copy-start | bytes 1572868
  92.5 9.5 %collective-permute-start.1 = (f32[64,1024]{1,0:T(8,128)S(1)}, f32[64,1024]{1,0:T(8,128)S(1)}, u32[]{:S(2)}, u32[]{:S(2)}) collective-permute-start(f32[64,1024]{1,0:T(8,128)S(1)} %get-tuple-element.34), channel_id=1, source_target_pairs={{0,64},{8,72},{16,80},{24,88},{32,96},{40,104},{48,112},{56,120},{... | collective-permute-start | bytes 786440 | tf_op jit(solution)/shard_map/ppermute | solution.py:379
  98.3 7.7 %collective-permute-start = (f32[64,1024]{1,0:T(8,128)S(1)}, f32[64,1024]{1,0:T(8,128)S(1)}, u32[]{:S(2)}, u32[]{:S(2)}) collective-permute-start(f32[64,1024]{1,0:T(8,128)S(1)} %get-tuple-element.30), channel_id=1, source_target_pairs={{0,64},{8,72},{16,80},{24,88},{32,96},{40,104},{48,112},{56,120},{... | collective-permute-start | bytes 786440 | tf_op jit(solution)/shard_map/ppermute | solution.py:379

commit v4 on v3

--- a/solution.py
+++ b/solution.py
@@ -9,7 +9,6 @@
 from jax.sharding import PartitionSpec as P
 
 PACK_VMEM = 60 << 20
-PACK_BLOCK = 1024
 MAIN_VMEM = 24 << 20
 AXES = ("bx", "by")
 ROWS = 32
@@ -25,43 +24,75 @@
     return high, low
 
 
-def pack_kernel(w_ref, *refs):
-    *slopes, out_ref = refs
-    rows = ROWS + SLOPES * (len(slopes) > 0)
-    for pair in range(w_ref.shape[1] // 128):
-        turned = w_ref[:, pair * 128 : pair * 128 + 128].T
-        for b in range(2):
-            for w in range(2):
-                at = 64 * b + 32 * w
-                to = (2 * pair + b) * rows
-                out_ref[w, to : to + ROWS, :] = turned[at : at + 32]
-    if slopes:
-        p0 = slopes[0][:, 0, :]
-        p1 = slopes[1][:, 0, :]
-        for b in range(w_ref.shape[1] // 64):
-            for w in range(2):
-                at = slice(64 * b + 32 * w, 64 * b + 32 * w + 32)
-                parts = [p0[0:4, at], p1[0:4, at], p0[4:8, at], p1[4:8, at]]
-                out_ref[w, b * rows + ROWS : b * rows + rows, :] = jnp.concatenate(parts, axis=1)
+def pack_kernel(top, rows, w_ref, *refs):
+    p_ref = refs[0] if rows > ROWS else None
+    out_ref, held_ref, made_ref, p_held_ref, in_sems, out_sems = refs[-6:]
+    pieces, _, lanes = held_ref.shape
+    half = pieces * lanes
+    tall = lanes // 64 * rows
+
+    def incoming(n):
+        at = pl.ds(pl.multiple_of(top * half + n * lanes, 128), lanes)
+        return pltpu.make_async_copy(w_ref.at[:, at], held_ref.at[n], in_sems.at[n])
+
+    def outgoing(n, w):
+        at = pl.ds(pl.multiple_of(n * tall, 8), tall)
+        return pltpu.make_async_copy(made_ref.at[w, at], out_ref.at[w, at], out_sems.at[n, w])
+
+    more = []
+    if p_ref is not None:
+        more = [pltpu.make_async_copy(p_ref, p_held_ref, in_sems.at[pieces])]
+        more[0].start()
+    for n in range(pieces):
+        incoming(n).start()
+    for copy in more:
+        copy.wait()
+
+    @pl.loop(0, pieces)
+    def _(n):
+        incoming(n).wait()
+        first = pl.multiple_of(n * tall, 8)
+        for pair in range(lanes // 128):
+            turned = held_ref[n, :, pair * 128 : pair * 128 + 128].T
+            for b in range(2):
+                for w in range(2):
+                    at = 64 * b + 32 * w
+                    made_ref[w, pl.ds(first + (2 * pair + b) * rows, ROWS), :] = turned[at : at + 32]
+        if p_ref is not None:
+            p0 = p_held_ref[:, 0, pl.ds(pl.multiple_of(n * lanes, 128), lanes)]
+            p1 = p_held_ref[:, 0, pl.ds(pl.multiple_of(half + n * lanes, 128), lanes)]
+            for b in range(lanes // 64):
+                for w in range(2):
+                    at = slice(64 * b + 32 * w, 64 * b + 32 * w + 32)
+                    parts = [p0[0:4, at], p1[0:4, at], p0[4:8, at], p1[4:8, at]]
+                    to = first + (b * rows + ROWS)
+                    made_ref[w, pl.ds(to, SLOPES), :] = jnp.concatenate(parts, axis=1)
+        for w in range(2):
+            outgoing(n, w).start()
+
+    @pl.loop(0, pieces)
+    def _(n):
+        for w in range(2):
+            outgoing(n, w).wait()
 
 
 def pack(weights, slopes, top):
-    block = PACK_BLOCK
-    half = weights.shape[1] // 2 // block
-    first = top * half
-    rows, more, specs = ROWS, [], []
-    if slopes is not None:
-        rows, more = ROWS + SLOPES, [slopes, slopes]
-        specs = [
-            pl.BlockSpec((8, 1, block), lambda i: (0, 0, i)),
-            pl.BlockSpec((8, 1, block), lambda i: (0, 0, i + half)),
-        ]
+    pieces, lanes = 8, 512
+    rows = ROWS if slopes is None else ROWS + SLOPES
+    more = [] if slopes is None else [slopes]
+    anywhere = pl.BlockSpec(memory_space=pl.ANY)
     return pl.pallas_call(
-        pack_kernel,
+        functools.partial(pack_kernel, top, rows),
         out_shape=jax.ShapeDtypeStruct((2, 64 * rows, 128), F32),
-        grid=(half,),
-        in_specs=[pl.BlockSpec((128, block), lambda i: (0, first + i))] + specs,
-        out_specs=pl.BlockSpec((2, block // 64 * rows, 128), lambda i: (0, i, 0)),
+        in_specs=[anywhere] * (1 + len(more)),
+        out_specs=anywhere,
+        scratch_shapes=[
+            pltpu.VMEM((pieces, 128, lanes), F32),
+            pltpu.VMEM((2, 64 * rows, 128), F32),
+            pltpu.VMEM((8, 1, 8192), F32),
+            pltpu.SemaphoreType.DMA((pieces + 1,)),
+            pltpu.SemaphoreType.DMA((pieces, 2)),
+        ],
         compiler_params=pltpu.CompilerParams(vmem_limit_bytes=PACK_VMEM),
         cost_estimate=pl.CostEstimate(flops=0, bytes_accessed=5 << 20, transcendentals=0),
     )(weights, *more)
@@ -162,7 +193,7 @@
     return jnp.dot(jnp.concatenate(rows, axis=0), matrix, preferred_element_type=F32)
 
 
-def early_steps(a_ref, stride, k_ref, cos_ref, sin_ref, outs, hi_ref, lo_ref, k3_ref):
+def early_steps(a_ref, stride, k_ref, cos_ref, sin_ref, outs, hi_ref, lo_ref, k3_ref, ready=lambda i: None):
     fill_matrices(k_ref, k3_ref)
 
     def arrived(pair, odd):
@@ -174,6 +205,7 @@
 
     @pl.loop(0, 2)
     def _(i):
+        ready(i)
         for sub in range(0, 32, 2 * SUB):
             boxes = [i * 32 + sub + n for n in range(2 * SUB)]
             rows = []
@@ -194,7 +226,8 @@
             rows = [widen(*(load((hi_ref, lo_ref), 4 * q + 2 * c + h) for c in range(2))) for q in pairs for h in range(2)]
             merged = product(rows, k3_ref[1])
             for n in range(2 * SUB):
-                box = 2 * pairs[0] + n
+                low_bits = 2 * sub + n
+                box = i * 32 + low_bits
                 c, s = factors(1, box, 1, cos_ref, sin_ref)
                 re, im = rotate(merged[ROWS * n : ROWS * n + ROWS], c, s)
                 for top, tile in enumerate(by_top(re, im)):
@@ -208,7 +241,15 @@
 
 
 def second_kernel(a_ref, k_ref, cos_ref, sin_ref, *refs):
-    early_steps(a_ref, ROWS, k_ref, cos_ref, sin_ref, refs[:4], *refs[4:])
+    outs, scratch, (held_ref, sems) = refs[:4], refs[4:-2], refs[-2:]
+
+    def incoming(i):
+        rows = pl.ds(pl.multiple_of(i * 64 * ROWS, 8), 64 * ROWS)
+        return pltpu.make_async_copy(a_ref.at[rows], held_ref.at[rows], sems.at[i])
+
+    for i in range(2):
+        incoming(i).start()
+    early_steps(held_ref, ROWS, k_ref, cos_ref, sin_ref, outs, *scratch, ready=lambda i: incoming(i).wait())
 
 
 def late_kernel(
@@ -292,9 +333,10 @@
     return pl.pallas_call(
         second_kernel,
         out_shape=[HALF] * 4,
-        in_specs=[VMEM] * 4,
+        in_specs=[pl.BlockSpec(memory_space=pl.ANY)] + [VMEM] * 3,
         out_specs=[VMEM] * 4,
-        scratch_shapes=[pltpu.VMEM((128, ROWS, 128), BF16)] * 2 + [MATRICES],
+        scratch_shapes=[pltpu.VMEM((128, ROWS, 128), BF16)] * 2
+        + [MATRICES, pltpu.VMEM((128 * ROWS, 128), F32), pltpu.SemaphoreType.DMA((2,))],
         compiler_params=pltpu.CompilerParams(vmem_limit_bytes=MAIN_VMEM),
         cost_estimate=cost(3_000_000_000),
     )(arrived, k, cos, sin)

time: 108 us -> 106 us (0.981)
  Pallas kernels: 44.1 us -> 41.7 us
  waiting for transfers between devices: 38.5 us -> 39.6 us
    pallas_call x3, Pallas kernels: 13.5 us -> 11.1 us  [the longest x2 6.57 us: pack(): pl.pallas_call(functools.partial(pack_kernel, top, rows), out_shape=jax.S...]
    all_to_all x2, waiting for transfers between devices: 35.4 us -> 36.6 us  [spread(): lax.all_to_all(packed.reshape(128, 1, -1), AXES, split_axis=0, concat_axi...]
  transfers between devices with their start and end apart: 6 -> 6, of which waited for: 3 -> 3; matrix products, arithmetic and copies ran while one was open for 1% -> 2% of each run, Pallas kernels for 36% -> 35%
where the time goes in v4:
time: 106 us
  Pallas kernels  41.7 us (39%)
  waiting for transfers between devices  39.6 us (37%)
  starting transfers between devices  22.5 us (21%)
  local copies, waits for them, and re-layouts  1.35 us (1%)
    all_to_all x2, waiting for transfers between devices, spread(): lax.all_to_all(packed.reshape(128, 1, -1), AXES, split_axis=0, concat_axi...  36.6 us
    pallas_call x4, Pallas kernels, late_part(): pl.pallas_call(functools.partial(late_kernel, x1), out_shape=[FIELD, FIEL...  21.8 us
    all_to_all x2, starting transfers between devices, spread(): lax.all_to_all(packed.reshape(128, 1, -1), AXES, split_axis=0, concat_axi...  18 us
    pallas_call x2, Pallas kernels, pack(): pl.pallas_call(functools.partial(pack_kernel, top, rows), out_shape=jax.S...  6.57 us
    pallas_call x1, Pallas kernels, first_part(): pl.pallas_call(first_kernel, out_shape=[HALF] * 4 + [TABLE] * 4, in_specs...  5.16 us
    ppermute x4, starting transfers between devices, swap(): return lax.ppermute(field, 'bx', [(i, i ^ 8) for i in range(16)])  4.55 us
    pallas_call x1, Pallas kernels, second_part(): pl.pallas_call(second_kernel, out_shape=[HALF] * 4, in_specs=[pl.BlockSpe...  4.54 us
    pallas_call x4, Pallas kernels, join(): pl.pallas_call(functools.partial(join_kernel, place), out_shape=jax.Shape...  3.69 us
  transfers between devices with their start and end apart: 6, of which 3 were waited for; matrix products, arithmetic and copies ran while one was open for 2% of the time, Pallas kernels for 35%

profile of v4, /device:TPU:0, one launch (start us, length us, event | category | flops | bytes accessed | tf_op | source)
XLA Modules:
  0.0 105.9 jit_solution(2231957619489794308)
XLA Ops:
  0.0 3.6 %shard_map.47 = f32[2,2304,128]{2,1,0:T(8,128)} custom-call(f32[128,8192]{1,0:T(8,128)} %bitcast.34, f32[8,1,8192]{2,1,0:T(1,128)} %bitcast.40), custom_call_target="tpu_custom_call" | custom-call | bytes 5242880 | tf_op jit(solution)/shard_map/pallas_call | solution.py:84
  3.6 11.1 %all-to-all-start.1 = ((f32[128,1,4608]{2,1,0:T(1,128)}), f32[128,1,4608]{2,1,0:T(1,128)S(1)}, u32[]{:S(2)}, u32[]{:S(2)}) async-start(f32[128,1,4608]{2,1,0:T(1,128)} %bitcast.36), calls=%async_computation.1 | async-start | bytes 4718592 | tf_op jit(solution)/shard_map/all_to_all | solution.py:418
  14.8 3.0 %shard_map.46 = f32[2,2048,128]{2,1,0:T(8,128)} custom-call(f32[128,8192]{1,0:T(8,128)} %bitcast.35), custom_call_target="tpu_custom_call" | custom-call | bytes 5242880 | tf_op jit(solution)/shard_map/pallas_call | solution.py:84
  17.7 28.5 %all-to-all-done.1 = f32[128,1,4608]{2,1,0:T(1,128)S(1)} async-done(((f32[128,1,4608]{2,1,0:T(1,128)}), f32[128,1,4608]{2,1,0:T(1,128)S(1)}, u32[]{:S(2)}, u32[]{:S(2)}) %all-to-all-start.1) | async-done | bytes 2359328 | tf_op jit(solution)/shard_map/all_to_all | solution.py:418
  46.2 6.8 %all-to-all-start = ((f32[128,1,4096]{2,1,0:T(1,128)}), f32[128,1,4096]{2,1,0:T(1,128)}, u32[]{:S(2)}, u32[]{:S(2)}) async-start(f32[128,1,4096]{2,1,0:T(1,128)} %bitcast.37), calls=%async_computation | async-start | bytes 4194304 | tf_op jit(solution)/shard_map/all_to_all | solution.py:418
  53.1 0.0 copy-start.3
  53.1 1.1 %fusion = (f32[2,1,2,64,2,64]{5,4,3,2,1,0:T(2,128)S(1)}, f32[2,1,2,64,2,64]{5,4,3,2,1,0:T(2,128)S(1)}) fusion(f32[2,2,2,64,2,64]{5,4,3,2,1,0:T(2,128)} %param.6), kind=kLoop, calls=%fused_computation.6 | loop fusion | bytes 524288 | tf_op jit(solution)/shard_map/slice | solution.py:396
  54.2 0.1 copy.14
  54.3 0.1 copy.13
  54.4 0.0 copy-done.3
  54.5 0.2 maximum_select_fusion.e_ref
  54.7 5.2 %shard_map.48 = (bf16[64,32,128]{2,1,0:T(8,128)(2,1)S(1)}, bf16[64,32,128]{2,1,0:T(8,128)(2,1)S(1)}, bf16[64,32,128]{2,1,0:T(8,128)(2,1)S(1)}, bf16[64,32,128]{2...) custom-call(f32[4608,128]{1,0:T(8,128)S(1)} %bitcast.27, ...), custom_call_target="tpu_custom_call" | custom-call | flops 4000000000 | bytes 4194304 | tf_op jit(solution)/shard_map/pallas_call | solution.py:321
  59.9 0.0 copy-start
  59.9 5.4 %shard_map.53 = (f32[64,1024]{1,0:T(8,128)S(1)}, f32[64,1024]{1,0:T(8,128)S(1)}) custom-call(bf16[64,32,128]{2,1,0:T(8,128)(2,1)S(1)} %get-tuple-element.41.hi_ref, bf16[64,32,128]{2,1,0:T(8,128)(2,1)S(1)} %get-tuple-element.42.lo_ref, f32[2,256,256]{2,1,0:T(8,128)S(1)} %bitcast.29, f32[128,256]{1,0:T(8,128)S(1)} %maximum_select_fusion.e_ref, ...), custom_call_target="tpu_custom_call" | custom-call | flops 5000000000 | bytes 4194304 | tf_op jit(solution)/shard_map/pallas_call | solution.py:346
  65.4 0.0 copy-done
  65.4 1.0 collective-permute-start.3
  66.3 0.0 copy-start.1
  66.3 5.4 %shard_map.52 = (f32[64,1024]{1,0:T(8,128)S(1)}, f32[64,1024]{1,0:T(8,128)S(1)}) custom-call(bf16[64,32,128]{2,1,0:T(8,128)(2,1)S(1)} %get-tuple-element.35.hi_ref, bf16[64,32,128]{2,1,0:T(8,128)(2,1)S(1)} %get-tuple-element.36.lo_ref, f32[2,256,256]{2,1,0:T(8,128)S(1)} %bitcast.30, f32[128,256]{1,0:T(8,128)S(1)} %maximum_select_fusion.e_ref, ...), custom_call_target="tpu_custom_call" | custom-call | flops 5000000000 | bytes 4194304 | tf_op jit(solution)/shard_map/pallas_call | solution.py:346
  71.8 1.4 %collective-permute-start.2 = (f32[64,1024]{1,0:T(8,128)S(1)}, f32[64,1024]{1,0:T(8,128)S(1)}, u32[]{:S(2)}, u32[]{:S(2)}) collective-permute-start(f32[64,1024]{1,0:T(8,128)S(1)} %get-tuple-element.40), channel_id=1, source_target_pairs={{0,64},{8,72},{16,80},{24,88},{32,96},{40,104},{48,112},{56,120},{... | collective-permute-start | bytes 786440 | tf_op jit(solution)/shard_map/ppermute | solution.py:421
  73.2 8.1 %all-to-all-done = f32[128,1,4096]{2,1,0:T(1,128)} async-done(((f32[128,1,4096]{2,1,0:T(1,128)}), f32[128,1,4096]{2,1,0:T(1,128)}, u32[]{:S(2)}, u32[]{:S(2)}) %all-to-all-start) | async-done | bytes 2097184 | tf_op jit(solution)/shard_map/all_to_all | solution.py:418
  81.3 0.0 copy-done.1
  81.3 0.0 copy-start.2
  81.3 4.5 %shard_map.49 = (bf16[64,32,128]{2,1,0:T(8,128)(2,1)S(1)}, bf16[64,32,128]{2,1,0:T(8,128)(2,1)S(1)}, bf16[64,32,128]{2,1,0:T(8,128)(2,1)S(1)}, bf16[64,32,128]{2,1,0:T(8,128)(2,1)S(1)}) custom-call(f32[4096,128]{1,0:T(8,128)} %bitcast.3.a_ref, f32[2,256,256]{2,1,0:T(8,128)S(1)} %bitcast.31, f32[32,32,128]{2,1,0:T(8,128)S(1)} %get-tuple-element.25.cos_ref, ...), custom_call_target="tpu_custom_call" | custom-call | flops 3000000000 | bytes 4194304 | tf_op jit(solution)/shard_map/pallas_call | solution.py:333
  85.8 0.0 copy-done.2
  85.8 5.4 %shard_map.51 = (f32[64,1024]{1,0:T(8,128)S(1)}, f32[64,1024]{1,0:T(8,128)S(1)}) custom-call(bf16[64,32,128]{2,1,0:T(8,128)(2,1)S(1)} %get-tuple-element.31.hi_ref, bf16[64,32,128]{2,1,0:T(8,128)(2,1)S(1)} %get-tuple-element.32.lo_ref, f32[2,256,256]{2,1,0:T(8,128)S(1)} %bitcast.32, f32[128,256]{1,0:T(8,128)S(1)} %maximum_select_fusion.e_ref, ...), custom_call_target="tpu_custom_call" | custom-call | flops 5000000000 | bytes 4194304 | tf_op jit(solution)/shard_map/pallas_call | solution.py:346
  91.3 0.3 collective-permute-start.1
  91.6 5.4 %shard_map.50 = (f32[64,1024]{1,0:T(8,128)S(1)}, f32[64,1024]{1,0:T(8,128)S(1)}) custom-call(bf16[64,32,128]{2,1,0:T(8,128)(2,1)S(1)} %get-tuple-element.27.hi_ref, bf16[64,32,128]{2,1,0:T(8,128)(2,1)S(1)} %get-tuple-element.28.lo_ref, f32[2,256,256]{2,1,0:T(8,128)S(1)} %bitcast.33, f32[128,256]{1,0:T(8,128)S(1)} %maximum_select_fusion.e_ref, ...), custom_call_target="tpu_custom_call" | custom-call | flops 5000000000 | bytes 4194304 | tf_op jit(solution)/shard_map/pallas_call | solution.py:346
  97.1 1.9 %collective-permute-start = (f32[64,1024]{1,0:T(8,128)S(1)}, f32[64,1024]{1,0:T(8,128)S(1)}, u32[]{:S(2)}, u32[]{:S(2)}) collective-permute-start(f32[64,1024]{1,0:T(8,128)S(1)} %get-tuple-element.30), channel_id=1, source_target_pairs={{0,64},{8,72},{16,80},{24,88},{32,96},{40,104},{48,112},{56,120},{... | collective-permute-start | bytes 786440 | tf_op jit(solution)/shard_map/ppermute | solution.py:421
  98.9 0.0 collective-permute-done.3.got_ref
  98.9 0.9 shard_map.54.rest_0_
  99.9 0.0 collective-permute-done.2.got_ref
  99.9 0.9 shard_map.55.rest_0_
  100.8 0.0 collective-permute-done.1.got_ref
  100.8 0.9 shard_map.56.rest_0_
  101.7 3.1 %collective-permute-done.got_ref = f32[64,1024]{1,0:T(8,128)S(1)} collective-permute-done((f32[64,1024]{1,0:T(8,128)S(1)}, f32[64,1024]{1,0:T(8,128)S(1)}, u32[]{:S(2)}, u32[]{:S(2)}) %collective-permute-start) | collective-permute-done | bytes 262176 | tf_op jit(solution)/shard_map/ppermute | solution.py:421
  104.8 0.9 shard_map.57
  (5 shorter events, 0.1 us)
Async XLA Ops:
  3.6 42.6 %all-to-all-start.1 = ((f32[128,1,4608]{2,1,0:T(1,128)}), f32[128,1,4608]{2,1,0:T(1,128)S(1)}, u32[]{:S(2)}, u32[]{:S(2)}) async-start(f32[128,1,4608]{2,1,0:T(1,128)} %bitcast.36), calls=%async_computation.1 | async-start | bytes 4718592 | tf_op jit(solution)/shard_map/all_to_all | solution.py:418
  46.2 35.0 %all-to-all-start = ((f32[128,1,4096]{2,1,0:T(1,128)}), f32[128,1,4096]{2,1,0:T(1,128)}, u32[]{:S(2)}, u32[]{:S(2)}) async-start(f32[128,1,4096]{2,1,0:T(1,128)} %bitcast.37), calls=%async_computation | async-start | bytes 4194304 | tf_op jit(solution)/shard_map/all_to_all | solution.py:418
  53.1 1.4 %copy-start.3 = (f32[2,64,64]{2,1,0:T(8,128)S(1)}, f32[2,64,64]{2,1,0:T(8,128)}, u32[]{:S(2)}) copy-start(f32[2,64,64]{2,1,0:T(8,128)} %param.7) | copy-start | bytes 98308
  59.9 5.5 %copy-start = (f32[32,32,128]{2,1,0:T(8,128)}, f32[32,32,128]{2,1,0:T(8,128)S(1)}, u32[]{:S(2)}) copy-start(f32[32,32,128]{2,1,0:T(8,128)S(1)} %get-tuple-element.26.sin_ref) | copy-start | bytes 1572868
  65.4 33.6 %collective-permute-start.3 = (f32[64,1024]{1,0:T(8,128)S(1)}, f32[64,1024]{1,0:T(8,128)S(1)}, u32[]{:S(2)}, u32[]{:S(2)}) collective-permute-start(f32[64,1024]{1,0:T(8,128)S(1)} %get-tuple-element.44), channel_id=1, source_target_pairs={{0,64},{8,72},{16,80},{24,88},{32,96},{40,104},{48,112},{56,120},{... | collective-permute-start | bytes 786440 | tf_op jit(solution)/shard_map/ppermute | solution.py:421
  66.3 14.9 %copy-start.1 = (f32[32,32,128]{2,1,0:T(8,128)S(1)}, f32[32,32,128]{2,1,0:T(8,128)}, u32[]{:S(2)}) copy-start(f32[32,32,128]{2,1,0:T(8,128)} %copy-done) | copy-start | bytes 1572868
  71.8 28.1 %collective-permute-start.2 = (f32[64,1024]{1,0:T(8,128)S(1)}, f32[64,1024]{1,0:T(8,128)S(1)}, u32[]{:S(2)}, u32[]{:S(2)}) collective-permute-start(f32[64,1024]{1,0:T(8,128)S(1)} %get-tuple-element.40), channel_id=1, source_target_pairs={{0,64},{8,72},{16,80},{24,88},{32,96},{40,104},{48,112},{56,120},{... | collective-permute-start | bytes 786440 | tf_op jit(solution)/shard_map/ppermute | solution.py:421
  81.3 4.6 %copy-start.2 = (f32[32,32,128]{2,1,0:T(8,128)S(1)}, f32[32,32,128]{2,1,0:T(8,128)}, u32[]{:S(2)}) copy-start(f32[32,32,128]{2,1,0:T(8,128)} %copy-done) | copy-start | bytes 1572868
  91.3 9.5 %collective-permute-start.1 = (f32[64,1024]{1,0:T(8,128)S(1)}, f32[64,1024]{1,0:T(8,128)S(1)}, u32[]{:S(2)}, u32[]{:S(2)}) collective-permute-start(f32[64,1024]{1,0:T(8,128)S(1)} %get-tuple-element.34), channel_id=1, source_target_pairs={{0,64},{8,72},{16,80},{24,88},{32,96},{40,104},{48,112},{56,120},{... | collective-permute-start | bytes 786440 | tf_op jit(solution)/shard_map/ppermute | solution.py:421
  97.1 7.7 %collective-permute-start = (f32[64,1024]{1,0:T(8,128)S(1)}, f32[64,1024]{1,0:T(8,128)S(1)}, u32[]{:S(2)}, u32[]{:S(2)}) collective-permute-start(f32[64,1024]{1,0:T(8,128)S(1)} %get-tuple-element.30), channel_id=1, source_target_pairs={{0,64},{8,72},{16,80},{24,88},{32,96},{40,104},{48,112},{56,120},{... | collective-permute-start | bytes 786440 | tf_op jit(solution)/shard_map/ppermute | solution.py:421

commit v5 on v4

v5 whole, which is shorter than its diff:
```python
import functools

import jax
import jax.numpy as jnp
import numpy as np
from jax import lax
from jax.experimental import pallas as pl
from jax.experimental.pallas import tpu as pltpu
from jax.sharding import PartitionSpec as P

PACK_VMEM = 60 << 20
MAIN_VMEM = 24 << 20
AXES = ("bx", "by")
ROWS = 32
SLOPES = 4
NODES = [float(np.cos(np.pi * (2 * m + 1) / 16)) for m in range(4)]
F32 = jnp.float32
BF16 = jnp.bfloat16


def split_two(value):
    high = value.astype(BF16)
    low = (value - high.astype(F32)).astype(BF16)
    return high, low


def pack_kernel(top, rows, w_ref, *refs):
    p_ref = refs[0] if rows > ROWS else None
    out_ref, held_ref, made_ref, p_held_ref, in_sems, out_sems = refs[-6:]
    pieces, _, lanes = held_ref.shape
    half = pieces * lanes
    tall = lanes // 64 * rows

    def incoming(n):
        at = pl.ds(pl.multiple_of(top * half + n * lanes, 128), lanes)
        return pltpu.make_async_copy(w_ref.at[:, at], held_ref.at[n], in_sems.at[n])

    def outgoing(n, w):
        at = pl.ds(pl.multiple_of(n * tall, 8), tall)
        return pltpu.make_async_copy(made_ref.at[w, at], out_ref.at[w, at], out_sems.at[n, w])

    more = []
    if p_ref is not None:
        more = [pltpu.make_async_copy(p_ref, p_held_ref, in_sems.at[pieces])]
        more[0].start()
    for n in range(pieces):
        incoming(n).start()
    if p_ref is not None:
        more[0].wait()

        @pl.loop(0, pieces)
        def _(n):
            first = pl.multiple_of(n * tall, 8)
            p0 = p_held_ref[:, 0, pl.ds(pl.multiple_of(n * lanes, 128), lanes)]
            p1 = p_held_ref[:, 0, pl.ds(pl.multiple_of(half + n * lanes, 128), lanes)]
            for b in range(lanes // 64):
                for w in range(2):
                    at = slice(64 * b + 32 * w, 64 * b + 32 * w + 32)
                    parts = [p0[0:4, at], p1[0:4, at], p0[4:8, at], p1[4:8, at]]
                    to = first + (b * rows + ROWS)
                    made_ref[w, pl.ds(to, SLOPES), :] = jnp.concatenate(parts, axis=1)

    @pl.loop(0, pieces)
    def _(n):
        incoming(n).wait()
        first = pl.multiple_of(n * tall, 8)
        for pair in range(lanes // 128):
            turned = held_ref[n, :, pair * 128 : pair * 128 + 128].T
            for b in range(2):
                for w in range(2):
                    at = 64 * b + 32 * w
                    made_ref[w, pl.ds(first + (2 * pair + b) * rows, ROWS), :] = turned[at : at + 32]
        for w in range(2):
            outgoing(n, w).start()

    @pl.loop(0, pieces)
    def _(n):
        for w in range(2):
            outgoing(n, w).wait()


def pack(weights, slopes, top):
    pieces, lanes = 4, 1024
    rows = ROWS if slopes is None else ROWS + SLOPES
    more = [] if slopes is None else [slopes]
    anywhere = pl.BlockSpec(memory_space=pl.ANY)
    return pl.pallas_call(
        functools.partial(pack_kernel, top, rows),
        out_shape=jax.ShapeDtypeStruct((2, 64 * rows, 128), F32),
        in_specs=[anywhere] * (1 + len(more)),
        out_specs=anywhere,
        scratch_shapes=[
            pltpu.VMEM((pieces, 128, lanes), F32),
            pltpu.VMEM((2, 64 * rows, 128), F32),
            pltpu.VMEM((8, 1, 8192), F32),
            pltpu.SemaphoreType.DMA((pieces + 1,)),
            pltpu.SemaphoreType.DMA((pieces, 2)),
        ],
        compiler_params=pltpu.CompilerParams(vmem_limit_bytes=PACK_VMEM),
        cost_estimate=pl.CostEstimate(flops=0, bytes_accessed=5 << 20, transcendentals=0),
    )(weights, *more)


def sincos(angle):
    h = angle * 0.5
    q = h * h
    s = q * (-1 / 39916800) + 1 / 362880
    s = s * q - 1 / 5040
    s = s * q + 1 / 120
    s = s * q - 1 / 6
    s = (s * q + 1.0) * h
    c = q * (1 / 479001600) - 1 / 3628800
    c = c * q + 1 / 40320
    c = c * q - 1 / 720
    c = c * q + 1 / 24
    c = c * q - 0.5
    c = c * q + 1.0
    return 2.0 * s * c, 1.0 - 2.0 * s * s


def lane_gather(value, index):
    return jnp.take_along_axis(value, index, axis=1, mode="promise_in_bounds")


def build_tables(a_ref, tables):
    lane = lax.broadcasted_iota(jnp.int32, (ROWS, 128), 1)
    m = lane % 4
    node = jnp.where(m == 0, NODES[0], jnp.where(m == 1, NODES[1], jnp.where(m == 2, NODES[2], NODES[3])))
    second = lane // 4 % 2 == 1
    g = lane // 8

    @pl.loop(0, SLOPES)
    def _(row):
        turned = a_ref[pl.ds(ROWS + row, 128, stride=ROWS + SLOPES), :].T
        for late in range(2):
            t0 = turned[64 * late : 64 * late + 32]
            t1 = turned[64 * late + 32 : 64 * late + 64]
            for tile in range(4):
                for h, (cos_ref, sin_ref) in enumerate(tables):
                    index = ((2 * (2 * tile + g // 8) + h) * 8) + g % 8
                    slope = jnp.where(second, lane_gather(t1, index), lane_gather(t0, index))
                    s, c = sincos(slope * node)
                    at = (row + SLOPES * late) * 4 + tile
                    cos_ref[at] = c
                    sin_ref[at] = s


def factors(step, box, direction, flip, cos_ref, sin_ref):
    lane = lax.broadcasted_iota(jnp.int32, (ROWS, 128), 1)
    p = lane % 64
    m = p // 8 if direction == 0 else p % 8
    index = (lane // 64 + flip) % 2 * 4 + jnp.where(m < 4, m, 7 - m) + (box % 16) * 8
    tile = step * 4 + box // 16
    c = lane_gather(cos_ref[tile], index)
    s = lane_gather(sin_ref[tile], index)
    return c, jnp.where(m < 4, s, -s)


def rotate(merged, c, s):
    re = merged[:, :128]
    im = merged[:, 128:]
    return re * c - im * s, re * s + im * c


def insert_bit(q, bit, value):
    return ((q >> bit) << (bit + 1)) | (value << bit) | (q & ((1 << bit) - 1))


SUB = 8


def fill_matrices(k_ref, e_ref, k3_ref, k0_ref, e3_ref):
    def fill(to, value):
        high, low = split_two(value)
        to[0:256] = high
        to[256:512] = high
        to[512:768] = low

    for d in range(2):
        for flip in range(2):
            value = k_ref[d]
            if flip:
                value = jnp.concatenate([pltpu.roll(value[:, 128 * n : 128 * n + 128], 64, 1) for n in range(2)], axis=1)
            if d == 0:
                fill(k0_ref.at[flip], value)
            for h in range(2):
                parts = [value[128 * c + 64 * part : 128 * c + 64 * part + 64] for part in range(2) for c in (h, 1 - h)]
                fill(k3_ref.at[d, h, flip], jnp.concatenate(parts, axis=0))
    high, low = split_two(e_ref[...])
    e3_ref[:, 0:256] = high
    e3_ref[:, 256:512] = high
    e3_ref[:, 512:768] = low


def product(rows, matrix):
    return jnp.dot(jnp.concatenate(rows, axis=0), matrix, preferred_element_type=F32)


def children(state, first, second):
    lower = lax.broadcasted_iota(jnp.int32, (ROWS, 128), 1).astype(F32).astype(BF16) < 64
    high_re, high_im, low_re, low_im = (jnp.where(lower, ref[first], ref[second]) for ref in state)
    return jnp.concatenate([high_re, high_im, low_re, low_im, high_re, high_im], axis=1)


def store(state, box, re, im):
    state[0][box], state[2][box] = split_two(re)
    state[1][box], state[3][box] = split_two(im)


def finish(merged, n, step, box, direction, flip, tables):
    c, s = factors(step, box, direction, flip, *tables)
    return rotate(merged[ROWS * n : ROWS * n + ROWS], c, s)


def early_steps(a_ref, stride, tables, middle, target, k3_ref, k0_ref, ready=lambda i: None):
    def arrived(pair, odd):
        at = pl.multiple_of(pair * 2 * stride, 8)
        if stride % 8 == 0:
            return a_ref[pl.ds(at + odd * stride, ROWS), :]
        shift = odd * stride % 8
        return a_ref[pl.ds(at + (odd * stride - shift), ROWS + 2 * shift), :][shift : shift + ROWS]

    @pl.loop(0, 2)
    def _(i):
        ready(i)
        for sub in range(0, 32, 2 * SUB):
            for y0 in range(2):
                boxes = [i * 32 + (sub + 2 * n + y0) for n in range(SUB)]
                rows = []
                for n in range(SUB):
                    pair = i * 32 + (sub // 8 * 8 + n // 4 * 8 + n % 4)
                    parts = [split_two(arrived(pair + 4 * c, y0)) for c in range(2)]
                    highs = [p[0] for p in parts]
                    lows = [p[1] for p in parts]
                    rows.append(jnp.concatenate(highs + lows + highs, axis=1))
                merged = product(rows, k0_ref[y0])
                for n, box in enumerate(boxes):
                    store(middle, box, *finish(merged, n, 0, box, 0, y0, tables))

    @pl.loop(0, 2)
    def _(i):
        for h in range(2):
            for x1 in range(2):
                pairs = [i * 32 + (n // 4 * 16 + x1 * 8 + n % 4 * 2) for n in range(SUB)]
                merged = product([children(middle, q + h, q + 1 - h) for q in pairs], k3_ref[1, h, x1])
                for n in range(SUB):
                    store(target, pairs[n] + h, *finish(merged, n, 1, pairs[n] + h, 1, x1, tables))


def first_kernel(a_ref, k_ref, e_ref, *refs):
    target, tables, (k3_ref, e3_ref, k0_ref), middle = refs[:4], refs[4:8], refs[8:11], refs[11:]
    build_tables(a_ref, (tables[:2], tables[2:]))
    fill_matrices(k_ref, e_ref, k3_ref, k0_ref, e3_ref)
    early_steps(a_ref, ROWS + SLOPES, tables[:2], middle, target, k3_ref, k0_ref)


def second_kernel(a_ref, k_ref, e_ref, cos_ref, sin_ref, *refs):
    target, (k3_ref, e3_ref, k0_ref), middle, (held_ref, sems) = refs[:4], refs[4:7], refs[7:11], refs[11:]

    def incoming(i):
        rows = pl.ds(pl.multiple_of(i * 64 * ROWS, 8), 64 * ROWS)
        return pltpu.make_async_copy(a_ref.at[rows], held_ref.at[rows], sems.at[i])

    for i in range(2):
        incoming(i).start()
    fill_matrices(k_ref, e_ref, k3_ref, k0_ref, e3_ref)
    early_steps(held_ref, ROWS, (cos_ref, sin_ref), middle, target, k3_ref, k0_ref, lambda i: incoming(i).wait())


def late_kernel(x1, *refs):
    source, (k3_ref, e3_ref), tables, (own_ref, send_ref) = refs[:4], refs[4:6], refs[6:8], refs[8:10]
    states = (refs[10:14], refs[14:18])

    def done(merged, n, step, box, direction, flip):
        return finish(merged, n, step, insert_bit(box, 3, x1), direction, flip, tables)

    for y1 in range(2):
        for half in range(2):
            boxes = [half * 16 + (n // 2 * 4 + y1 * 2 + n % 2) for n in range(SUB)]
            rows = [children(source, insert_bit(box, 3, x1), insert_bit(box, 3, 1 - x1)) for box in boxes]
            merged = product(rows, k3_ref[0, x1, y1])
            for n, box in enumerate(boxes):
                store(states[0], box, *done(merged, n, 2, box, 0, y1))

    def middle(step, bit, after, direction, source, target):
        for h in range(2):
            for flip in range(2):
                if direction == 0:
                    pairs = [[insert_bit(insert_bit(n, after, flip), bit, c) for c in (h, 1 - h)] for n in range(SUB)]
                else:
                    pairs = [[insert_bit(insert_bit(n, bit, c), after, flip) for c in (h, 1 - h)] for n in range(SUB)]
                merged = product([children(source, *pair) for pair in pairs], k3_ref[direction, h, flip])
                for n, (box, _) in enumerate(pairs):
                    store(target, box, *done(merged, n, step, box, direction, flip))

    @pl.loop(0, 2)
    def _(level):
        middle(2 * level + 3, level + 1, level + 3, 1, states[0], states[1])
        middle(2 * level + 4, level + 3, jnp.where(level == 0, 2, 0), 0, states[1], states[0])

    for quarter in range(2):
        tiles = {}
        for h in range(2):
            boxes = [quarter * 16 + 2 * n for n in range(SUB)]
            merged = product([children(states[0], box + h, box + 1 - h) for box in boxes], k3_ref[1, h, 0])
            for n, box in enumerate(boxes):
                high, low = split_two(jnp.concatenate(done(merged, n, 7, box + h, 1, 0), axis=1))
                tiles[2 * n + h] = jnp.concatenate([high, low, high], axis=1)
        for part in range(2):
            rows = [tiles[8 * part + n // 4 * 4 + (0, 2, 1, 3)[n % 4]] for n in range(8)]
            field = lax.dot_general(
                e3_ref[...], jnp.concatenate(rows, axis=0), (((1,), (1,)), ((), ())), preferred_element_type=F32
            )
            at = 512 * quarter + 256 * part
            own_ref[:, at : at + 256] = field[0:64]
            send_ref[:, at : at + 256] = field[64:128]


VMEM = pl.BlockSpec(memory_space=pltpu.VMEM)
TABLE = jax.ShapeDtypeStruct((32, ROWS, 128), F32)
STATE = jax.ShapeDtypeStruct((64, ROWS, 128), BF16)
FIELD = jax.ShapeDtypeStruct((64, 1024), F32)
K3 = jax.ShapeDtypeStruct((2, 2, 2, 768, 256), BF16)
K0 = pltpu.VMEM((2, 768, 256), BF16)
E3 = jax.ShapeDtypeStruct((128, 768), BF16)


def cost(flops):
    return pl.CostEstimate(flops=flops, bytes_accessed=4 << 20, transcendentals=0)


def first_part(arrived, k, e):
    return pl.pallas_call(
        first_kernel,
        out_shape=[STATE] * 4 + [TABLE] * 4 + [K3, E3],
        in_specs=[VMEM] * 3,
        out_specs=[VMEM] * 10,
        scratch_shapes=[K0] + [pltpu.VMEM(STATE.shape, BF16)] * 4,
        compiler_params=pltpu.CompilerParams(vmem_limit_bytes=MAIN_VMEM),
        cost_estimate=cost(4_000_000_000),
    )(arrived, k, e)


def second_part(arrived, k, e, cos, sin):
    return pl.pallas_call(
        second_kernel,
        out_shape=[STATE] * 4 + [K3, E3],
        in_specs=[pl.BlockSpec(memory_space=pl.ANY)] + [VMEM] * 4,
        out_specs=[VMEM] * 6,
        scratch_shapes=[K0]
        + [pltpu.VMEM(STATE.shape, BF16)] * 4
        + [pltpu.VMEM((128 * ROWS, 128), F32), pltpu.SemaphoreType.DMA((2,))],
        compiler_params=pltpu.CompilerParams(vmem_limit_bytes=MAIN_VMEM),
        cost_estimate=cost(3_000_000_000),
    )(arrived, k, e, cos, sin)


def late_part(x1, state, k3, e3, cos, sin):
    return pl.pallas_call(
        functools.partial(late_kernel, x1),
        out_shape=[FIELD, FIELD],
        in_specs=[VMEM] * 8,
        out_specs=[VMEM] * 2,
        scratch_shapes=[pltpu.VMEM((32, ROWS, 128), BF16)] * 8,
        compiler_params=pltpu.CompilerParams(vmem_limit_bytes=MAIN_VMEM),
        cost_estimate=cost(5_000_000_000),
    )(*state, k3, e3, cos, sin)


def join_kernel(place, w_ref, own_ref, got_ref, *rest):
    out_ref, held_ref, sems = rest[-3:]
    first = w_ref[0] == 0
    lane = lax.broadcasted_iota(jnp.int32, (64, 128), 1)
    even = lane // 32 % 2 == 0
    copies = []
    for box in range(4):
        for y2 in range(2):
            lanes = slice(256 * box + 128 * y2, 256 * box + 128 * y2 + 128)
            own = own_ref[:, lanes]
            got = got_ref[:, lanes]
            a = jnp.where(first, own, got)
            b = jnp.where(first, got, own)
            held_ref[box, :, 256 * y2 : 256 * y2 + 128] = jnp.where(even, a, pltpu.roll(b, 32, 1))
            held_ref[box, :, 256 * y2 + 128 : 256 * y2 + 256] = jnp.where(even, pltpu.roll(a, 96, 1), b)
        at = (4 * box + place) * 512
        copies.append(pltpu.make_async_copy(held_ref.at[box], out_ref.at[:, at : at + 512], sems.at[box]))
        copies[-1].start()
    for copy in copies:
        copy.wait()


def join(w, own, got, place, out):
    more = [] if out is None else [out]
    anywhere = pl.BlockSpec(memory_space=pl.ANY)
    return pl.pallas_call(
        functools.partial(join_kernel, place),
        out_shape=jax.ShapeDtypeStruct((64, 8192), F32),
        in_specs=[pl.BlockSpec(memory_space=pltpu.SMEM), VMEM, VMEM] + [anywhere] * len(more),
        out_specs=anywhere,
        scratch_shapes=[pltpu.VMEM((4, 64, 512), F32), pltpu.SemaphoreType.DMA((4,))],
        input_output_aliases={3: 0} if more else {},
        compiler_params=pltpu.CompilerParams(vmem_limit_bytes=MAIN_VMEM),
        cost_estimate=pl.CostEstimate(flops=0, bytes_accessed=1 << 20, transcendentals=0),
    )(w, own, got, *more)


def merge_matrices(interp_matrix):
    re = jnp.transpose(interp_matrix[:, 0], (0, 3, 4, 1, 2)).reshape(2, 2, 64, 128)
    im = jnp.transpose(interp_matrix[:, 1], (0, 3, 4, 1, 2)).reshape(2, 2, 64, 128)
    from_re = jnp.concatenate([re, im], axis=3)
    from_im = jnp.concatenate([-im, re], axis=3)
    return jnp.stack([from_re, from_im], axis=2).reshape(2, 256, 256)


def evaluation_matrix(evaluation, w):
    zero = jnp.zeros((64, 64), F32)
    re, im = evaluation[0], -evaluation[1]
    low = jnp.concatenate([re, zero, im, zero], axis=1)
    high = jnp.concatenate([zero, re, zero, im], axis=1)
    return jnp.where(w == 0, jnp.concatenate([low, high], axis=0), jnp.concatenate([high, low], axis=0))


def shards(weights, phase_slope, interp_matrix, evaluation):
    w = lax.axis_index("bx") >> 3
    w_one = w.astype(jnp.int32).reshape(1)
    planes = weights.reshape(128, 8192)
    k = merge_matrices(interp_matrix)
    e = evaluation_matrix(evaluation, w)

    def spread(packed):
        return lax.all_to_all(packed.reshape(128, 1, -1), AXES, split_axis=0, concat_axis=0, tiled=True).reshape(-1, 128)

    def swap(field):
        return lax.ppermute(field, "bx", [(i, i ^ 8) for i in range(16)])

    arrived0 = spread(pack(planes, phase_slope.reshape(8, 1, 8192), 0))
    arrived1 = spread(pack(planes, None, 1))
    *first, cos0, sin0, cos1, sin1, k3, e3 = first_part(arrived0, k, e)
    fields = [late_part(x1, first, k3, e3, cos0, sin0) for x1 in range(2)]
    *second, k3, e3 = second_part(arrived1, k, e, cos1, sin1)
    fields += [late_part(x1, second, k3, e3, cos1, sin1) for x1 in range(2)]
    out = None
    for n, (own, send) in enumerate(fields):
        out = join(w_one, own, swap(send), n % 2 * 2 + n // 2, out)
    return out[None, None]


def solution(mesh):
    in_specs = (P("bx", "by", None, None, None), P(None, "bx", "by", None), P(), P())
    out_specs = P("bx", "by", None, None)
    return jax.shard_map(shards, mesh=mesh, in_specs=in_specs, out_specs=out_specs, check_vma=False)
```

time: 106 us -> 105 us (level)
  Pallas kernels: 41.7 us -> 39 us
  waiting for transfers between devices: 39.6 us -> 40.8 us
    pallas_call x4, Pallas kernels: 21.8 us -> 19.8 us  [late_part(): pl.pallas_call(functools.partial(late_kernel, x1), out_shape=[FIELD, FIEL...]
    slice x1, local copies, waits for them, and re-layouts: 1.1 us -> 0.04 us  [merge_matrices(): interp_matrix[:, 1]]
  transfers between devices with their start and end apart: 6 -> 6, of which waited for: 3 -> 3; matrix products, arithmetic and copies ran while one was open for 2% -> 1% of each run, Pallas kernels for 35% -> 33%
where the time goes in v5:
time: 105 us
  waiting for transfers between devices  40.8 us (39%)
  Pallas kernels  39 us (37%)
  starting transfers between devices  22.5 us (21%)
  other arithmetic  1.06 us (1%)
  local copies, waits for them, and re-layouts  1.05 us (1%)
    all_to_all x2, waiting for transfers between devices, spread(): lax.all_to_all(packed.reshape(128, 1, -1), AXES, split_axis=0, concat_axi...  37.2 us
    pallas_call x4, Pallas kernels, late_part(): pl.pallas_call(functools.partial(late_kernel, x1), out_shape=[FIELD, FIEL...  19.8 us
    all_to_all x2, starting transfers between devices, spread(): lax.all_to_all(packed.reshape(128, 1, -1), AXES, split_axis=0, concat_axi...  18 us
    pallas_call x2, Pallas kernels, pack(): pl.pallas_call(functools.partial(pack_kernel, top, rows), out_shape=jax.S...  6.18 us
    pallas_call x1, Pallas kernels, first_part(): pl.pallas_call(first_kernel, out_shape=[STATE] * 4 + [TABLE] * 4 + [K3, E...  5.24 us
    ppermute x4, starting transfers between devices, swap(): return lax.ppermute(field, 'bx', [(i, i ^ 8) for i in range(16)])  4.56 us
    pallas_call x1, Pallas kernels, second_part(): pl.pallas_call(second_kernel, out_shape=[STATE] * 4 + [K3, E3], in_specs=...  4.09 us
    pallas_call x4, Pallas kernels, join(): pl.pallas_call(functools.partial(join_kernel, place), out_shape=jax.Shape...  3.69 us
  transfers between devices with their start and end apart: 6, of which 3 were waited for; matrix products, arithmetic and copies ran while one was open for 1% of the time, Pallas kernels for 33%

profile of v5, /device:TPU:0, one launch (start us, length us, event | category | flops | bytes accessed | tf_op | source)
XLA Modules:
  0.0 104.8 jit_solution(4650596563473713137)
XLA Ops:
  0.0 3.4 %shard_map.47 = f32[2,2304,128]{2,1,0:T(8,128)} custom-call(f32[128,8192]{1,0:T(8,128)} %bitcast.30, f32[8,1,8192]{2,1,0:T(1,128)} %bitcast.36), custom_call_target="tpu_custom_call" | custom-call | bytes 5242880 | tf_op jit(solution)/shard_map/pallas_call | solution.py:87
  3.4 11.1 %all-to-all-start.1 = ((f32[128,1,4608]{2,1,0:T(1,128)}), f32[128,1,4608]{2,1,0:T(1,128)S(1)}, u32[]{:S(2)}, u32[]{:S(2)}) async-start(f32[128,1,4608]{2,1,0:T(1,128)} %bitcast.32), calls=%async_computation.1 | async-start | bytes 4718592 | tf_op jit(solution)/shard_map/all_to_all | solution.py:431
  14.6 2.8 %shard_map.46 = f32[2,2048,128]{2,1,0:T(8,128)} custom-call(f32[128,8192]{1,0:T(8,128)} %bitcast.31), custom_call_target="tpu_custom_call" | custom-call | bytes 5242880 | tf_op jit(solution)/shard_map/pallas_call | solution.py:87
  17.4 28.7 %all-to-all-done.1 = f32[128,1,4608]{2,1,0:T(1,128)S(1)} async-done(((f32[128,1,4608]{2,1,0:T(1,128)}), f32[128,1,4608]{2,1,0:T(1,128)S(1)}, u32[]{:S(2)}, u32[]{:S(2)}) %all-to-all-start.1) | async-done | bytes 2359328 | tf_op jit(solution)/shard_map/all_to_all | solution.py:431
  46.0 0.0 copy-start.2
  46.0 6.8 %all-to-all-start = ((f32[128,1,4096]{2,1,0:T(1,128)}), f32[128,1,4096]{2,1,0:T(1,128)}, u32[]{:S(2)}, u32[]{:S(2)}) async-start(f32[128,1,4096]{2,1,0:T(1,128)} %bitcast.33), calls=%async_computation | async-start | bytes 4194304 | tf_op jit(solution)/shard_map/all_to_all | solution.py:431
  52.9 0.0 copy-done.2
  52.9 0.1 copy.14
  53.1 0.1 copy.13
  53.2 0.8 slice_bitcast_fusion
  54.0 0.2 maximum_select_fusion.e_ref
  54.2 5.2 %shard_map.48 = (bf16[64,32,128]{2,1,0:T(8,128)(2,1)S(1)}, bf16[64,32,128]{2,1,0:T(8,128)(2,1)S(1)}, bf16[64,32,128]{2,1,0:T(8,128)(2,1)S(1)}, bf16[64,32,128]{2...) custom-call(f32[4608,128]{1,0:T(8,128)S(1)} %bitcast.27, ...), custom_call_target="tpu_custom_call" | custom-call | flops 4000000000 | bytes 4194304 | tf_op jit(solution)/shard_map/pallas_call | solution.py:333
  59.5 0.0 copy-start
  59.5 0.8 copy-done
  60.3 4.9 %shard_map.53 = (f32[64,1024]{1,0:T(8,128)S(1)}, f32[64,1024]{1,0:T(8,128)S(1)}) custom-call(bf16[64,32,128]{2,1,0:T(8,128)(2,1)S(1)} %get-tuple-element.41.refs_0_, bf16[64,32,128]{2,1,0:T(8,128)(2,1)S(1)} %get-tuple-element.42.refs_1_, bf16[64,32,128]{2,1,0:T(8,128)(2,1)S(1)} %get-tuple-element.43.refs_2_, ...), custom_call_target="tpu_custom_call" | custom-call | flops 5000000000 | bytes 4194304 | tf_op jit(solution)/shard_map/pallas_call | solution.py:359
  65.2 0.0 copy-start.1
  65.2 1.0 collective-permute-start.3
  66.2 4.9 %shard_map.52 = (f32[64,1024]{1,0:T(8,128)S(1)}, f32[64,1024]{1,0:T(8,128)S(1)}) custom-call(bf16[64,32,128]{2,1,0:T(8,128)(2,1)S(1)} %get-tuple-element.41.refs_0_, bf16[64,32,128]{2,1,0:T(8,128)(2,1)S(1)} %get-tuple-element.42.refs_1_, bf16[64,32,128]{2,1,0:T(8,128)(2,1)S(1)} %get-tuple-element.43.refs_2_, ...), custom_call_target="tpu_custom_call" | custom-call | flops 5000000000 | bytes 4194304 | tf_op jit(solution)/shard_map/pallas_call | solution.py:359
  71.2 1.4 %collective-permute-start.2 = (f32[64,1024]{1,0:T(8,128)S(1)}, f32[64,1024]{1,0:T(8,128)S(1)}, u32[]{:S(2)}, u32[]{:S(2)}) collective-permute-start(f32[64,1024]{1,0:T(8,128)S(1)} %get-tuple-element.50), channel_id=1, source_target_pairs={{0,64},{8,72},{16,80},{24,88},{32,96},{40,104},{48,112},{56,120},{... | collective-permute-start | bytes 786440 | tf_op jit(solution)/shard_map/ppermute | solution.py:434
  72.6 8.5 %all-to-all-done = f32[128,1,4096]{2,1,0:T(1,128)} async-done(((f32[128,1,4096]{2,1,0:T(1,128)}), f32[128,1,4096]{2,1,0:T(1,128)}, u32[]{:S(2)}, u32[]{:S(2)}) %all-to-all-start) | async-done | bytes 2097184 | tf_op jit(solution)/shard_map/all_to_all | solution.py:431
  81.1 0.0 copy-done.1
  81.1 4.1 %shard_map.49 = (bf16[64,32,128]{2,1,0:T(8,128)(2,1)S(1)}, bf16[64,32,128]{2,1,0:T(8,128)(2,1)S(1)}, bf16[64,32,128]{2,1,0:T(8,128)(2,1)S(1)}, bf16[64,32,128]{2...) custom-call(f32[4096,128]{1,0:T(8,128)} %bitcast.3.a_ref, ...), custom_call_target="tpu_custom_call" | custom-call | flops 3000000000 | bytes 4194304 | tf_op jit(solution)/shard_map/pallas_call | solution.py:345
  85.2 5.0 %shard_map.51 = (f32[64,1024]{1,0:T(8,128)S(1)}, f32[64,1024]{1,0:T(8,128)S(1)}) custom-call(bf16[64,32,128]{2,1,0:T(8,128)(2,1)S(1)} %get-tuple-element.31.refs_0_, bf16[64,32,128]{2,1,0:T(8,128)(2,1)S(1)} %get-tuple-element.32.refs_1_, bf16[64,32,128]{2,1,0:T(8,128)(2,1)S(1)} %get-tuple-element.33.refs_2_, ...), custom_call_target="tpu_custom_call" | custom-call | flops 5000000000 | bytes 4194304 | tf_op jit(solution)/shard_map/pallas_call | solution.py:359
  90.2 0.3 collective-permute-start.1
  90.5 4.9 %shard_map.50 = (f32[64,1024]{1,0:T(8,128)S(1)}, f32[64,1024]{1,0:T(8,128)S(1)}) custom-call(bf16[64,32,128]{2,1,0:T(8,128)(2,1)S(1)} %get-tuple-element.31.refs_0_, bf16[64,32,128]{2,1,0:T(8,128)(2,1)S(1)} %get-tuple-element.32.refs_1_, bf16[64,32,128]{2,1,0:T(8,128)(2,1)S(1)} %get-tuple-element.33.refs_2_, ...), custom_call_target="tpu_custom_call" | custom-call | flops 5000000000 | bytes 4194304 | tf_op jit(solution)/shard_map/pallas_call | solution.py:359
  95.5 1.9 %collective-permute-start = (f32[64,1024]{1,0:T(8,128)S(1)}, f32[64,1024]{1,0:T(8,128)S(1)}, u32[]{:S(2)}, u32[]{:S(2)}) collective-permute-start(f32[64,1024]{1,0:T(8,128)S(1)} %get-tuple-element.38), channel_id=1, source_target_pairs={{0,64},{8,72},{16,80},{24,88},{32,96},{40,104},{48,112},{56,120},{... | collective-permute-start | bytes 786440 | tf_op jit(solution)/shard_map/ppermute | solution.py:434
  97.3 0.0 collective-permute-done.3.got_ref
  97.3 0.9 shard_map.54.rest_0_
  98.3 0.0 collective-permute-done.2.got_ref
  98.3 0.9 shard_map.55.rest_0_
  99.2 0.0 collective-permute-done.1.got_ref
  99.2 0.9 shard_map.56.rest_0_
  100.1 3.6 %collective-permute-done.got_ref = f32[64,1024]{1,0:T(8,128)S(1)} collective-permute-done((f32[64,1024]{1,0:T(8,128)S(1)}, f32[64,1024]{1,0:T(8,128)S(1)}, u32[]{:S(2)}, u32[]{:S(2)}) %collective-permute-start) | collective-permute-done | bytes 262176 | tf_op jit(solution)/shard_map/ppermute | solution.py:434
  103.7 0.9 shard_map.57
  (5 shorter events, 0.1 us)
Async XLA Ops:
  3.4 42.6 %all-to-all-start.1 = ((f32[128,1,4608]{2,1,0:T(1,128)}), f32[128,1,4608]{2,1,0:T(1,128)S(1)}, u32[]{:S(2)}, u32[]{:S(2)}) async-start(f32[128,1,4608]{2,1,0:T(1,128)} %bitcast.32), calls=%async_computation.1 | async-start | bytes 4718592 | tf_op jit(solution)/shard_map/all_to_all | solution.py:431
  46.0 6.8 %copy-start.2 = (f32[2,2,2,64,2,64]{5,4,3,2,1,0:T(2,128)S(1)}, f32[2,2,2,64,2,64]{5,4,3,2,1,0:T(2,128)}, u32[]{:S(2)}) copy-start(f32[2,2,2,64,2,64]{5,4,3,2,1,0:T(2,128)} %param.6) | copy-start | bytes 786436
  46.0 35.0 %all-to-all-start = ((f32[128,1,4096]{2,1,0:T(1,128)}), f32[128,1,4096]{2,1,0:T(1,128)}, u32[]{:S(2)}, u32[]{:S(2)}) async-start(f32[128,1,4096]{2,1,0:T(1,128)} %bitcast.33), calls=%async_computation | async-start | bytes 4194304 | tf_op jit(solution)/shard_map/all_to_all | solution.py:431
  59.5 0.8 copy-start
  65.2 15.8 %copy-start.1 = (f32[32,32,128]{2,1,0:T(8,128)S(1)}, f32[32,32,128]{2,1,0:T(8,128)}, u32[]{:S(2)}) copy-start(f32[32,32,128]{2,1,0:T(8,128)} %copy-done) | copy-start | bytes 1572868
  65.2 32.1 %collective-permute-start.3 = (f32[64,1024]{1,0:T(8,128)S(1)}, f32[64,1024]{1,0:T(8,128)S(1)}, u32[]{:S(2)}, u32[]{:S(2)}) collective-permute-start(f32[64,1024]{1,0:T(8,128)S(1)} %get-tuple-element.52), channel_id=1, source_target_pairs={{0,64},{8,72},{16,80},{24,88},{32,96},{40,104},{48,112},{56,120},{... | collective-permute-start | bytes 786440 | tf_op jit(solution)/shard_map/ppermute | solution.py:434
  71.2 27.1 %collective-permute-start.2 = (f32[64,1024]{1,0:T(8,128)S(1)}, f32[64,1024]{1,0:T(8,128)S(1)}, u32[]{:S(2)}, u32[]{:S(2)}) collective-permute-start(f32[64,1024]{1,0:T(8,128)S(1)} %get-tuple-element.50), channel_id=1, source_target_pairs={{0,64},{8,72},{16,80},{24,88},{32,96},{40,104},{48,112},{56,120},{... | collective-permute-start | bytes 786440 | tf_op jit(solution)/shard_map/ppermute | solution.py:434
  90.2 9.0 %collective-permute-start.1 = (f32[64,1024]{1,0:T(8,128)S(1)}, f32[64,1024]{1,0:T(8,128)S(1)}, u32[]{:S(2)}, u32[]{:S(2)}) collective-permute-start(f32[64,1024]{1,0:T(8,128)S(1)} %get-tuple-element.40), channel_id=1, source_target_pairs={{0,64},{8,72},{16,80},{24,88},{32,96},{40,104},{48,112},{56,120},{... | collective-permute-start | bytes 786440 | tf_op jit(solution)/shard_map/ppermute | solution.py:434
  95.5 8.3 %collective-permute-start = (f32[64,1024]{1,0:T(8,128)S(1)}, f32[64,1024]{1,0:T(8,128)S(1)}, u32[]{:S(2)}, u32[]{:S(2)}) collective-permute-start(f32[64,1024]{1,0:T(8,128)S(1)} %get-tuple-element.38), channel_id=1, source_target_pairs={{0,64},{8,72},{16,80},{24,88},{32,96},{40,104},{48,112},{56,120},{... | collective-permute-start | bytes 786440 | tf_op jit(solution)/shard_map/ppermute | solution.py:434

commit v6 on v5

--- a/solution.py
+++ b/solution.py
@@ -214,14 +214,10 @@
 
 def early_steps(a_ref, stride, tables, middle, target, k3_ref, k0_ref, ready=lambda i: None):
     def arrived(pair, odd):
-        at = pl.multiple_of(pair * 2 * stride, 8)
-        if stride % 8 == 0:
-            return a_ref[pl.ds(at + odd * stride, ROWS), :]
-        shift = odd * stride % 8
-        return a_ref[pl.ds(at + (odd * stride - shift), ROWS + 2 * shift), :][shift : shift + ROWS]
-
-    @pl.loop(0, 2)
-    def _(i):
+        at = (2 * pair + odd) * stride
+        return a_ref[at : at + ROWS, :]
+
+    for i in range(2):
         ready(i)
         for sub in range(0, 32, 2 * SUB):
             for y0 in range(2):
@@ -237,8 +233,7 @@
                 for n, box in enumerate(boxes):
                     store(middle, box, *finish(merged, n, 0, box, 0, y0, tables))
 
-    @pl.loop(0, 2)
-    def _(i):
+    for i in range(2):
         for h in range(2):
             for x1 in range(2):
                 pairs = [i * 32 + (n // 4 * 16 + x1 * 8 + n % 4 * 2) for n in range(SUB)]
@@ -293,10 +288,10 @@
                 for n, (box, _) in enumerate(pairs):
                     store(target, box, *done(merged, n, step, box, direction, flip))
 
-    @pl.loop(0, 2)
-    def _(level):
-        middle(2 * level + 3, level + 1, level + 3, 1, states[0], states[1])
-        middle(2 * level + 4, level + 3, jnp.where(level == 0, 2, 0), 0, states[1], states[0])
+    middle(3, 1, 3, 1, states[0], states[1])
+    middle(4, 3, 2, 0, states[1], states[0])
+    middle(5, 2, 4, 1, states[0], states[1])
+    middle(6, 4, 0, 0, states[1], states[0])
 
     for quarter in range(2):
         tiles = {}

time: 105 us -> 104 us (level)
  Pallas kernels: 39 us -> 33.9 us
  waiting for transfers between devices: 40.8 us -> 44.7 us
    pallas_call x4, Pallas kernels: 19.8 us -> 16.2 us  [late_part(): pl.pallas_call(functools.partial(late_kernel, x1), out_shape=[FIELD, FIEL...]
    all_to_all x2, waiting for transfers between devices: 37.2 us -> 40.2 us  [spread(): lax.all_to_all(packed.reshape(128, 1, -1), AXES, split_axis=0, concat_axi...]
    pallas_call x1, Pallas kernels: 5.24 us -> 4.03 us  [first_part(): pl.pallas_call(first_kernel, out_shape=[STATE] * 4 + [TABLE] * 4 + [K3, E...]
  transfers between devices with their start and end apart: 6 -> 6, of which waited for: 3 -> 4; matrix products, arithmetic and copies ran while one was open for 1% -> 1% of each run, Pallas kernels for 33% -> 29%
where the time goes in v6:
time: 104 us
  waiting for transfers between devices  44.7 us (43%)
  Pallas kernels  33.9 us (33%)
  starting transfers between devices  22.7 us (22%)
  other arithmetic  1.06 us (1%)
  local copies, waits for them, and re-layouts  1.05 us (1%)
    all_to_all x2, waiting for transfers between devices, spread(): lax.all_to_all(packed.reshape(128, 1, -1), AXES, split_axis=0, concat_axi...  40.2 us
    all_to_all x2, starting transfers between devices, spread(): lax.all_to_all(packed.reshape(128, 1, -1), AXES, split_axis=0, concat_axi...  18 us
    pallas_call x4, Pallas kernels, late_part(): pl.pallas_call(functools.partial(late_kernel, x1), out_shape=[FIELD, FIEL...  16.2 us
    pallas_call x2, Pallas kernels, pack(): pl.pallas_call(functools.partial(pack_kernel, top, rows), out_shape=jax.S...  6.18 us
    ppermute x4, starting transfers between devices, swap(): return lax.ppermute(field, 'bx', [(i, i ^ 8) for i in range(16)])  4.77 us
    ppermute x4, waiting for transfers between devices, swap(): return lax.ppermute(field, 'bx', [(i, i ^ 8) for i in range(16)])  4.49 us
    pallas_call x1, Pallas kernels, first_part(): pl.pallas_call(first_kernel, out_shape=[STATE] * 4 + [TABLE] * 4 + [K3, E...  4.03 us
    pallas_call x1, Pallas kernels, second_part(): pl.pallas_call(second_kernel, out_shape=[STATE] * 4 + [K3, E3], in_specs=...  3.83 us
  transfers between devices with their start and end apart: 6, of which 4 were waited for; matrix products, arithmetic and copies ran while one was open for 1% of the time, Pallas kernels for 29%

profile of v6, /device:TPU:0, one launch (start us, length us, event | category | flops | bytes accessed | tf_op | source)
XLA Modules:
  0.0 103.8 jit_solution(6163511370095019889)
XLA Ops:
  0.0 3.4 %shard_map.47 = f32[2,2304,128]{2,1,0:T(8,128)} custom-call(f32[128,8192]{1,0:T(8,128)} %bitcast.30, f32[8,1,8192]{2,1,0:T(1,128)} %bitcast.36), custom_call_target="tpu_custom_call" | custom-call | bytes 5242880 | tf_op jit(solution)/shard_map/pallas_call | solution.py:87
  3.4 11.1 %all-to-all-start.1 = ((f32[128,1,4608]{2,1,0:T(1,128)}), f32[128,1,4608]{2,1,0:T(1,128)S(1)}, u32[]{:S(2)}, u32[]{:S(2)}) async-start(f32[128,1,4608]{2,1,0:T(1,128)} %bitcast.32), calls=%async_computation.1 | async-start | bytes 4718592 | tf_op jit(solution)/shard_map/all_to_all | solution.py:426
  14.6 2.8 %shard_map.46 = f32[2,2048,128]{2,1,0:T(8,128)} custom-call(f32[128,8192]{1,0:T(8,128)} %bitcast.31), custom_call_target="tpu_custom_call" | custom-call | bytes 5242880 | tf_op jit(solution)/shard_map/pallas_call | solution.py:87
  17.4 28.7 %all-to-all-done.1 = f32[128,1,4608]{2,1,0:T(1,128)S(1)} async-done(((f32[128,1,4608]{2,1,0:T(1,128)}), f32[128,1,4608]{2,1,0:T(1,128)S(1)}, u32[]{:S(2)}, u32[]{:S(2)}) %all-to-all-start.1) | async-done | bytes 2359328 | tf_op jit(solution)/shard_map/all_to_all | solution.py:426
  46.0 0.0 copy-start.2
  46.0 6.8 %all-to-all-start = ((f32[128,1,4096]{2,1,0:T(1,128)}), f32[128,1,4096]{2,1,0:T(1,128)}, u32[]{:S(2)}, u32[]{:S(2)}) async-start(f32[128,1,4096]{2,1,0:T(1,128)} %bitcast.33), calls=%async_computation | async-start | bytes 4194304 | tf_op jit(solution)/shard_map/all_to_all | solution.py:426
  52.9 0.0 copy-done.2
  52.9 0.1 copy.14
  53.1 0.1 copy.13
  53.2 0.8 slice_bitcast_fusion
  54.0 0.2 maximum_select_fusion.e_ref
  54.2 4.0 %shard_map.48 = (bf16[64,32,128]{2,1,0:T(8,128)(2,1)S(1)}, bf16[64,32,128]{2,1,0:T(8,128)(2,1)S(1)}, bf16[64,32,128]{2,1,0:T(8,128)(2,1)S(1)}, bf16[64,32,128]{2...) custom-call(f32[4608,128]{1,0:T(8,128)S(1)} %bitcast.27, ...), custom_call_target="tpu_custom_call" | custom-call | flops 4000000000 | bytes 4194304 | tf_op jit(solution)/shard_map/pallas_call | solution.py:328
  58.3 0.0 copy-start
  58.3 0.8 copy-done
  59.1 4.1 %shard_map.53 = (f32[64,1024]{1,0:T(8,128)S(1)}, f32[64,1024]{1,0:T(8,128)S(1)}) custom-call(bf16[64,32,128]{2,1,0:T(8,128)(2,1)S(1)} %get-tuple-element.41.refs_0_, bf16[64,32,128]{2,1,0:T(8,128)(2,1)S(1)} %get-tuple-element.42.refs_1_, bf16[64,32,128]{2,1,0:T(8,128)(2,1)S(1)} %get-tuple-element.43.refs_2_, ...), custom_call_target="tpu_custom_call" | custom-call | flops 5000000000 | bytes 4194304 | tf_op jit(solution)/shard_map/pallas_call | solution.py:354
  63.1 0.0 copy-start.1
  63.2 1.2 %collective-permute-start.3 = (f32[64,1024]{1,0:T(8,128)S(1)}, f32[64,1024]{1,0:T(8,128)S(1)}, u32[]{:S(2)}, u32[]{:S(2)}) collective-permute-start(f32[64,1024]{1,0:T(8,128)S(1)} %get-tuple-element.52), channel_id=1, source_target_pairs={{0,64},{8,72},{16,80},{24,88},{32,96},{40,104},{48,112},{56,120},{... | collective-permute-start | bytes 786440 | tf_op jit(solution)/shard_map/ppermute | solution.py:429
  64.3 4.0 %shard_map.52 = (f32[64,1024]{1,0:T(8,128)S(1)}, f32[64,1024]{1,0:T(8,128)S(1)}) custom-call(bf16[64,32,128]{2,1,0:T(8,128)(2,1)S(1)} %get-tuple-element.41.refs_0_, bf16[64,32,128]{2,1,0:T(8,128)(2,1)S(1)} %get-tuple-element.42.refs_1_, bf16[64,32,128]{2,1,0:T(8,128)(2,1)S(1)} %get-tuple-element.43.refs_2_, ...), custom_call_target="tpu_custom_call" | custom-call | flops 5000000000 | bytes 4194304 | tf_op jit(solution)/shard_map/pallas_call | solution.py:354
  68.3 1.2 %collective-permute-start.2 = (f32[64,1024]{1,0:T(8,128)S(1)}, f32[64,1024]{1,0:T(8,128)S(1)}, u32[]{:S(2)}, u32[]{:S(2)}) collective-permute-start(f32[64,1024]{1,0:T(8,128)S(1)} %get-tuple-element.50), channel_id=1, source_target_pairs={{0,64},{8,72},{16,80},{24,88},{32,96},{40,104},{48,112},{56,120},{... | collective-permute-start | bytes 786440 | tf_op jit(solution)/shard_map/ppermute | solution.py:429
  69.6 11.5 %all-to-all-done = f32[128,1,4096]{2,1,0:T(1,128)} async-done(((f32[128,1,4096]{2,1,0:T(1,128)}), f32[128,1,4096]{2,1,0:T(1,128)}, u32[]{:S(2)}, u32[]{:S(2)}) %all-to-all-start) | async-done | bytes 2097184 | tf_op jit(solution)/shard_map/all_to_all | solution.py:426
  81.1 0.0 copy-done.1
  81.1 3.8 %shard_map.49 = (bf16[64,32,128]{2,1,0:T(8,128)(2,1)S(1)}, bf16[64,32,128]{2,1,0:T(8,128)(2,1)S(1)}, bf16[64,32,128]{2,1,0:T(8,128)(2,1)S(1)}, bf16[64,32,128]{2...) custom-call(f32[4096,128]{1,0:T(8,128)} %bitcast.3.a_ref, ...), custom_call_target="tpu_custom_call" | custom-call | flops 3000000000 | bytes 4194304 | tf_op jit(solution)/shard_map/pallas_call | solution.py:340
  84.9 4.1 %shard_map.51 = (f32[64,1024]{1,0:T(8,128)S(1)}, f32[64,1024]{1,0:T(8,128)S(1)}) custom-call(bf16[64,32,128]{2,1,0:T(8,128)(2,1)S(1)} %get-tuple-element.31.refs_0_, bf16[64,32,128]{2,1,0:T(8,128)(2,1)S(1)} %get-tuple-element.32.refs_1_, bf16[64,32,128]{2,1,0:T(8,128)(2,1)S(1)} %get-tuple-element.33.refs_2_, ...), custom_call_target="tpu_custom_call" | custom-call | flops 5000000000 | bytes 4194304 | tf_op jit(solution)/shard_map/pallas_call | solution.py:354
  89.0 0.6 collective-permute-start.1
  89.6 4.0 %shard_map.50 = (f32[64,1024]{1,0:T(8,128)S(1)}, f32[64,1024]{1,0:T(8,128)S(1)}) custom-call(bf16[64,32,128]{2,1,0:T(8,128)(2,1)S(1)} %get-tuple-element.31.refs_0_, bf16[64,32,128]{2,1,0:T(8,128)(2,1)S(1)} %get-tuple-element.32.refs_1_, bf16[64,32,128]{2,1,0:T(8,128)(2,1)S(1)} %get-tuple-element.33.refs_2_, ...), custom_call_target="tpu_custom_call" | custom-call | flops 5000000000 | bytes 4194304 | tf_op jit(solution)/shard_map/pallas_call | solution.py:354
  93.6 1.8 %collective-permute-start = (f32[64,1024]{1,0:T(8,128)S(1)}, f32[64,1024]{1,0:T(8,128)S(1)}, u32[]{:S(2)}, u32[]{:S(2)}) collective-permute-start(f32[64,1024]{1,0:T(8,128)S(1)} %get-tuple-element.38), channel_id=1, source_target_pairs={{0,64},{8,72},{16,80},{24,88},{32,96},{40,104},{48,112},{56,120},{... | collective-permute-start | bytes 786440 | tf_op jit(solution)/shard_map/ppermute | solution.py:429
  95.4 0.0 collective-permute-done.3.got_ref
  95.4 0.9 shard_map.54.rest_0_
  96.4 0.0 collective-permute-done.2.got_ref
  96.4 0.9 shard_map.55.rest_0_
  97.3 1.2 %collective-permute-done.1.got_ref = f32[64,1024]{1,0:T(8,128)S(1)} collective-permute-done((f32[64,1024]{1,0:T(8,128)S(1)}, f32[64,1024]{1,0:T(8,128)S(1)}, u32[]{:S(2)}, u32[]{:S(2)}) %collective-permute-start.1) | collective-permute-done | bytes 262176 | tf_op jit(solution)/shard_map/ppermute | solution.py:429
  98.5 0.9 shard_map.56.rest_0_
  99.5 3.3 %collective-permute-done.got_ref = f32[64,1024]{1,0:T(8,128)S(1)} collective-permute-done((f32[64,1024]{1,0:T(8,128)S(1)}, f32[64,1024]{1,0:T(8,128)S(1)}, u32[]{:S(2)}, u32[]{:S(2)}) %collective-permute-start) | collective-permute-done | bytes 262176 | tf_op jit(solution)/shard_map/ppermute | solution.py:429
  102.7 0.9 shard_map.57
  (5 shorter events, 0.1 us)
Async XLA Ops:
  3.4 42.6 %all-to-all-start.1 = ((f32[128,1,4608]{2,1,0:T(1,128)}), f32[128,1,4608]{2,1,0:T(1,128)S(1)}, u32[]{:S(2)}, u32[]{:S(2)}) async-start(f32[128,1,4608]{2,1,0:T(1,128)} %bitcast.32), calls=%async_computation.1 | async-start | bytes 4718592 | tf_op jit(solution)/shard_map/all_to_all | solution.py:426
  46.0 6.8 %copy-start.2 = (f32[2,2,2,64,2,64]{5,4,3,2,1,0:T(2,128)S(1)}, f32[2,2,2,64,2,64]{5,4,3,2,1,0:T(2,128)}, u32[]{:S(2)}) copy-start(f32[2,2,2,64,2,64]{5,4,3,2,1,0:T(2,128)} %param.6) | copy-start | bytes 786436
  46.0 35.0 %all-to-all-start = ((f32[128,1,4096]{2,1,0:T(1,128)}), f32[128,1,4096]{2,1,0:T(1,128)}, u32[]{:S(2)}, u32[]{:S(2)}) async-start(f32[128,1,4096]{2,1,0:T(1,128)} %bitcast.33), calls=%async_computation | async-start | bytes 4194304 | tf_op jit(solution)/shard_map/all_to_all | solution.py:426
  58.3 0.8 copy-start
  63.1 17.9 %copy-start.1 = (f32[32,32,128]{2,1,0:T(8,128)S(1)}, f32[32,32,128]{2,1,0:T(8,128)}, u32[]{:S(2)}) copy-start(f32[32,32,128]{2,1,0:T(8,128)} %copy-done) | copy-start | bytes 1572868
  63.2 32.3 %collective-permute-start.3 = (f32[64,1024]{1,0:T(8,128)S(1)}, f32[64,1024]{1,0:T(8,128)S(1)}, u32[]{:S(2)}, u32[]{:S(2)}) collective-permute-start(f32[64,1024]{1,0:T(8,128)S(1)} %get-tuple-element.52), channel_id=1, source_target_pairs={{0,64},{8,72},{16,80},{24,88},{32,96},{40,104},{48,112},{56,120},{... | collective-permute-start | bytes 786440 | tf_op jit(solution)/shard_map/ppermute | solution.py:429
  68.3 28.0 %collective-permute-start.2 = (f32[64,1024]{1,0:T(8,128)S(1)}, f32[64,1024]{1,0:T(8,128)S(1)}, u32[]{:S(2)}, u32[]{:S(2)}) collective-permute-start(f32[64,1024]{1,0:T(8,128)S(1)} %get-tuple-element.50), channel_id=1, source_target_pairs={{0,64},{8,72},{16,80},{24,88},{32,96},{40,104},{48,112},{56,120},{... | collective-permute-start | bytes 786440 | tf_op jit(solution)/shard_map/ppermute | solution.py:429
  89.0 9.5 %collective-permute-start.1 = (f32[64,1024]{1,0:T(8,128)S(1)}, f32[64,1024]{1,0:T(8,128)S(1)}, u32[]{:S(2)}, u32[]{:S(2)}) collective-permute-start(f32[64,1024]{1,0:T(8,128)S(1)} %get-tuple-element.40), channel_id=1, source_target_pairs={{0,64},{8,72},{16,80},{24,88},{32,96},{40,104},{48,112},{56,120},{... | collective-permute-start | bytes 786440 | tf_op jit(solution)/shard_map/ppermute | solution.py:429
  93.6 9.1 %collective-permute-start = (f32[64,1024]{1,0:T(8,128)S(1)}, f32[64,1024]{1,0:T(8,128)S(1)}, u32[]{:S(2)}, u32[]{:S(2)}) collective-permute-start(f32[64,1024]{1,0:T(8,128)S(1)} %get-tuple-element.38), channel_id=1, source_target_pairs={{0,64},{8,72},{16,80},{24,88},{32,96},{40,104},{48,112},{56,120},{... | collective-permute-start | bytes 786440 | tf_op jit(solution)/shard_map/ppermute | solution.py:429

commit v7 on v6

--- a/solution.py
+++ b/solution.py
@@ -80,7 +80,7 @@
 
 
 def pack(weights, slopes, top):
-    pieces, lanes = 4, 1024
+    pieces, lanes = 2, 2048
     rows = ROWS if slopes is None else ROWS + SLOPES
     more = [] if slopes is None else [slopes]
     anywhere = pl.BlockSpec(memory_space=pl.ANY)

time: 104 us -> 104 us (level)
  no operation moved by 1% of the time
where the time goes in v7:
time: 104 us
  waiting for transfers between devices  44.5 us (43%)
  Pallas kernels  34 us (33%)
  starting transfers between devices  22.7 us (22%)
  other arithmetic  1.06 us (1%)
  local copies, waits for them, and re-layouts  1.05 us (1%)
    all_to_all x2, waiting for transfers between devices, spread(): lax.all_to_all(packed.reshape(128, 1, -1), AXES, split_axis=0, concat_axi...  40 us
    all_to_all x2, starting transfers between devices, spread(): lax.all_to_all(packed.reshape(128, 1, -1), AXES, split_axis=0, concat_axi...  18 us
    pallas_call x4, Pallas kernels, late_part(): pl.pallas_call(functools.partial(late_kernel, x1), out_shape=[FIELD, FIEL...  16.2 us
    pallas_call x2, Pallas kernels, pack(): pl.pallas_call(functools.partial(pack_kernel, top, rows), out_shape=jax.S...  6.25 us
    ppermute x4, starting transfers between devices, swap(): return lax.ppermute(field, 'bx', [(i, i ^ 8) for i in range(16)])  4.76 us
    ppermute x4, waiting for transfers between devices, swap(): return lax.ppermute(field, 'bx', [(i, i ^ 8) for i in range(16)])  4.54 us
    pallas_call x1, Pallas kernels, first_part(): pl.pallas_call(first_kernel, out_shape=[STATE] * 4 + [TABLE] * 4 + [K3, E...  4.03 us
    pallas_call x1, Pallas kernels, second_part(): pl.pallas_call(second_kernel, out_shape=[STATE] * 4 + [K3, E3], in_specs=...  3.82 us
  transfers between devices with their start and end apart: 6, of which 4 were waited for; matrix products, arithmetic and copies ran while one was open for 1% of the time, Pallas kernels for 29%

profile of v7, /device:TPU:0, one launch (start us, length us, event | category | flops | bytes accessed | tf_op | source)
XLA Modules:
  0.0 103.8 jit_solution(14912192081005429389)
XLA Ops:
  0.0 3.3 %shard_map.47 = f32[2,2304,128]{2,1,0:T(8,128)} custom-call(f32[128,8192]{1,0:T(8,128)} %bitcast.30, f32[8,1,8192]{2,1,0:T(1,128)} %bitcast.36), custom_call_target="tpu_custom_call" | custom-call | bytes 5242880 | tf_op jit(solution)/shard_map/pallas_call | solution.py:87
  3.3 11.1 %all-to-all-start.1 = ((f32[128,1,4608]{2,1,0:T(1,128)}), f32[128,1,4608]{2,1,0:T(1,128)S(1)}, u32[]{:S(2)}, u32[]{:S(2)}) async-start(f32[128,1,4608]{2,1,0:T(1,128)} %bitcast.32), calls=%async_computation.1 | async-start | bytes 4718592 | tf_op jit(solution)/shard_map/all_to_all | solution.py:426
  14.5 2.9 %shard_map.46 = f32[2,2048,128]{2,1,0:T(8,128)} custom-call(f32[128,8192]{1,0:T(8,128)} %bitcast.31), custom_call_target="tpu_custom_call" | custom-call | bytes 5242880 | tf_op jit(solution)/shard_map/pallas_call | solution.py:87
  17.4 28.5 %all-to-all-done.1 = f32[128,1,4608]{2,1,0:T(1,128)S(1)} async-done(((f32[128,1,4608]{2,1,0:T(1,128)}), f32[128,1,4608]{2,1,0:T(1,128)S(1)}, u32[]{:S(2)}, u32[]{:S(2)}) %all-to-all-start.1) | async-done | bytes 2359328 | tf_op jit(solution)/shard_map/all_to_all | solution.py:426
  45.9 0.0 copy-start.2
  45.9 6.8 %all-to-all-start = ((f32[128,1,4096]{2,1,0:T(1,128)}), f32[128,1,4096]{2,1,0:T(1,128)}, u32[]{:S(2)}, u32[]{:S(2)}) async-start(f32[128,1,4096]{2,1,0:T(1,128)} %bitcast.33), calls=%async_computation | async-start | bytes 4194304 | tf_op jit(solution)/shard_map/all_to_all | solution.py:426
  52.8 0.0 copy-done.2
  52.8 0.1 copy.14
  53.0 0.1 copy.13
  53.1 0.8 slice_bitcast_fusion
  53.9 0.2 maximum_select_fusion.e_ref
  54.1 4.0 %shard_map.48 = (bf16[64,32,128]{2,1,0:T(8,128)(2,1)S(1)}, bf16[64,32,128]{2,1,0:T(8,128)(2,1)S(1)}, bf16[64,32,128]{2,1,0:T(8,128)(2,1)S(1)}, bf16[64,32,128]{2...) custom-call(f32[4608,128]{1,0:T(8,128)S(1)} %bitcast.27, ...), custom_call_target="tpu_custom_call" | custom-call | flops 4000000000 | bytes 4194304 | tf_op jit(solution)/shard_map/pallas_call | solution.py:328
  58.2 0.0 copy-start
  58.2 0.8 copy-done
  59.0 4.1 %shard_map.53 = (f32[64,1024]{1,0:T(8,128)S(1)}, f32[64,1024]{1,0:T(8,128)S(1)}) custom-call(bf16[64,32,128]{2,1,0:T(8,128)(2,1)S(1)} %get-tuple-element.41.refs_0_, bf16[64,32,128]{2,1,0:T(8,128)(2,1)S(1)} %get-tuple-element.42.refs_1_, bf16[64,32,128]{2,1,0:T(8,128)(2,1)S(1)} %get-tuple-element.43.refs_2_, ...), custom_call_target="tpu_custom_call" | custom-call | flops 5000000000 | bytes 4194304 | tf_op jit(solution)/shard_map/pallas_call | solution.py:354
  63.0 0.0 copy-start.1
  63.1 1.2 %collective-permute-start.3 = (f32[64,1024]{1,0:T(8,128)S(1)}, f32[64,1024]{1,0:T(8,128)S(1)}, u32[]{:S(2)}, u32[]{:S(2)}) collective-permute-start(f32[64,1024]{1,0:T(8,128)S(1)} %get-tuple-element.52), channel_id=1, source_target_pairs={{0,64},{8,72},{16,80},{24,88},{32,96},{40,104},{48,112},{56,120},{... | collective-permute-start | bytes 786440 | tf_op jit(solution)/shard_map/ppermute | solution.py:429
  64.2 4.0 %shard_map.52 = (f32[64,1024]{1,0:T(8,128)S(1)}, f32[64,1024]{1,0:T(8,128)S(1)}) custom-call(bf16[64,32,128]{2,1,0:T(8,128)(2,1)S(1)} %get-tuple-element.41.refs_0_, bf16[64,32,128]{2,1,0:T(8,128)(2,1)S(1)} %get-tuple-element.42.refs_1_, bf16[64,32,128]{2,1,0:T(8,128)(2,1)S(1)} %get-tuple-element.43.refs_2_, ...), custom_call_target="tpu_custom_call" | custom-call | flops 5000000000 | bytes 4194304 | tf_op jit(solution)/shard_map/pallas_call | solution.py:354
  68.3 1.2 %collective-permute-start.2 = (f32[64,1024]{1,0:T(8,128)S(1)}, f32[64,1024]{1,0:T(8,128)S(1)}, u32[]{:S(2)}, u32[]{:S(2)}) collective-permute-start(f32[64,1024]{1,0:T(8,128)S(1)} %get-tuple-element.50), channel_id=1, source_target_pairs={{0,64},{8,72},{16,80},{24,88},{32,96},{40,104},{48,112},{56,120},{... | collective-permute-start | bytes 786440 | tf_op jit(solution)/shard_map/ppermute | solution.py:429
  69.5 11.5 %all-to-all-done = f32[128,1,4096]{2,1,0:T(1,128)} async-done(((f32[128,1,4096]{2,1,0:T(1,128)}), f32[128,1,4096]{2,1,0:T(1,128)}, u32[]{:S(2)}, u32[]{:S(2)}) %all-to-all-start) | async-done | bytes 2097184 | tf_op jit(solution)/shard_map/all_to_all | solution.py:426
  81.0 0.0 copy-done.1
  81.0 3.8 %shard_map.49 = (bf16[64,32,128]{2,1,0:T(8,128)(2,1)S(1)}, bf16[64,32,128]{2,1,0:T(8,128)(2,1)S(1)}, bf16[64,32,128]{2,1,0:T(8,128)(2,1)S(1)}, bf16[64,32,128]{2...) custom-call(f32[4096,128]{1,0:T(8,128)} %bitcast.3.a_ref, ...), custom_call_target="tpu_custom_call" | custom-call | flops 3000000000 | bytes 4194304 | tf_op jit(solution)/shard_map/pallas_call | solution.py:340
  84.8 4.1 %shard_map.51 = (f32[64,1024]{1,0:T(8,128)S(1)}, f32[64,1024]{1,0:T(8,128)S(1)}) custom-call(bf16[64,32,128]{2,1,0:T(8,128)(2,1)S(1)} %get-tuple-element.31.refs_0_, bf16[64,32,128]{2,1,0:T(8,128)(2,1)S(1)} %get-tuple-element.32.refs_1_, bf16[64,32,128]{2,1,0:T(8,128)(2,1)S(1)} %get-tuple-element.33.refs_2_, ...), custom_call_target="tpu_custom_call" | custom-call | flops 5000000000 | bytes 4194304 | tf_op jit(solution)/shard_map/pallas_call | solution.py:354
  88.9 0.6 collective-permute-start.1
  89.5 4.0 %shard_map.50 = (f32[64,1024]{1,0:T(8,128)S(1)}, f32[64,1024]{1,0:T(8,128)S(1)}) custom-call(bf16[64,32,128]{2,1,0:T(8,128)(2,1)S(1)} %get-tuple-element.31.refs_0_, bf16[64,32,128]{2,1,0:T(8,128)(2,1)S(1)} %get-tuple-element.32.refs_1_, bf16[64,32,128]{2,1,0:T(8,128)(2,1)S(1)} %get-tuple-element.33.refs_2_, ...), custom_call_target="tpu_custom_call" | custom-call | flops 5000000000 | bytes 4194304 | tf_op jit(solution)/shard_map/pallas_call | solution.py:354
  93.5 1.8 %collective-permute-start = (f32[64,1024]{1,0:T(8,128)S(1)}, f32[64,1024]{1,0:T(8,128)S(1)}, u32[]{:S(2)}, u32[]{:S(2)}) collective-permute-start(f32[64,1024]{1,0:T(8,128)S(1)} %get-tuple-element.38), channel_id=1, source_target_pairs={{0,64},{8,72},{16,80},{24,88},{32,96},{40,104},{48,112},{56,120},{... | collective-permute-start | bytes 786440 | tf_op jit(solution)/shard_map/ppermute | solution.py:429
  95.3 0.0 collective-permute-done.3.got_ref
  95.3 0.9 shard_map.54.rest_0_
  96.3 0.0 collective-permute-done.2.got_ref
  96.3 0.9 shard_map.55.rest_0_
  97.2 1.2 %collective-permute-done.1.got_ref = f32[64,1024]{1,0:T(8,128)S(1)} collective-permute-done((f32[64,1024]{1,0:T(8,128)S(1)}, f32[64,1024]{1,0:T(8,128)S(1)}, u32[]{:S(2)}, u32[]{:S(2)}) %collective-permute-start.1) | collective-permute-done | bytes 262176 | tf_op jit(solution)/shard_map/ppermute | solution.py:429
  98.4 0.9 shard_map.56.rest_0_
  99.3 3.3 %collective-permute-done.got_ref = f32[64,1024]{1,0:T(8,128)S(1)} collective-permute-done((f32[64,1024]{1,0:T(8,128)S(1)}, f32[64,1024]{1,0:T(8,128)S(1)}, u32[]{:S(2)}, u32[]{:S(2)}) %collective-permute-start) | collective-permute-done | bytes 262176 | tf_op jit(solution)/shard_map/ppermute | solution.py:429
  102.7 0.9 shard_map.57
  (5 shorter events, 0.1 us)
Async XLA Ops:
  3.3 42.6 %all-to-all-start.1 = ((f32[128,1,4608]{2,1,0:T(1,128)}), f32[128,1,4608]{2,1,0:T(1,128)S(1)}, u32[]{:S(2)}, u32[]{:S(2)}) async-start(f32[128,1,4608]{2,1,0:T(1,128)} %bitcast.32), calls=%async_computation.1 | async-start | bytes 4718592 | tf_op jit(solution)/shard_map/all_to_all | solution.py:426
  45.9 6.8 %copy-start.2 = (f32[2,2,2,64,2,64]{5,4,3,2,1,0:T(2,128)S(1)}, f32[2,2,2,64,2,64]{5,4,3,2,1,0:T(2,128)}, u32[]{:S(2)}) copy-start(f32[2,2,2,64,2,64]{5,4,3,2,1,0:T(2,128)} %param.6) | copy-start | bytes 786436
  45.9 35.0 %all-to-all-start = ((f32[128,1,4096]{2,1,0:T(1,128)}), f32[128,1,4096]{2,1,0:T(1,128)}, u32[]{:S(2)}, u32[]{:S(2)}) async-start(f32[128,1,4096]{2,1,0:T(1,128)} %bitcast.33), calls=%async_computation | async-start | bytes 4194304 | tf_op jit(solution)/shard_map/all_to_all | solution.py:426
  58.2 0.8 copy-start
  63.0 17.9 %copy-start.1 = (f32[32,32,128]{2,1,0:T(8,128)S(1)}, f32[32,32,128]{2,1,0:T(8,128)}, u32[]{:S(2)}) copy-start(f32[32,32,128]{2,1,0:T(8,128)} %copy-done) | copy-start | bytes 1572868
  63.1 32.3 %collective-permute-start.3 = (f32[64,1024]{1,0:T(8,128)S(1)}, f32[64,1024]{1,0:T(8,128)S(1)}, u32[]{:S(2)}, u32[]{:S(2)}) collective-permute-start(f32[64,1024]{1,0:T(8,128)S(1)} %get-tuple-element.52), channel_id=1, source_target_pairs={{0,64},{8,72},{16,80},{24,88},{32,96},{40,104},{48,112},{56,120},{... | collective-permute-start | bytes 786440 | tf_op jit(solution)/shard_map/ppermute | solution.py:429
  68.3 28.0 %collective-permute-start.2 = (f32[64,1024]{1,0:T(8,128)S(1)}, f32[64,1024]{1,0:T(8,128)S(1)}, u32[]{:S(2)}, u32[]{:S(2)}) collective-permute-start(f32[64,1024]{1,0:T(8,128)S(1)} %get-tuple-element.50), channel_id=1, source_target_pairs={{0,64},{8,72},{16,80},{24,88},{32,96},{40,104},{48,112},{56,120},{... | collective-permute-start | bytes 786440 | tf_op jit(solution)/shard_map/ppermute | solution.py:429
  88.9 9.5 %collective-permute-start.1 = (f32[64,1024]{1,0:T(8,128)S(1)}, f32[64,1024]{1,0:T(8,128)S(1)}, u32[]{:S(2)}, u32[]{:S(2)}) collective-permute-start(f32[64,1024]{1,0:T(8,128)S(1)} %get-tuple-element.40), channel_id=1, source_target_pairs={{0,64},{8,72},{16,80},{24,88},{32,96},{40,104},{48,112},{56,120},{... | collective-permute-start | bytes 786440 | tf_op jit(solution)/shard_map/ppermute | solution.py:429
  93.5 9.1 %collective-permute-start = (f32[64,1024]{1,0:T(8,128)S(1)}, f32[64,1024]{1,0:T(8,128)S(1)}, u32[]{:S(2)}, u32[]{:S(2)}) collective-permute-start(f32[64,1024]{1,0:T(8,128)S(1)} %get-tuple-element.38), channel_id=1, source_target_pairs={{0,64},{8,72},{16,80},{24,88},{32,96},{40,104},{48,112},{56,120},{... | collective-permute-start | bytes 786440 | tf_op jit(solution)/shard_map/ppermute | solution.py:429
